TPU v7x, 32 devices: a whole 2x2x4 slice. The times are simulated.
32 devices in a mesh: fsdp: 32 (over z, y, x, core).
Axes of the slice: x: 2, y: 2, z: 4, core: 2. Of those that a mesh axis runs over, the one named last changes fastest.
Arguments:
- tokens: bfloat16 [4096, 1152], P('fsdp'), may hold values from -6 to 6
- cond: bfloat16 [96, 1152], P('fsdp'), may hold values from -6 to 6
- image_lengths: int32 [32, 3], P('fsdp'), may hold values from 1 to 102, 128 in all within a row
- ada_weight: bfloat16 [7962624], P('fsdp'), may hold values from -0.1875 to 0.1875
- ada_bias: bfloat16 [6912], P('fsdp'), may hold values from -3 to 3
- qkv_weight: bfloat16 [3981312], P('fsdp'), may hold values from -0.1875 to 0.1875
- qv_bias: bfloat16 [2304], P('fsdp'), may hold values from -3 to 3
- attn_weight: bfloat16 [1327104], P('fsdp'), may hold values from -0.5 to 0.5
- tail_bias: bfloat16 [2304], P('fsdp'), may hold values from -3 to 3
- up_weight: bfloat16 [5308416], P('fsdp'), may hold values from -0.1875 to 0.1875
- up_bias: bfloat16 [4608], P('fsdp'), may hold values from -3 to 3
- down_weight: bfloat16 [5308416], P('fsdp'), may hold values from -0.09375 to 0.09375
- projector_in: bfloat16 [2359296], P('fsdp'), may hold values from -0.1875 to 0.1875
- projector_in_bias: bfloat16 [2048], P('fsdp'), may hold values from -3 to 3
- projector_mid: bfloat16 [4194304], P('fsdp'), may hold values from -0.125 to 0.125
- projector_mid_bias: bfloat16 [2048], P('fsdp'), may hold values from -3 to 3
- projector_out: bfloat16 [1572864], P('fsdp'), may hold values from -0.125 to 0.125
- projector_out_bias: bfloat16 [768], P('fsdp'), may hold values from -3 to 3
- targets: bfloat16 [4096, 768], P('fsdp'), may hold values from -6 to 6
- out_grad: bfloat16 [4096, 1152], P('fsdp'), may hold values from -6 to 6
Outputs:
- mixed: bfloat16 [4096, 1152], P('fsdp')
- tokens_grad: bfloat16 [4096, 1152], P('fsdp')
- cond_grad: bfloat16 [96, 1152], P('fsdp')
- ada_weight_grad: float32 [7962624], P('fsdp')
- ada_bias_grad: float32 [6912], P('fsdp')
- qkv_weight_grad: float32 [3981312], P('fsdp')
- qv_bias_grad: float32 [2304], P('fsdp')
- attn_weight_grad: float32 [1327104], P('fsdp')
- tail_bias_grad: float32 [2304], P('fsdp')
- up_weight_grad: float32 [5308416], P('fsdp')
- up_bias_grad: float32 [4608], P('fsdp')
- down_weight_grad: float32 [5308416], P('fsdp')
- projector_in_grad: float32 [2359296], P('fsdp')
- projector_in_bias_grad: float32 [2048], P('fsdp')
- projector_mid_grad: float32 [4194304], P('fsdp')
- projector_mid_bias_grad: float32 [2048], P('fsdp')
- projector_out_grad: float32 [1572864], P('fsdp')
- projector_out_bias_grad: float32 [768], P('fsdp')
Inputs may be any that keep to these rules, and one draw needn't show every extreme that they name: Each row of image_lengths sums to 128, and its longest image has 102 tokens.
All inputs are finite; a program needn't handle non-finite values.
Results may differ from a plain program's by a relative error of at most 0.015.
The roundings to bfloat16 on the way count: a program that leaves them out, or rounds other values in their place, can miss the bound.
Values may be sent and summed in bfloat16 or wider, within the bound.
A program may use at most 512 MiB of HBM per device.

v0:
```python
import jax
import jax.numpy as jnp
from jax import lax
from jax.sharding import PartitionSpec as P

D = 1152
HEADS = 16
HD = 72
FF = 4608
P_SIZE = 2048
Z = 768


EPSILON = 1e-06
PRECISE = lax.Precision.HIGHEST


def layer_norm(values):
    centred = values - jnp.mean(values, axis=-1, keepdims=True)
    spread = jnp.mean(centred * centred, axis=-1, keepdims=True)
    return centred * lax.rsqrt(spread + EPSILON)


def sigmoid_linear(values):
    return values * jax.nn.sigmoid(values)


def gelu_tanh(values):
    inner = 0.7978845608028654 * (values + 0.044715 * values * values * values)
    return 0.5 * values * (1.0 + jnp.tanh(inner))


def image_onehot(lengths, row_count):
    ends = jnp.cumsum(lengths)
    position = jnp.arange(row_count, dtype=jnp.int32)
    image_of = jnp.sum((position[:, None] >= ends[None, :]).astype(jnp.int32), axis=1)
    images = jnp.arange(lengths.shape[0], dtype=jnp.int32)
    return (image_of, (image_of[:, None] == images[None, :]).astype(jnp.float32))


def pull_back(function, point, cotangent):
    return jax.vjp(function, point)[1](cotangent)[0]


def lowered(values):
    return values.astype(jnp.bfloat16)


def matmul(left, right):
    return jnp.dot(left, right, preferred_element_type=jnp.float32)


def transposed_left(left, right):
    return lax.dot_general(
        left, right, (((0,), (0,)), ((), ())), preferred_element_type=jnp.float32
    )


def transposed_right(left, right):
    return lax.dot_general(
        left, right, (((1,), (1,)), ((), ())), preferred_element_type=jnp.float32
    )


def column_sums(values):
    return jnp.sum(values.astype(jnp.float32), axis=0)


def by_owner(values, owners):
    return values.reshape(owners, -1)


def flatten_all(pieces):
    return tuple((piece.reshape(-1) for piece in pieces))


def unpack_mix(gathered):
    return (
        gathered[0].reshape(D, 6 * D),
        gathered[1].astype(jnp.float32),
        gathered[2].reshape(D, 3 * D),
        gathered[3].astype(jnp.float32),
        gathered[4].reshape(D, D),
        gathered[5].astype(jnp.float32),
    )


def unpack_dense(gathered):
    return (
        gathered[0].reshape(D, FF),
        gathered[1].astype(jnp.float32),
        gathered[2].reshape(FF, D),
        gathered[3].reshape(D, P_SIZE),
        gathered[4].astype(jnp.float32),
        gathered[5].reshape(P_SIZE, P_SIZE),
        gathered[6].astype(jnp.float32),
        gathered[7].reshape(P_SIZE, Z),
        gathered[8].astype(jnp.float32),
    )


def per_device(
    tokens,
    cond,
    image_lengths,
    ada_weight,
    ada_bias,
    qkv_weight,
    qv_bias,
    attn_weight,
    tail_bias,
    up_weight,
    up_bias,
    down_weight,
    projector_in,
    projector_in_bias,
    projector_mid,
    projector_mid_bias,
    projector_out,
    projector_out_bias,
    targets,
    out_grad,
):
    owners = lax.axis_size("fsdp")
    mix_gathered = (
        lax.all_gather(ada_weight, "fsdp", axis=0, tiled=True),
        lax.all_gather(ada_bias, "fsdp", axis=0, tiled=True),
        lax.all_gather(qkv_weight, "fsdp", axis=0, tiled=True),
        lax.all_gather(qv_bias, "fsdp", axis=0, tiled=True),
        lax.all_gather(attn_weight, "fsdp", axis=0, tiled=True),
        lax.all_gather(tail_bias, "fsdp", axis=0, tiled=True),
    )
    mix_full = unpack_mix(mix_gathered)
    ada_full, ada_bias_full, qkv_full, qv_full, attn_full, tail_full = mix_full
    row_count = tokens.shape[0]
    cond_values = cond.astype(jnp.float32)
    cond_low = lowered(sigmoid_linear(cond_values))
    modulation = matmul(cond_low, ada_full) + ada_bias_full
    image_of, onehot = image_onehot(image_lengths[0], row_count)
    per_token = jnp.dot(onehot, modulation, precision=PRECISE)
    shift_one, scale_one, gate_one, shift_two, scale_two, gate_two = jnp.split(per_token, 6, axis=1)
    inputs = tokens.astype(jnp.float32)
    normed_one = layer_norm(inputs)
    first_in = lowered(normed_one * (1.0 + scale_one) + shift_one)
    key_zero = jnp.zeros((D,), jnp.float32)
    bias_full = jnp.concatenate([qv_full[:D], key_zero, qv_full[D:]])
    projected = lowered(matmul(first_in, qkv_full) + bias_full)
    queries = projected[:, :D].reshape(row_count, HEADS, HD)
    keys_all = projected[:, D : 2 * D].reshape(row_count, HEADS, HD)
    values_all = projected[:, 2 * D :].reshape(row_count, HEADS, HD)
    same_image = (image_of[:, None] == image_of[None, :])[None]
    score_scale = HD ** (-0.5)

    def masked_scores():
        raw_scores = (
            jnp.einsum("qhd,khd->hqk", queries, keys_all, preferred_element_type=jnp.float32)
            * score_scale
        )
        return jnp.where(same_image, raw_scores, -1e30)

    masked = masked_scores()
    row_max = jnp.max(masked, axis=-1, keepdims=True)
    exp_scores = jnp.exp(masked - row_max)
    row_total = jnp.sum(exp_scores, axis=-1, keepdims=True)
    attn_probs = exp_scores / row_total
    head_out = jnp.einsum(
        "hqk,khd->qhd", lowered(attn_probs), values_all, preferred_element_type=jnp.float32
    )
    heads_low = lowered(head_out.reshape(row_count, D))
    branch_attn = matmul(heads_low, attn_full) + tail_full[:D]
    middle = inputs + gate_one * branch_attn
    normed_two = layer_norm(middle)
    second_in = lowered(normed_two * (1.0 + scale_two) + shift_two)
    dense_gathered = (
        lax.all_gather(up_weight, "fsdp", axis=0, tiled=True),
        lax.all_gather(up_bias, "fsdp", axis=0, tiled=True),
        lax.all_gather(down_weight, "fsdp", axis=0, tiled=True),
        lax.all_gather(projector_in, "fsdp", axis=0, tiled=True),
        lax.all_gather(projector_in_bias, "fsdp", axis=0, tiled=True),
        lax.all_gather(projector_mid, "fsdp", axis=0, tiled=True),
        lax.all_gather(projector_mid_bias, "fsdp", axis=0, tiled=True),
        lax.all_gather(projector_out, "fsdp", axis=0, tiled=True),
        lax.all_gather(projector_out_bias, "fsdp", axis=0, tiled=True),
    )
    dense_full = unpack_dense(dense_gathered)
    (
        up_full,
        up_bias_full,
        down_full,
        proj_in_full,
        proj_in_bias_full,
        proj_mid_full,
        proj_mid_bias_full,
        proj_out_full,
        proj_out_bias_full,
    ) = dense_full
    up_pre = matmul(second_in, up_full) + up_bias_full
    up_act = lowered(gelu_tanh(up_pre))
    branch_mlp = matmul(up_act, down_full) + tail_full[D:]
    hidden = middle + gate_two * branch_mlp
    mixed = lowered(hidden)
    first_pre = matmul(mixed, proj_in_full) + proj_in_bias_full
    first_act = lowered(sigmoid_linear(first_pre))
    second_pre = matmul(first_act, proj_mid_full) + proj_mid_bias_full
    second_act = lowered(sigmoid_linear(second_pre))
    features = matmul(second_act, proj_out_full) + proj_out_bias_full
    target_values = targets.astype(jnp.float32)

    def cosine_loss(values):
        value_norm = jnp.sqrt(jnp.sum(values * values, axis=1) + EPSILON)
        target_norm = jnp.sqrt(jnp.sum(target_values * target_values, axis=1) + EPSILON)
        return -0.5 * jnp.sum(jnp.sum(values * target_values, axis=1) / (value_norm * target_norm))

    feature_grad = lowered(jax.grad(cosine_loss)(features))
    dense_again = (
        lax.all_gather(up_weight, "fsdp", axis=0, tiled=True),
        lax.all_gather(up_bias, "fsdp", axis=0, tiled=True),
        lax.all_gather(down_weight, "fsdp", axis=0, tiled=True),
        lax.all_gather(projector_in, "fsdp", axis=0, tiled=True),
        lax.all_gather(projector_in_bias, "fsdp", axis=0, tiled=True),
        lax.all_gather(projector_mid, "fsdp", axis=0, tiled=True),
        lax.all_gather(projector_mid_bias, "fsdp", axis=0, tiled=True),
        lax.all_gather(projector_out, "fsdp", axis=0, tiled=True),
        lax.all_gather(projector_out_bias, "fsdp", axis=0, tiled=True),
    )
    dense_back = unpack_dense(dense_again)
    up_back = dense_back[0]
    down_back = dense_back[2]
    proj_in_back = dense_back[3]
    proj_mid_back = dense_back[5]
    proj_out_back = dense_back[7]
    grad_proj_out = transposed_left(second_act, feature_grad)
    second_back = lowered(
        pull_back(sigmoid_linear, second_pre, transposed_right(feature_grad, proj_out_back))
    )
    grad_proj_mid = transposed_left(first_act, second_back)
    first_back = lowered(
        pull_back(sigmoid_linear, first_pre, transposed_right(second_back, proj_mid_back))
    )
    grad_proj_in = transposed_left(mixed, first_back)
    hidden_grad = out_grad.astype(jnp.float32) + transposed_right(first_back, proj_in_back)
    gate_two_grad = hidden_grad * branch_mlp
    branch_mlp_grad = lowered(hidden_grad * gate_two)
    grad_down = transposed_left(up_act, branch_mlp_grad)
    up_grad = lowered(pull_back(gelu_tanh, up_pre, transposed_right(branch_mlp_grad, down_back)))
    grad_up = transposed_left(second_in, up_grad)
    second_in_grad = transposed_right(up_grad, up_back)
    middle_grad = hidden_grad + pull_back(layer_norm, middle, second_in_grad * (1.0 + scale_two))
    up_rows = by_owner(grad_up, owners)
    up_bias_rows = by_owner(column_sums(up_grad), owners)
    down_rows = by_owner(grad_down, owners)
    proj_in_rows = by_owner(grad_proj_in, owners)
    proj_in_sums = by_owner(column_sums(first_back), owners)
    proj_mid_rows = by_owner(grad_proj_mid, owners)
    proj_mid_sums = by_owner(column_sums(second_back), owners)
    proj_out_rows = by_owner(grad_proj_out, owners)
    proj_out_sums = by_owner(column_sums(feature_grad), owners)
    dense_grads = flatten_all(
        (
            lax.psum_scatter(up_rows, "fsdp", scatter_dimension=0, tiled=True),
            lax.psum_scatter(up_bias_rows, "fsdp", scatter_dimension=0, tiled=True),
            lax.psum_scatter(down_rows, "fsdp", scatter_dimension=0, tiled=True),
            lax.psum_scatter(proj_in_rows, "fsdp", scatter_dimension=0, tiled=True),
            lax.psum_scatter(proj_in_sums, "fsdp", scatter_dimension=0, tiled=True),
            lax.psum_scatter(proj_mid_rows, "fsdp", scatter_dimension=0, tiled=True),
            lax.psum_scatter(proj_mid_sums, "fsdp", scatter_dimension=0, tiled=True),
            lax.psum_scatter(proj_out_rows, "fsdp", scatter_dimension=0, tiled=True),
            lax.psum_scatter(proj_out_sums, "fsdp", scatter_dimension=0, tiled=True),
        )
    )
    mix_again = (
        lax.all_gather(ada_weight, "fsdp", axis=0, tiled=True),
        lax.all_gather(ada_bias, "fsdp", axis=0, tiled=True),
        lax.all_gather(qkv_weight, "fsdp", axis=0, tiled=True),
        lax.all_gather(qv_bias, "fsdp", axis=0, tiled=True),
        lax.all_gather(attn_weight, "fsdp", axis=0, tiled=True),
        lax.all_gather(tail_bias, "fsdp", axis=0, tiled=True),
    )
    mix_back = unpack_mix(mix_again)
    ada_back = mix_back[0]
    qkv_back = mix_back[2]
    attn_back = mix_back[4]
    gate_one_grad = middle_grad * branch_attn
    branch_attn_grad = lowered(middle_grad * gate_one)
    grad_attn = transposed_left(heads_low, branch_attn_grad)
    heads_grad = lowered(transposed_right(branch_attn_grad, attn_back)).reshape(
        row_count, HEADS, HD
    )
    again_probs = jnp.exp(masked_scores() - row_max) / row_total
    prob_grad = jnp.einsum(
        "qhd,khd->hqk", heads_grad, values_all, preferred_element_type=jnp.float32
    )
    value_grad = jnp.einsum(
        "hqk,qhd->khd", lowered(again_probs), heads_grad, preferred_element_type=jnp.float32
    )
    score_grad = lowered(
        again_probs * (prob_grad - jnp.sum(again_probs * prob_grad, axis=-1, keepdims=True))
    )
    query_grad = (
        jnp.einsum("hqk,khd->qhd", score_grad, keys_all, preferred_element_type=jnp.float32)
        * score_scale
    )
    key_grad = (
        jnp.einsum("hqk,qhd->khd", score_grad, queries, preferred_element_type=jnp.float32)
        * score_scale
    )
    projected_grad = lowered(
        jnp.concatenate(
            [
                query_grad.reshape(row_count, D),
                key_grad.reshape(row_count, D),
                value_grad.reshape(row_count, D),
            ],
            axis=1,
        )
    )
    grad_qkv = transposed_left(first_in, projected_grad)
    projected_sums = column_sums(projected_grad)
    grad_qv_bias = jnp.concatenate([projected_sums[:D], projected_sums[2 * D :]])
    first_in_grad = transposed_right(projected_grad, qkv_back)
    input_grad = middle_grad + pull_back(layer_norm, inputs, first_in_grad * (1.0 + scale_one))
    token_mod_grad = jnp.concatenate(
        [
            first_in_grad,
            first_in_grad * normed_one,
            gate_one_grad,
            second_in_grad,
            second_in_grad * normed_two,
            gate_two_grad,
        ],
        axis=1,
    )
    modulation_grad = lowered(
        lax.dot_general(onehot, token_mod_grad, (((0,), (0,)), ((), ())), precision=PRECISE)
    )
    grad_ada = transposed_left(cond_low, modulation_grad)
    cond_grad = pull_back(
        sigmoid_linear, cond_values, transposed_right(modulation_grad, ada_back)
    ).astype(jnp.bfloat16)
    grad_tail = jnp.concatenate([column_sums(branch_attn_grad), column_sums(branch_mlp_grad)])
    ada_rows = by_owner(grad_ada, owners)
    ada_sums = by_owner(column_sums(modulation_grad), owners)
    qkv_rows = by_owner(grad_qkv, owners)
    qv_rows = by_owner(grad_qv_bias, owners)
    attn_rows = by_owner(grad_attn, owners)
    tail_rows = by_owner(grad_tail, owners)
    mix_grads = flatten_all(
        (
            lax.psum_scatter(ada_rows, "fsdp", scatter_dimension=0, tiled=True),
            lax.psum_scatter(ada_sums, "fsdp", scatter_dimension=0, tiled=True),
            lax.psum_scatter(qkv_rows, "fsdp", scatter_dimension=0, tiled=True),
            lax.psum_scatter(qv_rows, "fsdp", scatter_dimension=0, tiled=True),
            lax.psum_scatter(attn_rows, "fsdp", scatter_dimension=0, tiled=True),
            lax.psum_scatter(tail_rows, "fsdp", scatter_dimension=0, tiled=True),
        )
    )
    return (
        mixed,
        input_grad.astype(jnp.bfloat16),
        cond_grad,
        mix_grads[0],
        mix_grads[1],
        mix_grads[2],
        mix_grads[3],
        mix_grads[4],
        mix_grads[5],
        dense_grads[0],
        dense_grads[1],
        dense_grads[2],
        dense_grads[3],
        dense_grads[4],
        dense_grads[5],
        dense_grads[6],
        dense_grads[7],
        dense_grads[8],
    )


def solution(mesh):
    in_specs = (
        P("fsdp", None),
        P("fsdp", None),
        P("fsdp", None),
        P("fsdp"),
        P("fsdp"),
        P("fsdp"),
        P("fsdp"),
        P("fsdp"),
        P("fsdp"),
        P("fsdp"),
        P("fsdp"),
        P("fsdp"),
        P("fsdp"),
        P("fsdp"),
        P("fsdp"),
        P("fsdp"),
        P("fsdp"),
        P("fsdp"),
        P("fsdp", None),
        P("fsdp", None),
    )
    out_specs = (
        P("fsdp", None),
        P("fsdp", None),
        P("fsdp", None),
        P("fsdp"),
        P("fsdp"),
        P("fsdp"),
        P("fsdp"),
        P("fsdp"),
        P("fsdp"),
        P("fsdp"),
        P("fsdp"),
        P("fsdp"),
        P("fsdp"),
        P("fsdp"),
        P("fsdp"),
        P("fsdp"),
        P("fsdp"),
        P("fsdp"),
    )
    return jax.shard_map(
        per_device, mesh=mesh, in_specs=in_specs, out_specs=out_specs, check_vma=False
    )
```

profile of v0, /device:TPU:0, one launch (start us, length us, event | category | flops | bytes accessed | tf_op | source)
XLA Modules:
  0.0 2904.2 jit_solution(17500441279698728829)
XLA Ops:
  10.5 2.0 reshape.367
  21.2 43.7 %all-reduce.24 = (bf16[6912]{0:T(1024)(128)(2,1)S(1)}, bf16[2304]{0:T(1024)(128)(2,1)S(1)}, bf16[2304]{0:T(1024)(128)(2,1)S(1)}, bf16[4608]{0:T(1024)(128)(2,1)S...) all-reduce(bf16[6912]{0:T(1024)(128)(2,1)S(1)} %dynamic-update-slic, ...), channel_id=1, replica_groups=mesh['fsdp'=32] {'fsdp'}, use_global_device_ids=true, to_apply=%add | all-reduce | flops 20992 | bytes 83968
  69.8 11.0 all-gather.25.cloned.1.call-done
  80.8 47.1 %reduce.1 = bf16[32,41472]{1,0:T(8,128)(2,1)S(1)} reduce(bf16[32,1,41472]{2,1,0:T(2,128)(2,1)} %all-gather.25.cloned.1.call-done, bf16[]{:T(256)} %constant.124), dimensions={1}, to_apply=%all-gather.1.reduce_sub_computation | reduce | bytes 5308418 | tf_op jit(solution)/shard_map/all_gather | solution.py:130
  127.9 5.0 reshape.315
  132.9 8.2 all-gather.21.cloned.1.call-done
  141.0 6.4 reshape.320
  147.4 59.0 %all-gather.17.cloned.1.call-done = bf16[2359296]{0:T(1024)(128)(2,1)} async-done(((bf16[73728]{0:T(1024)(128)(2,1)}), bf16[2359296]{0:T(1024)(128)(2,1)}) %all-gather.17.cloned.1.call-update) | async-done | bytes 4718608 | tf_op jit(solution)/shard_map/all_gather | solution.py:178
  206.5 8.2 reshape.318
  214.6 105.0 %all-gather.23.cloned.1.call-done = bf16[32,1,124416]{2,1,0:T(2,128)(2,1)} async-done(((bf16[1,1,124416]{2,1,0:T(2,128)(2,1)}), bf16[32,1,124416]{2,1,0:T(2,128)(2,1)}) %all-gather.23.cloned.1.call-update) | async-done | bytes 7962640 | tf_op jit(solution)/shard_map/all_gather | solution.py:128
  319.6 167.3 %reduce = bf16[32,124416]{1,0:T(8,128)(2,1)} reduce(bf16[32,1,124416]{2,1,0:T(2,128)(2,1)} %all-gather.23.cloned.1.call-done, bf16[]{:T(256)} %constant.124), dimensions={1}, to_apply=%all-gather.reduce_sub_computation | reduce | bytes 15925250 | tf_op jit(solution)/shard_map/all_gather | solution.py:128
  487.0 14.7 reshape.311
  501.7 13.4 reshape.319
  515.1 19.1 reshape.316
  534.2 40.8 %all-gather.15.cloned.1.call-done = bf16[5308416]{0:T(1024)(128)(2,1)} async-done(((bf16[165888]{0:T(1024)(128)(2,1)}), bf16[5308416]{0:T(1024)(128)(2,1)}) %all-gather.15.cloned.1.call-update) | async-done | bytes 10616848 | tf_op jit(solution)/shard_map/all_gather | solution.py:177
  575.0 20.4 reshape.317
  595.4 92.0 %all-gather.11.cloned.1.call-done = bf16[7962624]{0:T(1024)(128)(2,1)} async-done(((bf16[248832]{0:T(1024)(128)(2,1)}), bf16[7962624]{0:T(1024)(128)(2,1)}) %all-gather.11.cloned.1.call-update) | async-done | bytes 15925264 | tf_op jit(solution)/shard_map/all_gather | solution.py:126
  687.4 29.4 %reshape.310 = bf16[1152,6912]{1,0:T(8,128)(2,1)} reshape(bf16[7962624]{0:T(1024)(128)(2,1)} %all-gather.11.cloned.1.call-done) | data formatting | bytes 31850496 | tf_op jit(solution)/shard_map/reshape | solution.py:79
  716.9 7.7 convolution_add_fusion
  726.5 4.8 fusion.1
  737.8 2.6 fusion.82
  740.3 2.6 convolution_convert_fusion.3
  742.9 3.3 fusion.77
  746.7 5.9 convolution_add_fusion.1
  752.7 7.8 add_convert_fusion.1
  765.3 1.8 convert_reduce_fusion.2
  767.2 3.7 convert_reduce_fusion.3
  770.9 3.0 convert_reduce_fusion.5
  773.9 10.5 convert_reduce_fusion
  784.4 4.8 multiply_reduce_fusion.1
  792.3 2.0 convolution_convert_fusion.1
  794.3 1.9 copy.70
  796.2 2.7 convolution_convert_fusion.2
  798.9 1.9 multiply_reduce_fusion
  801.9 7.5 constant_dynamic-update-slice_fusion.1
  809.8 3.8 fusion.67
  813.6 5.0 fusion.85
  818.5 7.7 fusion.64
  826.3 8.1 fusion.66
  843.5 2.4 fusion.75
  845.9 2.3 multiply_dynamic-update-slice_fusion.2
  851.2 3.3 convert_reduce_fusion.8
  856.8 3.2 fusion.83
  859.9 5.9 reshape.332
  865.8 6.2 reshape.349
  872.0 10.1 reshape.341
  882.1 12.6 reshape.329
  894.7 12.3 reshape.345
  908.6 8.8 fusion.68
  917.4 22.6 reshape.339
  939.9 8.9 fusion.84
  948.8 30.1 %reshape.335 = f32[32,165888]{1,0:T(8,128)} reshape(f32[1152,4608]{1,0:T(8,128)} %fusion.84) | data formatting | bytes 42467328 | tf_op jit(solution)/shard_map/reshape | solution.py:70
  979.0 12.6 fusion.61
  991.5 37.2 %reshape.325 = f32[32,248832]{1,0:T(8,128)} reshape(f32[1152,6912]{1,0:T(8,128)} %fusion.61) | data formatting | bytes 63700992 | tf_op jit(solution)/shard_map/reshape | solution.py:70
  1028.8 10.7 fusion.49
  1045.6 98.6 %all-reduce.29.cloned.1.call-done = f32[32,49152]{1,0:T(8,128)} async-done(((f32[32,49152]{1,0:T(8,128)}), f32[32,49152]{1,0:T(8,128)}) %all-reduce.29.cloned.1.call-update) | async-done | bytes 6291472
  1144.2 2.2 constant_dynamic-slice_fusion.1
  1146.4 1728.4 %all-reduce.33.cloned.1.call-done = (f32[32,248832]{1,0:T(8,128)}, f32[32,124416]{1,0:T(8,128)}, f32[32,41472]{1,0:T(8,128)}, f32[32,165888]{1,0:T(8,128)}, f32[...) async-done(((f32[32,248832]{1,0:T(8,128)}, f32[32,124416]{1,0:T(8,128)}, f32[32,41472]{1,0:T(8,128)}, f32[32,165888]{1,0:T(8,128)}, ...) | async-done | bytes 121765904
  2874.9 4.5 constant_dynamic-slice_fusion.12
  2879.3 2.4 dynamic-slice_reduce_fusion.1
  2881.8 2.6 constant_dynamic-slice_fusion.5
  2884.3 4.2 dynamic-slice_reduce_fusion
  2888.6 3.3 constant_dynamic-slice_fusion.3
  2891.9 5.6 constant_dynamic-slice_fusion.6
  (246 shorter events, 56.8 us)
Async XLA Ops:
  7.2 60.1 %copy-start.63 = (s32[1,3]{1,0:T(1,128)S(1)}, s32[1,3]{1,0:T(1,128)}, u32[]{:S(2)}) copy-start(s32[1,3]{1,0:T(1,128)} %param.22) | copy-start | bytes 40
  7.2 60.4 %copy-start.7 = (bf16[128,1152]{1,0:T(8,128)(2,1)S(1)}, bf16[128,1152]{1,0:T(8,128)(2,1)}, u32[]{:S(2)}) copy-start(bf16[128,1152]{1,0:T(8,128)(2,1)} %param.20) | copy-start | bytes 884740
  7.2 73.6 %all-gather.25.cloned.1.call-start = ((), (), s32[]{:S(2)}) async-start(), calls=%async_computation.7 | async-start | bytes 5474304 | tf_op jit(solution)/shard_map/all_gather | solution.py:130
  9.0 132.1 %all-gather.21.cloned.1.call-start = ((), (), s32[]{:S(2)}) async-start(), calls=%async_computation.5 | async-start | bytes 3244032 | tf_op jit(solution)/shard_map/all_gather | solution.py:182
  9.7 196.7 %all-gather.17.cloned.1.call-start = ((), (), s32[]{:S(2)}) async-start(), calls=%async_computation.3 | async-start | bytes 4866048 | tf_op jit(solution)/shard_map/all_gather | solution.py:178
  10.4 309.2 %all-gather.23.cloned.1.call-start = ((), (), s32[]{:S(2)}) async-start(), calls=%async_computation.6 | async-start | bytes 16422912 | tf_op jit(solution)/shard_map/all_gather | solution.py:128
  12.5 489.2 %all-gather.19.cloned.1.call-start = ((), (), s32[]{:S(2)}) async-start(), calls=%async_computation.4 | async-start | bytes 8650752 | tf_op jit(solution)/shard_map/all_gather | solution.py:180
  13.1 502.0 %all-gather.13.cloned.1.call-start = ((), (), s32[]{:S(2)}) async-start(), calls=%async_computation.1 | async-start | bytes 10948608 | tf_op jit(solution)/shard_map/all_gather | solution.py:175
  13.7 561.4 %all-gather.15.cloned.1.call-start = ((), (), s32[]{:S(2)}) async-start(), calls=%async_computation.2 | async-start | bytes 10948608 | tf_op jit(solution)/shard_map/all_gather | solution.py:177
  14.4 673.0 %all-gather.11.cloned.1.call-start = ((), (), s32[]{:S(2)}) async-start(), calls=%async_computation | async-start | bytes 16422912 | tf_op jit(solution)/shard_map/all_gather | solution.py:126
  15.2 1024.3 %all-reduce.31.cloned.1.call-start = ((), (), s32[]{:S(2)}) async-start(), calls=%async_computation.9 | async-start | bytes 294912
  67.6 60.3 %copy-start.50 = (s32[128]{0:T(128)}, s32[128]{0:T(128)S(1)}, u32[]{:S(2)}) copy-start(s32[128]{0:T(128)S(1)} %convert_reduce_fusion.9) | copy-start | bytes 1540
  67.7 60.2 %copy-start.55 = (f32[128]{0:T(128)}, f32[128]{0:T(128)S(1)}, u32[]{:S(2)}) copy-start(f32[128]{0:T(128)S(1)} %broadcast_multiply_fusion.1) | copy-start | bytes 1540
  68.0 60.0 %copy-start.62 = (f32[128]{0:T(128)}, f32[128]{0:T(128)S(1)}, u32[]{:S(2)}) copy-start(f32[128]{0:T(128)S(1)} %fusion.30) | copy-start | bytes 1540
  595.4 121.4 %copy-start.41 = (bf16[3,1152]{1,0:T(4,128)(2,1)S(1)}, bf16[3,1152]{1,0:T(4,128)(2,1)}, u32[]{:S(2)}) copy-start(bf16[3,1152]{1,0:T(4,128)(2,1)} %param.21) | copy-start | bytes 20740
  716.8 7.7 copy-start.51
  726.5 4.8 copy-start.12
  737.8 5.1 copy-start.45
  742.9 3.8 copy-start.43
  746.2 43.0 %copy-start.1 = (f32[128,1152]{1,0:T(8,128)}, f32[128,1152]{1,0:T(8,128)S(1)}, u32[]{:S(2)}) copy-start(f32[128,1152]{1,0:T(8,128)S(1)} %get-tuple-element.60) | copy-start | bytes 1769476
  746.2 43.0 %copy-start.48 = (f32[128]{0:T(128)}, f32[128]{0:T(128)S(1)}, u32[]{:S(2)}) copy-start(f32[128]{0:T(128)S(1)} %broadcast_multiply_fusion) | copy-start | bytes 1540
  746.4 42.8 %copy-start.58 = (f32[128]{0:T(128)}, f32[128]{0:T(128)S(1)}, u32[]{:S(2)}) copy-start(f32[128]{0:T(128)S(1)} %fusion.56) | copy-start | bytes 1540
  746.7 6.0 copy-start.17
  746.7 6.0 copy-start.54
  746.7 13.8 slice-start.3
  746.7 14.7 slice-start.5
  752.6 21.2 copy-start.3
  752.7 7.8 slice-start.4
  752.7 7.8 copy-start.44
  752.7 8.7 slice-start.6
  761.4 5.8 copy-start.14
  767.2 3.7 copy-start.37
  767.2 3.7 copy-start.39
  770.9 13.5 slice-start
  773.8 16.1 copy-start.10
  773.9 10.5 slice-start.1
  773.9 10.5 slice-start.2
  789.2 3.1 copy-start
  798.9 3.0 copy-start.9
  798.9 3.0 copy-start.31
  798.9 3.0 copy-start.57
  801.9 7.8 copy-start.20
  801.9 7.8 copy-start.35
  809.8 3.8 copy-start.26
  809.8 3.8 copy-start.28
  813.6 5.0 copy-start.13
  818.5 7.8 copy-start.15
  818.5 7.8 copy-start.38
  842.7 5.5 copy-start.6
  842.7 6.4 copy-start.2
  842.7 6.4 copy-start.49
  842.7 6.4 copy-start.59
  843.5 6.8 copy-start.11
  843.5 6.8 copy-start.36
  845.9 5.3 copy-start.52
  849.1 6.3 copy-start.46
  849.1 6.3 copy-start.47
  849.1 7.6 copy-start.23
  849.1 7.6 copy-start.24
  856.7 287.5 %all-reduce.29.cloned.1.call-start = ((), (), s32[]{:S(2)}) async-start(), calls=%async_computation.8 | async-start | bytes 12582912
  906.9 1967.9 %all-reduce.33.cloned.1.call-start = ((), (), s32[]{:S(2)}) async-start(), calls=%async_computation.10 | async-start | bytes 243531776
  917.4 22.6 copy-start.16
  917.4 22.6 copy-start.18
  948.8 30.2 %copy-start.42 = (bf16[3,1152]{1,0:T(4,128)(2,1)S(1)}, bf16[3,1152]{1,0:T(4,128)(2,1)}, u32[]{:S(2)}) copy-start(bf16[3,1152]{1,0:T(4,128)(2,1)} %param.21) | copy-start | bytes 20740
  (18 other events, 33.2 us)
Sparse Core Ops, SparseCore 0:
  11.5 69.1 all-gather.24
  83.6 57.3 all-gather.20
  144.0 62.4 all-gather.16
  209.8 109.7 all-gather.22
  322.3 75.6 all-gather.18
  400.8 85.7 all-gather.12
  489.4 85.5 all-gather.14
  578.0 109.4 all-gather.10
  856.8 121.9 all-reduce.30
  985.2 158.9 all-reduce.28
  1150.7 1724.1 all-reduce.32
where the time goes:
time: 2910 us; the launch traced here: 2900 us
  waiting for transfers between devices  2150 us (74%)
  local copies, waits for them, and re-layouts  317 us (11%)
  other arithmetic  231 us (8%)
  matrix products  150 us (5%)
  blocking collectives  43.7 us (2%)
    unnamed x14, waiting for transfers between devices  1830 us
    all_gather x1, other arithmetic, per_device(): lax.all_gather(qkv_weight, 'fsdp', axis=0, tiled=True)  167 us
    reshape x13, local copies, waits for them, and re-layouts, by_owner(): return values.reshape(owners, -1)  143 us
    all_gather x1, waiting for transfers between devices, per_device(): lax.all_gather(qkv_weight, 'fsdp', axis=0, tiled=True)  105 us
    all_gather x1, waiting for transfers between devices, per_device(): lax.all_gather(ada_weight, 'fsdp', axis=0, tiled=True)  92 us
    all_gather x1, waiting for transfers between devices, per_device(): lax.all_gather(projector_in, 'fsdp', axis=0, tiled=True)  59 us
  transfers between devices with their start and end apart: 11, of which 8 were waited for; matrix products, arithmetic and copies ran while one was open for 17% of the time, Pallas kernels for 0%

commit v1 on v0

--- a/solution.py
+++ b/solution.py
@@ -1,6 +1,10 @@
+import functools
+
 import jax
 import jax.numpy as jnp
 from jax import lax
+from jax.experimental import pallas as pl
+from jax.experimental.pallas import tpu as pltpu
 from jax.sharding import PartitionSpec as P
 
 D = 1152
@@ -97,6 +101,303 @@
         gathered[7].reshape(P_SIZE, Z),
         gathered[8].astype(jnp.float32),
     )
+
+
+MESH = pl.DeviceIdType.MESH
+
+class Place:
+    def __init__(self, n):
+        self.me = me = lax.axis_index("fsdp")
+        self.Z = n // 8
+        self.z, self.y, self.x, self.c = me // 8, (me // 4) % 2, (me // 2) % 2, me % 2
+        self.xp = me + 2 - 4 * self.x
+        self.yp = me + 4 - 8 * self.y
+        self.cp = me + 1 - 2 * self.c
+
+def barrier(pc):
+    sem = pltpu.get_barrier_semaphore()
+    for q in (pc.xp, pc.yp, pc.cp):
+        pl.semaphore_signal(sem, inc=1, device_id=(q,), device_id_type=MESH)
+    @pl.when(pc.z > 0)
+    def _():
+        pl.semaphore_signal(sem, inc=1, device_id=(pc.me - 8,), device_id_type=MESH)
+    @pl.when(pc.z < pc.Z - 1)
+    def _():
+        pl.semaphore_signal(sem, inc=1, device_id=(pc.me + 8,), device_id_type=MESH)
+    ends = (pc.z == 0).astype(jnp.int32) + (pc.z == pc.Z - 1).astype(jnp.int32)
+    pl.semaphore_wait(sem, 5 - ends)
+
+def region(out, quart, zs, y, x, c, off, w):
+    if quart:
+        q = out.shape[3] // 4
+        col = pl.multiple_of((x * 2 + c) * q + off, 128)
+        return out.at[zs, y, :, pl.ds(col, w)]
+    return out.at[zs, y, x, c, :, pl.ds(off, w)]
+
+def ag_kernel(n, quarts, rounds, offs, *refs):
+    na = len(quarts)
+    ins, outs = refs[:na], refs[na:2 * na]
+    lsem, zs_sem, zr_sem, xs_sem, xr_sem, cs_sem, cr_sem = refs[2 * na:]
+    pc = Place(n)
+    Z = pc.Z
+    z, y, x, c = pc.z, pc.y, pc.x, pc.c
+    barrier(pc)
+    def reg(r, zs, y_, x_, c_=None):
+        a, off, w = rounds[r]
+        return region(outs[a], quarts[a], zs, y_, x_, c if c_ is None else c_, off, w)
+    def own_in(r):
+        a, off, w = rounds[r]
+        return ins[a].at[:, pl.ds(off, w)]
+    def rcopy(src, dst, ss, rs, dev):
+        return pltpu.make_async_remote_copy(src_ref=src, dst_ref=dst, send_sem=ss, recv_sem=rs, device_id=(dev,), device_id_type=MESH)
+    def zcopy(r, side, s, src=None):
+        org = z - s if side == 0 else z + s
+        dst = reg(r, org, y, x)
+        return rcopy(own_in(r) if s == 0 else dst, dst, zs_sem.at[r, side, s], zr_sem.at[r, side, s], pc.me + (8 if side == 0 else -8))
+    def zrecv(r, side, s):
+        org = z - 1 - s if side == 0 else z + 1 + s
+        d = reg(r, org, y, x)
+        rcopy(d, d, zs_sem.at[r, side, s], zr_sem.at[r, side, s], pc.me).wait_recv()
+    def local(r):
+        return pltpu.make_async_copy(own_in(r), reg(r, z, y, x), lsem.at[r])
+    allz = slice(None); lo = slice(0, Z // 2); hi = slice(Z // 2, Z)
+    def xy(r, k):
+        if k == 0:
+            d = reg(r, allz, y, x); return rcopy(d, d, xs_sem.at[r, 0], xr_sem.at[r, 0], pc.xp)
+        if k == 1:
+            d = reg(r, allz, y, x); return rcopy(d, d, xs_sem.at[r, 1], xr_sem.at[r, 1], pc.yp)
+        if k == 2:
+            d = reg(r, lo, y, 1 - x); return rcopy(d, d, xs_sem.at[r, 2], xr_sem.at[r, 2], pc.yp)
+        d = reg(r, hi, 1 - y, x); return rcopy(d, d, xs_sem.at[r, 3], xr_sem.at[r, 3], pc.xp)
+    def core(r, k):
+        d = reg(r, allz, y if k in (0, 1) else 1 - y, x if k in (0, 2) else 1 - x)
+        return rcopy(d, d, cs_sem.at[r, k], cr_sem.at[r, k], pc.cp)
+    R = len(rounds)
+    def zstart(r, s):
+        @pl.when((z - s >= 0) & (z < Z - 1))
+        def _(): zcopy(r, 0, s).start()
+        @pl.when((z + s <= Z - 1) & (z > 0))
+        def _(): zcopy(r, 1, s).start()
+    def zwait(r, s):
+        @pl.when(z - 1 - s >= 0)
+        def _(): zrecv(r, 0, s)
+        @pl.when(z + 1 + s <= Z - 1)
+        def _(): zrecv(r, 1, s)
+    def stage(r, s):
+        if s == 0:
+            local(r).start()
+            zstart(r, 0)
+        elif s < Z - 1:
+            zwait(r, s - 1)
+            zstart(r, s)
+        elif s == Z - 1:
+            zwait(r, s - 1)
+            local(r).wait()
+            xy(r, 0).start(); xy(r, 1).start(); core(r, 0).start()
+        elif s == Z:
+            xy(r, 0).wait_recv(); xy(r, 2).start(); core(r, 1).start()
+            xy(r, 1).wait_recv(); xy(r, 3).start(); core(r, 2).start()
+        elif s == Z + 1:
+            xy(r, 2).wait_recv(); xy(r, 3).wait_recv(); core(r, 3).start()
+        elif s == Z + 2:
+            for k in range(4): core(r, k).wait_recv()
+    S = Z + 3
+    last = R - 1 + offs[S - 1]
+    for t in range(last + 1):
+        for s in reversed(range(S)):
+            r = t - offs[s]
+            if 0 <= r < R:
+                stage(r, s)
+    for r in range(R):
+        for s in range(Z - 1):
+            @pl.when((z - s >= 0) & (z < Z - 1))
+            def _(): zcopy(r, 0, s).wait_send()
+            @pl.when((z + s <= Z - 1) & (z > 0))
+            def _(): zcopy(r, 1, s).wait_send()
+        for k in range(4):
+            xy(r, k).wait_send(); core(r, k).wait_send()
+
+def all_gather(n, shards, quarts, rounds, offs, cid):
+    Z = n // 8
+    shapes = []
+    for sh, qt in zip(shards, quarts):
+        k, w = sh.shape
+        shapes.append(jax.ShapeDtypeStruct((Z, 2, k, 4 * w) if qt else (Z, 2, 2, 2, k, w), sh.dtype))
+    R = len(rounds)
+    D = pltpu.SemaphoreType.DMA
+    return pl.pallas_call(
+        functools.partial(ag_kernel, n, quarts, rounds, offs),
+        out_shape=shapes,
+        in_specs=[pl.BlockSpec(memory_space=pltpu.HBM)] * len(shards),
+        out_specs=[pl.BlockSpec(memory_space=pltpu.HBM)] * len(shards),
+        scratch_shapes=[D((R,)), D((R, 2, Z - 1)), D((R, 2, Z - 1)), D((R, 4)), D((R, 4)), D((R, 4)), D((R, 4))],
+        compiler_params=pltpu.CompilerParams(collective_id=cid, has_side_effects=True),
+    )(*shards)
+
+
+def rs_kernel(n, quarts, rounds, cls, slots, offs, *refs):
+    na = len(quarts)
+    ncls = len(slots)
+    R = len(rounds)
+    ins, outs = refs[:na], refs[na:2 * na]
+    rest = list(refs[2 * na:])
+    S0 = rest[:ncls]; rest = rest[ncls:]
+    CR = rest[:ncls]; rest = rest[ncls:]
+    XR = rest[:R]; rest = rest[R:]
+    ZR = rest[:R]; rest = rest[R:]
+    lsem, cs, cr, xs, xr, zs_, zr, credit = rest
+    pc = Place(n)
+    Z = pc.Z; H = Z // 2
+    z, y, x, c = pc.z, pc.y, pc.x, pc.c
+    barrier(pc)
+    slot, seen = [], [0] * ncls
+    prev = []
+    for r in range(R):
+        k = cls[r]
+        slot.append(seen[k] % slots[k])
+        prior = [q for q in range(r) if cls[q] == k and (slot[q] == seen[k] % slots[k])]
+        prev.append(prior[-1] if prior else None)
+        seen[k] += 1
+    def rcopy(src, dst, ss, rs, dev):
+        return pltpu.make_async_remote_copy(src_ref=src, dst_ref=dst, send_sem=ss, recv_sem=rs, device_id=(dev,), device_id_type=MESH)
+    def s0(r): return S0[cls[r]].at[slot[r]]
+    def crb(r): return CR[cls[r]].at[slot[r]]
+    def src(r, x_, c_):
+        a, off, w = rounds[r]
+        return region(ins[a], quarts[a], slice(None), slice(None), x_, c_, off, w)
+    def load(r, x_): return pltpu.make_async_copy(src(r, x_, c), s0(r).at[x_], lsem.at[r, x_])
+    def core(r, x_): return rcopy(src(r, x_, 1 - c), crb(r).at[x_], cs.at[r, x_], cr.at[r, x_], pc.cp)
+    def xy(r, k):
+        b = s0(r)
+        if k == 0: return rcopy(b.at[1 - x, 0:H, 1 - y], XR[r].at[0:H], xs.at[r, 0], xr.at[r, 0], pc.yp)
+        if k == 1: return rcopy(b.at[1 - x, H:Z, 1 - y], XR[r].at[H:Z], xs.at[r, 1], xr.at[r, 1], pc.xp)
+        if k == 2: return rcopy(b.at[1 - x, :, y], XR[r].at[Z:2 * Z], xs.at[r, 2], xr.at[r, 2], pc.xp)
+        return rcopy(b.at[x, :, 1 - y], XR[r].at[2 * Z:3 * Z], xs.at[r, 3], xr.at[r, 3], pc.yp)
+    def zc(r, side, d):
+        return rcopy(XR[r].at[Z + d], ZR[r].at[side, d], zs_.at[r, side, d], zr.at[r, side, d], jnp.clip(pc.me + (8 if side == 0 else -8), 0, n - 1))
+    def waits_send(r):
+        for k in range(2): core(r, k).wait_send()
+        for k in range(4): xy(r, k).wait_send()
+    def zwaits_send(r):
+        for d in range(Z):
+            @pl.when(d > z)
+            def _(): zc(r, 0, d).wait_send()
+            @pl.when(d < z)
+            def _(): zc(r, 1, d).wait_send()
+    def zstep(r, s):
+        for side in (0, 1):
+            p = s if side == 0 else Z - 1 - s
+            @pl.when(z == p)
+            def _():
+                for d in range(Z):
+                    if (d > p) if side == 0 else (d < p):
+                        if s > 0:
+                            zc(r, side, d).wait_recv()
+                            XR[r][Z + d] = XR[r][Z + d] + ZR[r][side, d]
+                        zc(r, side, d).start()
+    def stage(r, s):
+        b, cb = s0(r), crb(r)
+        if s == 0:
+            if prev[r] is not None:
+                waits_send(prev[r])
+                pl.semaphore_wait(credit, 1)
+            for k in range(2):
+                core(r, k).start(); load(r, k).start()
+        elif s == 1:
+            for k in range(2):
+                load(r, k).wait(); core(r, k).wait_recv()
+            def add(i, _):
+                xx, zz, yy = i // (2 * Z), (i // 2) % Z, i % 2
+                b[xx, zz, yy] = b[xx, zz, yy] + cb[xx, zz, yy]
+                return _
+            lax.fori_loop(0, 4 * Z, add, 0)
+            if any(prev[q] == r for q in range(R)):
+                pl.semaphore_signal(credit, inc=1, device_id=(pc.cp,), device_id_type=MESH)
+            xy(r, 0).start(); xy(r, 1).start()
+        elif s == 2:
+            xy(r, 0).wait_recv()
+            def add(i, _):
+                b[1 - x, i, y] = b[1 - x, i, y] + XR[r][i]
+                return _
+            lax.fori_loop(0, H, add, 0)
+            xy(r, 2).start()
+            xy(r, 1).wait_recv()
+            def add(i, _):
+                b[x, i, 1 - y] = b[x, i, 1 - y] + XR[r][i]
+                return _
+            lax.fori_loop(H, Z, add, 0)
+            xy(r, 3).start()
+        elif s == 3:
+            xy(r, 2).wait_recv(); xy(r, 3).wait_recv()
+            def add(i, _):
+                XR[r][Z + i] = b[x, i, y] + XR[r][Z + i] + XR[r][2 * Z + i]
+                return _
+            lax.fori_loop(0, Z, add, 0)
+            zstep(r, 0)
+        elif s < Z + 2:
+            zstep(r, s - 3)
+        else:
+            a, off, w = rounds[r]
+            for d in range(Z):
+                @pl.when(d == z)
+                def _():
+                    tot = XR[r][Z + d].astype(jnp.float32)
+                    if d > 0:
+                        zc(r, 0, d).wait_recv()
+                        tot = tot + ZR[r][0, d].astype(jnp.float32)
+                    if d < Z - 1:
+                        zc(r, 1, d).wait_recv()
+                        tot = tot + ZR[r][1, d].astype(jnp.float32)
+                    outs[a][:, off:off + w] = tot
+    S = Z + 3
+    last = R - 1 + offs[S - 1]
+    for t in range(last + 1):
+        for s in reversed(range(S)):
+            r = t - offs[s]
+            if 0 <= r < R:
+                stage(r, s)
+    for r in range(R):
+        zwaits_send(r)
+        if not any(prev[q] == r for q in range(R)):
+            waits_send(r)
+
+def reduce_scatter(n, grads, quarts, rounds, cls, slots, offs, cid):
+    Z = n // 8
+    shapes, R = [], len(rounds)
+    for g, qt in zip(grads, quarts):
+        shapes.append(jax.ShapeDtypeStruct((g.shape[2], g.shape[3] // 4) if qt else g.shape[4:], jnp.float32))
+    dims = []
+    for a, off, w in rounds:
+        dims.append((shapes[a].shape[0], w))
+    cdims = [next(dims[r] for r in range(R) if cls[r] == k) for k in range(len(slots))]
+    for r in range(R): assert dims[r] == cdims[cls[r]], (r, dims[r], cdims)
+    D = pltpu.SemaphoreType.DMA
+    bf = jnp.bfloat16
+    scratch = [pltpu.VMEM((slots[k], 2, Z, 2) + cdims[k], bf) for k in range(len(slots))] * 2
+    scratch += [pltpu.VMEM((3 * Z,) + dims[r], bf) for r in range(R)]
+    scratch += [pltpu.VMEM((2, Z) + dims[r], bf) for r in range(R)]
+    scratch += [D((R, 2)), D((R, 2)), D((R, 2)), D((R, 4)), D((R, 4)), D((R, 2, Z)), D((R, 2, Z)), pltpu.SemaphoreType.REGULAR]
+    return pl.pallas_call(
+        functools.partial(rs_kernel, n, quarts, rounds, cls, slots, offs),
+        out_shape=shapes,
+        in_specs=[pl.BlockSpec(memory_space=pltpu.HBM)] * len(grads),
+        out_specs=[pl.BlockSpec(memory_space=pltpu.VMEM)] * len(grads),
+        scratch_shapes=scratch,
+        compiler_params=pltpu.CompilerParams(collective_id=cid, has_side_effects=True, vmem_limit_bytes=62 * 2**20),
+    )(*grads)
+
+GATHER_ROUNDS = ((0, 0, 128),) + tuple(
+    (array, at * width, width)
+    for array, width, count in ((1, 384, 3), (2, 384, 3), (3, 384, 3), (4, 512, 1), (5, 1024, 2), (6, 768, 1))
+    for at in range(count)
+)
+SCATTER_ROUNDS = tuple(
+    (array, at * width, width)
+    for array, width, count in ((0, 768, 1), (1, 1024, 2), (2, 512, 1), (3, 384, 3), (4, 384, 3), (5, 384, 3), (6, 128, 1))
+    for at in range(count)
+)
+SCATTER_CLASSES = (0, 1, 1, 2, 3, 3, 3, 3, 3, 3, 3, 3, 3, 4)
+SCATTER_SLOTS = (1, 2, 1, 3, 1)
 
 
 def per_device(
@@ -376,6 +677,294 @@
     )
 
 
+def per_device_kernels(
+    tokens,
+    cond,
+    image_lengths,
+    ada_weight,
+    ada_bias,
+    qkv_weight,
+    qv_bias,
+    attn_weight,
+    tail_bias,
+    up_weight,
+    up_bias,
+    down_weight,
+    projector_in,
+    projector_in_bias,
+    projector_mid,
+    projector_mid_bias,
+    projector_out,
+    projector_out_bias,
+    targets,
+    out_grad,
+):
+    owners = lax.axis_size("fsdp")
+    me = lax.axis_index("fsdp")
+    groups = [[4 * g + i for i in range(4)] for g in range(owners // 4)]
+    row_count = tokens.shape[0]
+    rows = D // owners
+    row_sharded = jnp.concatenate(
+        [
+            qkv_weight.reshape(rows, 3 * D),
+            attn_weight.reshape(rows, D),
+            up_weight.reshape(rows, FF),
+            projector_in.reshape(rows, P_SIZE),
+        ],
+        axis=1,
+    )
+    quarters = jnp.concatenate(
+        [part.reshape(rows, 4, -1) for part in jnp.split(row_sharded, (4 * D, 8 * D), axis=1)], axis=2
+    ).transpose(1, 0, 2)
+    quarters = lax.all_to_all(
+        quarters, "fsdp", 0, 0, axis_index_groups=groups, tiled=True
+    ).reshape(4 * rows, -1)
+    bias_row = jnp.concatenate(
+        [ada_bias, qv_bias, tail_bias, up_bias, projector_in_bias, projector_mid_bias, projector_out_bias]
+    )
+    bias_width = bias_row.shape[0]
+    bias_row = jnp.pad(bias_row, (0, 2048 - bias_width)).reshape(16, 128)
+    gathered = all_gather(
+        owners,
+        (
+            bias_row,
+            quarters[:, :D],
+            quarters[:, D : 2 * D],
+            down_weight.reshape(-1, D),
+            quarters[:, 2 * D :],
+            projector_mid.reshape(-1, P_SIZE),
+            projector_out.reshape(-1, Z),
+        ),
+        (False, True, True, False, True, False, False),
+        GATHER_ROUNDS,
+        (0, 1, 2, 3, 5, 7, 8),
+        1,
+    )
+    bias_all = gathered[0].reshape(owners, 2048)[:, :bias_width].astype(jnp.float32)
+    widths = (6 * D, 2 * D, 2 * D, FF, P_SIZE, P_SIZE, Z)
+    ends, at = [], 0
+    for width in widths:
+        at += width // owners
+        ends.append(at)
+    (
+        ada_bias_full, qv_full, tail_full, up_bias_full, proj_in_bias_full, proj_mid_bias_full, proj_out_bias_full
+    ) = [part.reshape(-1) for part in jnp.split(bias_all, ends[:-1], axis=1)]
+    first_full = gathered[1].reshape(D, 4 * D)
+    qkv_full, attn_full = first_full[:, : 3 * D], first_full[:, 3 * D :]
+    up_full = gathered[2].reshape(D, FF)
+    down_full = gathered[3].reshape(FF, D)
+    proj_in_full = gathered[4].reshape(D, P_SIZE)
+    proj_mid_full = gathered[5].reshape(P_SIZE, P_SIZE)
+    proj_out_full = gathered[6].reshape(P_SIZE, Z)
+    cond_values = cond.astype(jnp.float32)
+    cond_low = lowered(sigmoid_linear(cond_values))
+    cond_all = lax.all_gather(cond_low, "fsdp", axis=0, tiled=True)
+    cond_mine = lax.dynamic_slice(cond_all, (0, me * rows), (cond_all.shape[0], rows))
+    ada_mine = ada_weight.reshape(rows, 6 * D)
+    modulation = (
+        lax.psum_scatter(matmul(cond_mine, ada_mine), "fsdp", scatter_dimension=0, tiled=True)
+        + ada_bias_full
+    )
+    image_of, onehot = image_onehot(image_lengths[0], row_count)
+    per_token = jnp.dot(onehot, modulation, precision=PRECISE)
+    shift_one, scale_one, gate_one, shift_two, scale_two, gate_two = jnp.split(per_token, 6, axis=1)
+    inputs = tokens.astype(jnp.float32)
+    normed_one = layer_norm(inputs)
+    first_in = lowered(normed_one * (1.0 + scale_one) + shift_one)
+    key_zero = jnp.zeros((D,), jnp.float32)
+    bias_full = jnp.concatenate([qv_full[:D], key_zero, qv_full[D:]])
+    projected = lowered(matmul(first_in, qkv_full) + bias_full)
+    queries = projected[:, :D].reshape(row_count, HEADS, HD)
+    keys_all = projected[:, D : 2 * D].reshape(row_count, HEADS, HD)
+    values_all = projected[:, 2 * D :].reshape(row_count, HEADS, HD)
+    same_image = (image_of[:, None] == image_of[None, :])[None]
+    score_scale = HD ** (-0.5)
+
+    def masked_scores():
+        raw_scores = (
+            jnp.einsum("qhd,khd->hqk", queries, keys_all, preferred_element_type=jnp.float32)
+            * score_scale
+        )
+        return jnp.where(same_image, raw_scores, -1e30)
+
+    masked = masked_scores()
+    row_max = jnp.max(masked, axis=-1, keepdims=True)
+    exp_scores = jnp.exp(masked - row_max)
+    row_total = jnp.sum(exp_scores, axis=-1, keepdims=True)
+    attn_probs = exp_scores / row_total
+    head_out = jnp.einsum(
+        "hqk,khd->qhd", lowered(attn_probs), values_all, preferred_element_type=jnp.float32
+    )
+    heads_low = lowered(head_out.reshape(row_count, D))
+    branch_attn = matmul(heads_low, attn_full) + tail_full[:D]
+    middle = inputs + gate_one * branch_attn
+    normed_two = layer_norm(middle)
+    second_in = lowered(normed_two * (1.0 + scale_two) + shift_two)
+    up_pre = matmul(second_in, up_full) + up_bias_full
+    up_act = lowered(gelu_tanh(up_pre))
+    branch_mlp = matmul(up_act, down_full) + tail_full[D:]
+    hidden = middle + gate_two * branch_mlp
+    mixed = lowered(hidden)
+    first_pre = matmul(mixed, proj_in_full) + proj_in_bias_full
+    first_act = lowered(sigmoid_linear(first_pre))
+    second_pre = matmul(first_act, proj_mid_full) + proj_mid_bias_full
+    second_act = lowered(sigmoid_linear(second_pre))
+    features = matmul(second_act, proj_out_full) + proj_out_bias_full
+    target_values = targets.astype(jnp.float32)
+
+    def cosine_loss(values):
+        value_norm = jnp.sqrt(jnp.sum(values * values, axis=1) + EPSILON)
+        target_norm = jnp.sqrt(jnp.sum(target_values * target_values, axis=1) + EPSILON)
+        return -0.5 * jnp.sum(jnp.sum(values * target_values, axis=1) / (value_norm * target_norm))
+
+    feature_grad = lowered(jax.grad(cosine_loss)(features))
+    grad_proj_out = transposed_left(second_act, feature_grad)
+    second_back = lowered(
+        pull_back(sigmoid_linear, second_pre, transposed_right(feature_grad, proj_out_full))
+    )
+    grad_proj_mid = transposed_left(first_act, second_back)
+    first_back = lowered(
+        pull_back(sigmoid_linear, first_pre, transposed_right(second_back, proj_mid_full))
+    )
+    grad_proj_in = transposed_left(mixed, first_back)
+    hidden_grad = out_grad.astype(jnp.float32) + transposed_right(first_back, proj_in_full)
+    gate_two_grad = hidden_grad * branch_mlp
+    branch_mlp_grad = lowered(hidden_grad * gate_two)
+    grad_down = transposed_left(up_act, branch_mlp_grad)
+    up_grad = lowered(pull_back(gelu_tanh, up_pre, transposed_right(branch_mlp_grad, down_full)))
+    grad_up = transposed_left(second_in, up_grad)
+    second_in_grad = transposed_right(up_grad, up_full)
+    middle_grad = hidden_grad + pull_back(layer_norm, middle, second_in_grad * (1.0 + scale_two))
+    gate_one_grad = middle_grad * branch_attn
+    branch_attn_grad = lowered(middle_grad * gate_one)
+    grad_attn = transposed_left(heads_low, branch_attn_grad)
+    heads_grad = lowered(transposed_right(branch_attn_grad, attn_full)).reshape(
+        row_count, HEADS, HD
+    )
+    again_probs = jnp.exp(masked_scores() - row_max) / row_total
+    prob_grad = jnp.einsum(
+        "qhd,khd->hqk", heads_grad, values_all, preferred_element_type=jnp.float32
+    )
+    value_grad = jnp.einsum(
+        "hqk,qhd->khd", lowered(again_probs), heads_grad, preferred_element_type=jnp.float32
+    )
+    score_grad = lowered(
+        again_probs * (prob_grad - jnp.sum(again_probs * prob_grad, axis=-1, keepdims=True))
+    )
+    query_grad = (
+        jnp.einsum("hqk,khd->qhd", score_grad, keys_all, preferred_element_type=jnp.float32)
+        * score_scale
+    )
+    key_grad = (
+        jnp.einsum("hqk,qhd->khd", score_grad, queries, preferred_element_type=jnp.float32)
+        * score_scale
+    )
+    projected_grad = lowered(
+        jnp.concatenate(
+            [
+                query_grad.reshape(row_count, D),
+                key_grad.reshape(row_count, D),
+                value_grad.reshape(row_count, D),
+            ],
+            axis=1,
+        )
+    )
+    grad_qkv = transposed_left(first_in, projected_grad)
+    projected_sums = column_sums(projected_grad)
+    grad_qv_bias = jnp.concatenate([projected_sums[:D], projected_sums[2 * D :]])
+    first_in_grad = transposed_right(projected_grad, qkv_full)
+    input_grad = middle_grad + pull_back(layer_norm, inputs, first_in_grad * (1.0 + scale_one))
+    token_mod_grad = jnp.concatenate(
+        [
+            first_in_grad,
+            first_in_grad * normed_one,
+            gate_one_grad,
+            second_in_grad,
+            second_in_grad * normed_two,
+            gate_two_grad,
+        ],
+        axis=1,
+    )
+    modulation_grad = lowered(
+        lax.dot_general(onehot, token_mod_grad, (((0,), (0,)), ((), ())), precision=PRECISE)
+    )
+    modulation_all = lax.all_gather(modulation_grad, "fsdp", axis=0, tiled=True)
+    grad_ada = transposed_left(cond_mine, modulation_all)
+    cond_back = transposed_right(modulation_all, ada_mine)
+    cond_back = lax.all_to_all(cond_back, "fsdp", 0, 1, tiled=True)
+    cond_grad = pull_back(sigmoid_linear, cond_values, cond_back).astype(jnp.bfloat16)
+    grad_ada_bias = lax.dynamic_slice(
+        column_sums(modulation_all), (me * (6 * D // owners),), (6 * D // owners,)
+    )
+    grad_tail = jnp.concatenate([column_sums(branch_attn_grad), column_sums(branch_mlp_grad)])
+    bias_grads = jnp.concatenate(
+        [
+            by_owner(part, owners)
+            for part in (
+                grad_qv_bias,
+                grad_tail,
+                column_sums(up_grad),
+                column_sums(first_back),
+                column_sums(second_back),
+                column_sums(feature_grad),
+            )
+        ],
+        axis=1,
+    )
+    bias_grads = jnp.pad(bias_grads, ((0, 0), (0, 2048 - bias_grads.shape[1])))
+    lines = owners // 8
+    summed = reduce_scatter(
+        owners,
+        (
+            lowered(grad_proj_out).reshape(lines, 2, 2, 2, -1, Z),
+            lowered(grad_proj_mid).reshape(lines, 2, 2, 2, -1, P_SIZE),
+            lowered(grad_proj_in).reshape(lines, 2, -1, P_SIZE),
+            lowered(grad_down).reshape(lines, 2, 2, 2, -1, D),
+            lowered(grad_up).reshape(lines, 2, -1, FF),
+            jnp.concatenate([lowered(grad_qkv), lowered(grad_attn)], axis=1).reshape(lines, 2, -1, 4 * D),
+            lowered(bias_grads).reshape(lines, 2, 2, 2, 16, 128),
+        ),
+        (False, False, True, False, True, True, False),
+        SCATTER_ROUNDS,
+        SCATTER_CLASSES,
+        SCATTER_SLOTS,
+        (0, 1, 2, 3, 4, 5, 6),
+        2,
+    )
+    back = jnp.concatenate([summed[5], summed[4], summed[2]], axis=1)
+    back = lax.all_to_all(back, "fsdp", 0, 0, axis_index_groups=groups, tiled=True)
+    back = back.reshape(4, rows, -1).transpose(1, 0, 2)
+    first_rows = back[:, :, :D].reshape(rows, 4 * D)
+    up_rows = back[:, :, D : 2 * D].reshape(-1)
+    proj_in_rows = back[:, :, 2 * D :].reshape(-1)
+    small = summed[6].reshape(-1)
+    small_parts, at = [], 0
+    for width in widths[1:]:
+        small_parts.append(small[at : at + width // owners])
+        at += width // owners
+    qv_sum, tail_sum, up_bias_sum, in_sum, mid_sum, out_sum = small_parts
+    return (
+        mixed,
+        input_grad.astype(jnp.bfloat16),
+        cond_grad,
+        grad_ada.reshape(-1),
+        grad_ada_bias,
+        first_rows[:, : 3 * D].reshape(-1),
+        qv_sum,
+        first_rows[:, 3 * D :].reshape(-1),
+        tail_sum,
+        up_rows,
+        up_bias_sum,
+        summed[3].reshape(-1),
+        proj_in_rows,
+        in_sum,
+        summed[1].reshape(-1),
+        mid_sum,
+        summed[0].reshape(-1),
+        out_sum,
+    )
+
+
 def solution(mesh):
     in_specs = (
         P("fsdp", None),
@@ -419,6 +1008,8 @@
         P("fsdp"),
         P("fsdp"),
     )
+    owners = mesh.shape["fsdp"]
+    program = per_device_kernels if owners % 16 == 0 and D % owners == 0 else per_device
     return jax.shard_map(
-        per_device, mesh=mesh, in_specs=in_specs, out_specs=out_specs, check_vma=False
-    )
+        program, mesh=mesh, in_specs=in_specs, out_specs=out_specs, check_vma=False
+    )

time: 2910 us -> 732 us (0.25)
  waiting for transfers between devices: 2150 us -> 24.9 us
  Pallas kernels: 0 us -> 456 us
  local copies, waits for them, and re-layouts: 317 us -> 48.8 us
  other arithmetic: 231 us -> 20.7 us
  matrix products: 150 us -> 107 us
    unnamed x14 -> x3, waiting for transfers between devices: 1830 us -> 0.03 us
    pallas_call x0 -> x2, Pallas kernels: none -> 456 us  [the longest x1 230 us: reduce_scatter(): pl.pallas_call(functools.partial(rs_kernel, n, quarts, rounds, cls, slots...]
    all_gather x8 -> x1, waiting for transfers between devices: 316 us -> 0.01 us  [per_device_kernels(): modulation_all = lax.all_gather(modulation_grad, 'fsdp', axis=0, tiled=True)]
    all_gather x2 -> x0, other arithmetic: 214 us -> none  [the longest x1 167 us: per_device(): lax.all_gather(qkv_weight, 'fsdp', axis=0, tiled=True)]
    reshape x13 -> x4, local copies, waits for them, and re-layouts: 143 us -> 0.34 us  [by_owner(): return values.reshape(owners, -1)]
    reshape x13 -> x16, local copies, waits for them, and re-layouts: 127 us -> 14 us  [the longest x2 2.93 us: per_device_kernels(): ada_mine = ada_weight.reshape(rows, 6 * D)]
    all_gather x0 -> x1, blocking collectives: none -> 44 us  [per_device_kernels(): cond_all = lax.all_gather(cond_low, 'fsdp', axis=0, tiled=True)]
    unnamed x1 -> x0, blocking collectives: 43.7 us -> none
  transfers between devices with their start and end apart: 11 -> 5, of which waited for: 8 -> 3; matrix products, arithmetic and copies ran while one was open for 17% -> 7% of each run, Pallas kernels for 0% -> 63%
where the time goes in v1:
time: 732 us; the launch traced here: 726 us
  Pallas kernels  456 us (62%)
  matrix products  107 us (15%)
  local copies, waits for them, and re-layouts  48.8 us (7%)
  blocking collectives  44 us (6%)
  waiting for transfers between devices  24.9 us (3%)
  other arithmetic  20.7 us (3%)
  between operations  15.6 us (2%)
  starting transfers between devices  10.1 us (1%)
    pallas_call x1, Pallas kernels, reduce_scatter(): pl.pallas_call(functools.partial(rs_kernel, n, quarts, rounds, cls, slots...  230 us
    pallas_call x1, Pallas kernels, all_gather(): pl.pallas_call(functools.partial(ag_kernel, n, quarts, rounds, offs), out...  225 us
    all_gather x1, blocking collectives, per_device_kernels(): cond_all = lax.all_gather(cond_low, 'fsdp', axis=0, tiled=True)  44 us
    dot_general x8, matrix products, transposed_left(): lax.dot_general(left, right, (((0,), (0,)), ((), ())), preferred_element_...  32.2 us
    dot_general x8, matrix products, transposed_right(): lax.dot_general(left, right, (((1,), (1,)), ((), ())), preferred_element_...  31.3 us
    dot_general x8, matrix products, matmul(): return jnp.dot(left, right, preferred_element_type=jnp.float32)  27.4 us
  transfers between devices with their start and end apart: 5, of which 3 were waited for; matrix products, arithmetic and copies ran while one was open for 7% of the time, Pallas kernels for 63%

profile of v1, /device:TPU:0, one launch (start us, length us, event | category | flops | bytes accessed | tf_op | source)
XLA Modules:
  0.0 726.4 jit_solution(9989390199080186266)
XLA Ops:
  7.2 1.6 reshape.328
  9.6 44.0 %all-gather = bf16[32,3,1152]{2,1,0:T(4,128)(2,1)S(1)} all-gather(bf16[1,3,1152]{2,1,0:T(4,128)(2,1)S(1)} %fusion.69), channel_id=1, replica_groups=mesh['fsdp'=32] {'fsdp'}, dimensions={0}, use_global_device_ids=true | all-gather | bytes 228096 | tf_op jit(solution)/shard_map/all_gather | solution.py:761
  53.8 2.1 fusion.60
  57.8 1.0 copy.82
  58.8 3.5 all-to-all-start
  65.3 1.1 reshape.334.refs_3_
  68.0 9.3 %all-to-all-done = bf16[4,36,2816]{2,1,0:T(8,128)(2,1)S(1)} async-done(((bf16[4,36,2816]{2,1,0:T(8,128)(2,1)}), bf16[4,36,2816]{2,1,0:T(8,128)(2,1)S(1)}, u32[]{:S(2)}, u32[]{:S(2)}) %all-to-all-start) | async-done | bytes 811040 | tf_op jit(solution)/shard_map/all_to_all | solution.py:719
  79.0 225.4 %shard_map.331 = (bf16[4,2,2,2,16,128]{5,4,3,2,1,0:T(8,128)(2,1)}, bf16[4,2,144,4608]{3,2,1,0:T(8,128)(2,1)}, bf16[4,2,144,4608]{3,2,1,0:T(8,128)(2,1)}, bf16[4,...) custom-call(bf16[16,128]{1,0:T(8,128)(2,1)} %pad_bitcast_fusion.1.re, ...), custom_call_target="tpu_custom_call" | custom-call | tf_op jit(solution)/shard_map/pallas_call | solution.py:228
  304.5 0.9 copy.113
  310.1 2.6 fusion.54
  312.8 1.3 fusion.42
  314.0 4.8 fusion.9
  318.9 0.9 fusion.96
  319.8 1.8 copy.83
  321.6 1.8 copy.84
  323.5 1.8 copy.85
  325.3 3.2 fusion.103
  328.5 2.6 convolution_convert_fusion.10
  331.1 3.3 fusion.94
  334.9 5.9 convolution_add_fusion
  340.9 7.8 %add_convert_fusion.1 = (bf16[128,1152]{1,0:T(8,128)(2,1)S(1)}, f32[128,1152]{1,0:T(8,128)}) fusion(f32[128,1152]{1,0:T(8,128)S(1)} %get-tuple-element.67, f32[128,6912]{1,0:T(8,128)S(1)} %fusion.54, f32[1152]{0:T(1024)S(1)} %copy-done.63, bf16[4608,1152]{1,0:T(8,128)(2,1)} %bitcast.167, f32[128,4608]{1,0:T(8,128)S(1)} %convolution_add_fusion), kind=kOutput, calls=%fused_computation.101 | convolution fusion | flops 1364852736 | bytes 15045120 | tf_op jit(solution)/shard_map/dot_general | solution.py:54
  348.7 1.3 convolution_add_fusion.4
  350.1 1.3 convolution_add_fusion.5
  351.5 0.9 copy-done.81
  354.0 1.8 fusion.84
  355.9 3.6 fusion.86
  359.6 2.4 fusion.91
  362.0 10.5 %fusion.88 = (bf16[4608]{0:T(1024)(128)(2,1)}, bf16[128,4608]{1,0:T(8,128)(2,1)}) fusion(f32[128,4608]{1,0:T(8,128)S(1)} %convolution_add_fusion, bf16[128,1152]{1,0:T(8,128)(2,1)} %get-tuple-element.61, bf16[4608,1152]{1,0:T(8,128)(2,1)} %bitcast.168), kind=kOutput, calls=%fused_computation.173 | convolution fusion | flops 1373695488 | bytes 14459904 | tf_op jit(solution)/shard_map/dot_general | solution.py:64
  372.5 4.8 multiply_reduce_fusion.1
  378.2 1.0 fusion.90
  379.9 3.4 convolution_convert_fusion.8
  383.3 1.8 copy.87
  385.1 2.7 convolution_convert_fusion.9
  387.8 1.9 multiply_reduce_fusion
  391.1 2.7 convolution_convert_fusion.7
  393.8 3.5 convolution_convert_fusion.5
  397.4 5.8 convolution_convert_fusion.1
  403.2 5.6 convolution_convert_fusion
  408.8 2.3 convolution_convert_fusion.4
  411.2 2.6 constant_dynamic-update-slice_fusion.1
  413.8 5.4 convolution_convert_fusion.2
  422.1 1.9 fusion.1
  425.6 8.9 %pad_maximum_fusion = bf16[1152,4608]{1,0:T(8,128)(2,1)} fusion(bf16[1152,1152]{1,0:T(8,128)(2,1)S(1)} %copy-done.4, bf16[1152,3456]{1,0:T(8,128)(2,1)} %convolution_convert_fusion.2), kind=kLoop, calls=%fused_computation.4 | loop fusion | flops 21233664 | bytes 21233664 | tf_op jit(solution)/shard_map/concatenate | solution.py:924
  434.6 5.6 convolution_convert_fusion.6
  440.2 230.2 %shard_map.332 = (f32[64,768]{1,0:T(8,128)}, f32[64,2048]{1,0:T(8,128)}, f32[144,512]{1,0:T(8,128)}, f32[144,1152]{1,0:T(8,128)}, f32[144,1152]{1,0:T(8,128)}, /*index=5*/f32[144,1152]{1,0:T(8,128)}, f32[16,128]{1,0:T(8,128)}) custom-call(bf16[4,2,2,2,64,768]{5,4,3,2,1,0:T(8,128)(2,1)} %bitcast.122, bf16[4,2,2,2,64,2048]{5,4,3,2,1,0:T(8,128)(2,1)} %bitcast.113, ...), custom_call_target="tpu_custom_call" | custom-call | tf_op jit(solution)/shard_map/pallas_call | solution.py:380
  670.5 1.5 pad_maximum_fusion.1
  672.0 1.4 all_to_all.25
  673.4 4.0 all-to-all-start.2
  677.4 1.4 reshape.377
  678.7 1.3 slice.155
  680.0 1.3 slice.159
  682.2 0.9 copy.107
  683.0 1.6 reshape.371
  684.7 1.3 fusion.101
  686.0 1.3 fusion.100
  687.3 12.5 %all-to-all-done.2 = f32[4,36,2816]{2,1,0:T(8,128)S(1)} async-done(((f32[4,36,2816]{2,1,0:T(8,128)}), f32[4,36,2816]{2,1,0:T(8,128)S(1)}, u32[]{:S(2)}, u32[]{:S(2)}) %all-to-all-start.2) | async-done | bytes 1622048 | tf_op jit(solution)/shard_map/all_to_all | solution.py:935
  701.9 1.6 reshape.366
  703.7 1.1 reshape.367
  705.8 2.1 fusion.25
  708.5 2.6 all-to-all-start.1
  711.1 1.2 reshape.375
  712.3 1.2 fusion.58
  713.8 1.0 reshape.351
  715.5 3.1 all-to-all-done.1
  (291 shorter events, 29.3 us)
Async XLA Ops:
  7.2 303.0 %all-reduce.5.cloned.1.call-start = ((), (), s32[]{:S(2)}) async-start(), calls=%async_computation.4 | async-start | bytes 5308416
  57.3 5.1 copy-start.82
  57.3 5.3 copy-start.7
  57.3 6.0 copy-start.74
  57.3 6.0 copy-start.75
  57.4 6.0 copy-start.76
  57.4 6.0 copy-start.77
  57.4 5.9 copy-start.78
  57.4 5.9 copy-start.79
  57.4 5.9 copy-start.80
  57.4 7.8 %copy-start.41 = (bf16[165888]{0:T(1024)(128)(2,1)S(1)}, bf16[165888]{0:T(1024)(128)(2,1)}, u32[]{:S(2)}) copy-start(bf16[165888]{0:T(1024)(128)(2,1)} %param.31) | copy-start | bytes 995332
  57.8 8.6 %copy-start.44 = (bf16[131072]{0:T(1024)(128)(2,1)S(1)}, bf16[131072]{0:T(1024)(128)(2,1)}, u32[]{:S(2)}) copy-start(bf16[131072]{0:T(1024)(128)(2,1)} %param.34) | copy-start | bytes 786436
  57.8 9.4 %copy-start.50 = (bf16[49152]{0:T(1024)(128)(2,1)S(1)}, bf16[49152]{0:T(1024)(128)(2,1)}, u32[]{:S(2)}) copy-start(bf16[49152]{0:T(1024)(128)(2,1)} %param.36) | copy-start | bytes 294916
  58.8 18.5 %all-to-all-start = ((bf16[4,36,2816]{2,1,0:T(8,128)(2,1)}), bf16[4,36,2816]{2,1,0:T(8,128)(2,1)S(1)}, u32[]{:S(2)}, u32[]{:S(2)}) async-start(bf16[4,36,2816]{2,1,0:T(8,128)(2,1)} %copy.82), calls=%async_computation | async-start | bytes 1802240 | tf_op jit(solution)/shard_map/all_to_all | solution.py:719
  62.3 643.4 %all-gather.4.cloned.1.call-start = ((), (), s32[]{:S(2)}) async-start(), calls=%async_computation.3 | async-start | bytes 1824768 | tf_op jit(solution)/shard_map/all_gather | solution.py:891
  62.9 5.0 copy-start.72
  63.4 241.1 %copy-start.60 = (s32[128]{0:T(128)}, s32[128]{0:T(128)S(1)}, u32[]{:S(2)}) copy-start(s32[128]{0:T(128)S(1)} %convert_reduce_fusion.2) | copy-start | bytes 1540
  310.1 3.9 copy-start.54
  314.0 4.8 copy-start.24
  331.1 3.8 copy-start.52
  334.4 42.9 %copy-start = (f32[128,1152]{1,0:T(8,128)}, f32[128,1152]{1,0:T(8,128)S(1)}, u32[]{:S(2)}) copy-start(f32[128,1152]{1,0:T(8,128)S(1)} %get-tuple-element.67) | copy-start | bytes 1769476
  334.4 42.9 %copy-start.55 = (f32[128]{0:T(128)}, f32[128]{0:T(128)S(1)}, u32[]{:S(2)}) copy-start(f32[128]{0:T(128)S(1)} %broadcast_multiply_fusion) | copy-start | bytes 1540
  334.6 42.7 %copy-start.66 = (f32[128]{0:T(128)}, f32[128]{0:T(128)S(1)}, u32[]{:S(2)}) copy-start(f32[128]{0:T(128)S(1)} %fusion.74) | copy-start | bytes 1540
  334.9 6.0 copy-start.14
  334.9 6.0 copy-start.63
  334.9 13.8 %slice-start.3 = ((s8[4718592]{0:T(1024)(128)(4,1)}), s8[4194304]{0:T(1024)(128)(4,1)S(1)}, s32[]{:S(2)}) async-start(s8[4718592]{0:T(1024)(128)(4,1)} %bitcast.116), calls=%async_computation.8 | async-start | bytes 8388608
  334.9 15.1 %slice-start.8 = ((s8[8388608]{0:T(1024)(128)(4,1)}), s8[4194304]{0:T(1024)(128)(4,1)S(1)}, s32[]{:S(2)}) async-start(s8[8388608]{0:T(1024)(128)(4,1)} %bitcast.169), calls=%async_computation.13 | async-start | bytes 8388608
  340.9 21.1 %copy-start.2 = (f32[128,4608]{1,0:T(8,128)}, f32[128,4608]{1,0:T(8,128)S(1)}, u32[]{:S(2)}) copy-start(f32[128,4608]{1,0:T(8,128)S(1)} %convolution_add_fusion) | copy-start | bytes 7077892
  340.9 7.8 %slice-start.4 = ((s8[4718592]{0:T(1024)(128)(4,1)}), s8[524288]{0:T(1024)(128)(4,1)S(1)}, s32[]{:S(2)}) async-start(s8[4718592]{0:T(1024)(128)(4,1)} %bitcast.116), calls=%async_computation.9 | async-start | bytes 1048576
  340.9 9.1 %slice-start.9 = ((s8[8388608]{0:T(1024)(128)(4,1)}), s8[4194304]{0:T(1024)(128)(4,1)S(1)}, s32[]{:S(2)}) async-start(s8[8388608]{0:T(1024)(128)(4,1)} %bitcast.169), calls=%async_computation.14 | async-start | bytes 8388608
  350.0 5.9 copy-start.9
  355.9 3.7 copy-start.37
  355.9 3.7 copy-start.43
  359.5 12.9 %slice-start = ((s8[10616832]{0:T(1024)(128)(4,1)}), s8[4194304]{0:T(1024)(128)(4,1)S(1)}, s32[]{:S(2)}) async-start(s8[10616832]{0:T(1024)(128)(4,1)} %bitcast.109), calls=%async_computation.5 | async-start | bytes 8388608
  362.0 16.2 %copy-start.11 = (f32[128,1152]{1,0:T(8,128)}, f32[128,1152]{1,0:T(8,128)S(1)}, u32[]{:S(2)}) copy-start(f32[128,1152]{1,0:T(8,128)S(1)} %get-tuple-element.100) | copy-start | bytes 1769476
  362.0 10.5 %slice-start.1 = ((s8[10616832]{0:T(1024)(128)(4,1)}), s8[4194304]{0:T(1024)(128)(4,1)S(1)}, s32[]{:S(2)}) async-start(s8[10616832]{0:T(1024)(128)(4,1)} %bitcast.109), calls=%async_computation.6 | async-start | bytes 8388608
  362.0 10.5 %slice-start.2 = ((s8[10616832]{0:T(1024)(128)(4,1)}), s8[2228224]{0:T(1024)(128)(4,1)S(1)}, s32[]{:S(2)}) async-start(s8[10616832]{0:T(1024)(128)(4,1)} %bitcast.109), calls=%async_computation.7 | async-start | bytes 4456448
  379.2 5.9 copy-start.58
  391.1 2.7 copy-start.19
  391.1 2.7 copy-start.21
  393.8 3.5 copy-start.3
  393.8 3.5 copy-start.32
  397.4 5.8 copy-start.13
  397.4 5.8 copy-start.15
  397.4 13.7 %slice-start.5 = ((s8[10616832]{0:T(1024)(128)(4,1)}), s8[2228224]{0:T(1024)(128)(4,1)S(1)}, s32[]{:S(2)}) async-start(s8[10616832]{0:T(1024)(128)(4,1)} %bitcast.149), calls=%async_computation.10 | async-start | bytes 4456448
  397.4 13.7 %slice-start.6 = ((s8[10616832]{0:T(1024)(128)(4,1)}), s8[4194304]{0:T(1024)(128)(4,1)S(1)}, s32[]{:S(2)}) async-start(s8[10616832]{0:T(1024)(128)(4,1)} %bitcast.149), calls=%async_computation.11 | async-start | bytes 8388608
  403.2 5.6 copy-start.27
  403.2 5.6 copy-start.31
  403.2 8.0 %slice-start.7 = ((s8[10616832]{0:T(1024)(128)(4,1)}), s8[4194304]{0:T(1024)(128)(4,1)S(1)}, s32[]{:S(2)}) async-start(s8[10616832]{0:T(1024)(128)(4,1)} %bitcast.149), calls=%async_computation.12 | async-start | bytes 8388608
  413.8 5.7 copy-start.73
  413.8 5.8 copy-start.71
  421.9 2.7 copy-start.68
  421.9 2.8 copy-start.59
  421.9 3.7 copy-start.4
  425.6 9.0 %copy-start.10 = (f32[128,2048]{1,0:T(8,128)S(1)}, f32[128,2048]{1,0:T(8,128)}, u32[]{:S(2)}) copy-start(f32[128,2048]{1,0:T(8,128)} %copy-done.9) | copy-start | bytes 3145732
  425.6 9.0 %copy-start.38 = (bf16[128,2048]{1,0:T(8,128)(2,1)S(1)}, bf16[128,2048]{1,0:T(8,128)(2,1)}, u32[]{:S(2)}) copy-start(bf16[128,2048]{1,0:T(8,128)(2,1)} %copy-done.37) | copy-start | bytes 1572868
  673.4 4.0 copy-start.22
  673.4 7.9 %copy-start.34 = (f32[144,1152]{1,0:T(8,128)S(1)}, f32[144,1152]{1,0:T(8,128)}, u32[]{:S(2)}) copy-start(f32[144,1152]{1,0:T(8,128)} %get-tuple-element.43) | copy-start | bytes 1990660
  673.4 8.8 %copy-start.39 = (f32[64,2048]{1,0:T(8,128)S(1)}, f32[64,2048]{1,0:T(8,128)}, u32[]{:S(2)}) copy-start(f32[64,2048]{1,0:T(8,128)} %get-tuple-element.44) | copy-start | bytes 1572868
  673.4 26.5 %all-to-all-start.2 = ((f32[4,36,2816]{2,1,0:T(8,128)}), f32[4,36,2816]{2,1,0:T(8,128)S(1)}, u32[]{:S(2)}, u32[]{:S(2)}) async-start(f32[4,36,2816]{2,1,0:T(8,128)} %all_to_all.25), calls=%async_computation.2 | async-start | bytes 3604480 | tf_op jit(solution)/shard_map/all_to_all | solution.py:935
  701.1 4.7 copy-start.36
  705.8 5.3 copy-start.23
  708.5 10.0 %all-to-all-start.1 = ((f32[32,3,36]{2,1,0:T(4,128)}), f32[32,3,36]{2,1,0:T(4,128)S(1)}, u32[]{:S(2)}, u32[]{:S(2)}) async-start(f32[32,3,36]{2,1,0:T(4,128)} %copy.92), calls=%async_computation.1 | async-start | bytes 131072 | tf_op jit(solution)/shard_map/all_to_all | solution.py:894
  712.3 6.3 copy-start.53
  (36 other events, 61.8 us)
Sparse Core Ops, SparseCore 0:
  56.1 137.0 all-reduce.4
  424.1 57.1 all-gather.3

commit v2 on v0

--- a/solution.py
+++ b/solution.py
@@ -1,6 +1,10 @@
+import functools
+
 import jax
 import jax.numpy as jnp
 from jax import lax
+from jax.experimental import pallas as pl
+from jax.experimental.pallas import tpu as pltpu
 from jax.sharding import PartitionSpec as P
 
 D = 1152
@@ -9,6 +13,7 @@
 FF = 4608
 P_SIZE = 2048
 Z = 768
+Z_OUT = Z
 
 
 EPSILON = 1e-06
@@ -97,6 +102,721 @@
         gathered[7].reshape(P_SIZE, Z),
         gathered[8].astype(jnp.float32),
     )
+
+
+MESH = pl.DeviceIdType.MESH
+
+class Place:
+    def __init__(self, n):
+        self.me = me = lax.axis_index("fsdp")
+        self.Z = n // 8
+        self.z, self.y, self.x, self.c = me // 8, (me // 4) % 2, (me // 2) % 2, me % 2
+        self.xp = me + 2 - 4 * self.x
+        self.yp = me + 4 - 8 * self.y
+        self.cp = me + 1 - 2 * self.c
+
+def barrier(pc):
+    sem = pltpu.get_barrier_semaphore()
+    for q in (pc.xp, pc.yp, pc.cp):
+        pl.semaphore_signal(sem, inc=1, device_id=(q,), device_id_type=MESH)
+    @pl.when(pc.z > 0)
+    def _():
+        pl.semaphore_signal(sem, inc=1, device_id=(pc.me - 8,), device_id_type=MESH)
+    @pl.when(pc.z < pc.Z - 1)
+    def _():
+        pl.semaphore_signal(sem, inc=1, device_id=(pc.me + 8,), device_id_type=MESH)
+    ends = (pc.z == 0).astype(jnp.int32) + (pc.z == pc.Z - 1).astype(jnp.int32)
+    pl.semaphore_wait(sem, 5 - ends)
+
+def region(out, quart, zs, y, x, c, off, w):
+    if quart:
+        q = out.shape[3] // 4
+        col = pl.multiple_of((x * 2 + c) * q + off, 128)
+        return out.at[zs, y, :, pl.ds(col, w)]
+    return out.at[zs, y, x, c, :, pl.ds(off, w)]
+
+
+CHUNKS = (
+    tuple((0, 384 * i, 384, 1) for i in range(3))
+    + tuple((1, 384 * i, 384, 1) for i in range(3))
+    + tuple((2, 384 * i, 384, 1) for i in range(3))
+    + ((3, 0, 384, 1), (3, 384, 128, 1))
+    + ((4, 0, 768, 2), (4, 768, 768, 2), (4, 1536, 512, 2))
+    + ((5, 0, 768, 2),)
+)
+QUARTERED = (True, True, False, True, False, False)
+
+def dot(a, b):
+    return jnp.dot(a, b, preferred_element_type=jnp.float32)
+
+def dot_nt(a, b):
+    return lax.dot_general(a, b, (((1,), (1,)), ((), ())), preferred_element_type=jnp.float32)
+
+def norm_parts(values):
+    centred = values - jnp.mean(values, axis=-1, keepdims=True)
+    spread = jnp.mean(centred * centred, axis=-1, keepdims=True)
+    return centred, lax.rsqrt(spread + EPSILON)
+
+def token_rows(onehot, mod, k):
+    cols = slice(k * D, (k + 1) * D)
+    total = onehot[:, 0:1] * mod[0:1, cols]
+    for i in range(1, mod.shape[0]):
+        total = total + onehot[:, i:i + 1] * mod[i:i + 1, cols]
+    return total
+
+def head_window(h):
+    start = jnp.minimum((h * HD) // 128 * 128, D - 256)
+    start = pl.multiple_of(start, 128)
+    lane = lax.broadcasted_iota(jnp.int32, (1, 256), 1) + start
+    return start, (lane >= h * HD) & (lane < h * HD + HD)
+
+def gather_program(n, ins, outs, sems, rounds, quarts):
+    lsem, zs_sem, zr_sem, xs_sem, xr_sem, cs_sem, cr_sem = sems
+    pc = Place(n)
+    Z = pc.Z
+    z, y, x, c = pc.z, pc.y, pc.x, pc.c
+    def reg(r, zs, y_, x_, c_=None):
+        a, off, w = rounds[r][:3]
+        return region(outs[a], quarts[a], zs, y_, x_, c if c_ is None else c_, off, w)
+    def own_in(r):
+        a, off, w = rounds[r][:3]
+        return ins[a].at[:, pl.ds(off, w)]
+    def rcopy(src, dst, ss, rs, dev):
+        return pltpu.make_async_remote_copy(src_ref=src, dst_ref=dst, send_sem=ss, recv_sem=rs, device_id=(dev,), device_id_type=MESH)
+    def zcopy(r, side, s):
+        org = z - s if side == 0 else z + s
+        dst = reg(r, org, y, x)
+        return rcopy(own_in(r) if s == 0 else dst, dst, zs_sem.at[r, side, s], zr_sem.at[r, side, s], pc.me + (8 if side == 0 else -8))
+    def zrecv(r, side, s):
+        org = z - 1 - s if side == 0 else z + 1 + s
+        d = reg(r, org, y, x)
+        rcopy(d, d, zs_sem.at[r, side, s], zr_sem.at[r, side, s], pc.me).wait_recv()
+    def local(r):
+        return pltpu.make_async_copy(own_in(r), reg(r, z, y, x), lsem.at[r])
+    allz = slice(None); lo = slice(0, Z // 2); hi = slice(Z // 2, Z)
+    def xy(r, k):
+        if k < 2: d = reg(r, allz, y, x)
+        elif k == 2: d = reg(r, lo, y, 1 - x)
+        else: d = reg(r, hi, 1 - y, x)
+        return rcopy(d, d, xs_sem.at[r, k], xr_sem.at[r, k], pc.xp if k in (0, 3) else pc.yp)
+    def core(r, k):
+        d = reg(r, allz, y if k in (0, 1) else 1 - y, x if k in (0, 2) else 1 - x)
+        return rcopy(d, d, cs_sem.at[r, k], cr_sem.at[r, k], pc.cp)
+    def zstart(r, s):
+        @pl.when((z - s >= 0) & (z < Z - 1))
+        def _(): zcopy(r, 0, s).start()
+        @pl.when((z + s <= Z - 1) & (z > 0))
+        def _(): zcopy(r, 1, s).start()
+    def zwait(r, s):
+        @pl.when(z - 1 - s >= 0)
+        def _(): zrecv(r, 0, s)
+        @pl.when(z + 1 + s <= Z - 1)
+        def _(): zrecv(r, 1, s)
+    def stage(r, s):
+        if s == 0:
+            local(r).start()
+            zstart(r, 0)
+        elif s < Z - 1:
+            zwait(r, s - 1)
+            zstart(r, s)
+        elif s == Z - 1:
+            zwait(r, s - 1)
+            local(r).wait()
+            xy(r, 0).start(); xy(r, 1).start(); core(r, 0).start()
+        elif s == Z:
+            xy(r, 0).wait_recv(); xy(r, 2).start(); core(r, 1).start()
+            xy(r, 1).wait_recv(); xy(r, 3).start(); core(r, 2).start()
+        elif s == Z + 1:
+            xy(r, 2).wait_recv(); xy(r, 3).wait_recv(); core(r, 3).start()
+        elif s == Z + 2:
+            for k in range(4): core(r, k).wait_recv()
+    def finish(r):
+        for s in range(Z - 1):
+            @pl.when((z - s >= 0) & (z < Z - 1))
+            def _(): zcopy(r, 0, s).wait_send()
+            @pl.when((z + s <= Z - 1) & (z > 0))
+            def _(): zcopy(r, 1, s).wait_send()
+        for k in range(4):
+            xy(r, k).wait_send(); core(r, k).wait_send()
+    return stage, finish, Z + 3
+
+def weight_loads(chunk, full, slot, attn_slot, sem, parts=range(4)):
+    a, off, w, stacks = chunk
+    ref, cps = full[a], []
+    for j in parts:
+        if QUARTERED[a]:
+            dst = attn_slot if a == 0 and j == 3 else slot.at[j, :, :, :, pl.ds(0, w)]
+            cps.append((ref.at[:, :, :, pl.ds(j * (ref.shape[3] // 4) + off, w)], dst))
+        else:
+            rows, sw = ref.shape[4], w // stacks
+            for s in range(stacks):
+                cps.append((ref.at[:, :, j // 2, j % 2, :, pl.ds(off + s * sw, sw)],
+                            slot.at[j, :, :, pl.ds(s * rows, rows), pl.ds(0, sw)]))
+    return [pltpu.make_async_copy(s, d, sem.at[k]) for k, (s, d) in enumerate(cps)]
+
+def chunk_weight(chunk, slot, attn_slot, rows, part):
+    a, off, w, stacks = chunk
+    if QUARTERED[a]:
+        value = attn_slot[...] if a == 0 and part == 3 else slot[part, :, :, :, 0:w]
+        return value.reshape(-1, w)
+    sw = w // stacks
+    value = slot[:, :, :, part * rows:(part + 1) * rows, 0:sw]
+    Z = value.shape[1]
+    return jnp.concatenate([value[j, zz, yy] for zz in range(Z) for yy in range(2) for j in range(4)], axis=0)
+
+def scatter_program(n, R, G, CR, XR, ZR, keep, sems, final):
+    cs, cr, xs, xr, zs_, zr, credit = sems
+    keep_g, keep_c, keep_x = keep
+    pc = Place(n)
+    Z = pc.Z; H = Z // 2
+    z, y, x, c = pc.z, pc.y, pc.x, pc.c
+    up_dev = jnp.minimum(pc.me + 8, n - 1)
+    down_dev = jnp.maximum(pc.me - 8, 0)
+    def rcopy(src, dst, ss, rs, dev):
+        return pltpu.make_async_remote_copy(src_ref=src, dst_ref=dst, send_sem=ss, recv_sem=rs, device_id=(dev,), device_id_type=MESH)
+    def signal(k, dev):
+        pl.semaphore_signal(credit.at[k], inc=1, device_id=(dev,), device_id_type=MESH)
+    def core(r): return rcopy(G(r).at[1 - c], CR(r), cs.at[r], cr.at[r], pc.cp)
+    def xy(r, k):
+        b, xb = G(r).at[c], XR(r)
+        if k == 0: return rcopy(b.at[1 - x, 0:H, 1 - y], xb.at[0:H], xs.at[r, 0], xr.at[r, 0], pc.yp)
+        if k == 1: return rcopy(b.at[1 - x, H:Z, 1 - y], xb.at[H:Z], xs.at[r, 1], xr.at[r, 1], pc.xp)
+        if k == 2: return rcopy(b.at[1 - x, :, y], xb.at[Z:2 * Z], xs.at[r, 2], xr.at[r, 2], pc.xp)
+        return rcopy(b.at[x, :, 1 - y], xb.at[2 * Z:3 * Z], xs.at[r, 3], xr.at[r, 3], pc.yp)
+    def zc(r, side, d):
+        return rcopy(XR(r).at[Z + d], ZR(r).at[side, d], zs_.at[r, side, d], zr.at[r, side, d], up_dev if side == 0 else down_dev)
+    def waits_send(r):
+        core(r).wait_send()
+        for k in range(4): xy(r, k).wait_send()
+    def zwaits_send(r):
+        for d in range(Z):
+            @pl.when(d > z)
+            def _(): zc(r, 0, d).wait_send()
+            @pl.when(d < z)
+            def _(): zc(r, 1, d).wait_send()
+    def zstep(r, s):
+        for side in (0, 1):
+            p = s if side == 0 else Z - 1 - s
+            @pl.when(z == p)
+            def _():
+                if r >= keep_x and (p < Z - 1 if side == 0 else p > 0):
+                    pl.semaphore_wait(credit.at[3 + side], 1)
+                for d in range(Z):
+                    if (d > p) if side == 0 else (d < p):
+                        if s > 0:
+                            zc(r, side, d).wait_recv()
+                            XR(r)[Z + d] = XR(r)[Z + d] + ZR(r)[side, d]
+                        zc(r, side, d).start()
+    def before(r):
+        if r >= keep_g:
+            waits_send(r - keep_g)
+    def stage(r, s):
+        b = G(r).at[c]
+        if s == 0:
+            if r >= keep_c:
+                pl.semaphore_wait(credit.at[0], 1)
+            core(r).start()
+        elif s == 1:
+            core(r).wait_recv()
+            def add(i, carry):
+                xx, zz, yy = i // (2 * Z), (i // 2) % Z, i % 2
+                b[xx, zz, yy] = b[xx, zz, yy] + CR(r)[xx, zz, yy]
+                return carry
+            lax.fori_loop(0, 4 * Z, add, 0)
+            if r + keep_c < R:
+                signal(0, pc.cp)
+            if r >= keep_x:
+                pl.semaphore_wait(credit.at[1], 1)
+                pl.semaphore_wait(credit.at[2], 1)
+            xy(r, 0).start(); xy(r, 1).start()
+        elif s == 2:
+            xy(r, 0).wait_recv()
+            def add(i, carry):
+                b[1 - x, i, y] = b[1 - x, i, y] + XR(r)[i]
+                return carry
+            lax.fori_loop(0, H, add, 0)
+            xy(r, 2).start()
+            xy(r, 1).wait_recv()
+            def add(i, carry):
+                b[x, i, 1 - y] = b[x, i, 1 - y] + XR(r)[i]
+                return carry
+            lax.fori_loop(H, Z, add, 0)
+            xy(r, 3).start()
+        elif s == 3:
+            xy(r, 2).wait_recv(); xy(r, 3).wait_recv()
+            def add(i, carry):
+                XR(r)[Z + i] = b[x, i, y] + XR(r)[Z + i] + XR(r)[2 * Z + i]
+                return carry
+            lax.fori_loop(0, Z, add, 0)
+            zstep(r, 0)
+        elif s < Z + 2:
+            zstep(r, s - 3)
+        else:
+            for d in range(Z):
+                @pl.when(d == z)
+                def _():
+                    tot = XR(r)[Z + d].astype(jnp.float32)
+                    if d > 0:
+                        zc(r, 0, d).wait_recv()
+                        tot = tot + ZR(r)[0, d].astype(jnp.float32)
+                    if d < Z - 1:
+                        zc(r, 1, d).wait_recv()
+                        tot = tot + ZR(r)[1, d].astype(jnp.float32)
+                    final(r, tot)
+            zwaits_send(r)
+            if r + keep_x < R:
+                signal(1, pc.xp)
+                signal(2, pc.yp)
+                @pl.when(z < Z - 1)
+                def _(): signal(4, up_dev)
+                @pl.when(z > 0)
+                def _(): signal(3, down_dev)
+    def finish():
+        for r in range(max(0, R - keep_g), R):
+            waits_send(r)
+    return before, stage, finish, Z + 3
+
+def scatter_sems(R, Z):
+    D_ = pltpu.SemaphoreType.DMA
+    return [D_((R,)), D_((R,)), D_((R, 4)), D_((R, 4)), D_((R, 2, Z)), D_((R, 2, Z)), pltpu.SemaphoreType.REGULAR((5,))]
+
+def forward_kernel(n, offs, *refs):
+    rounds = CHUNKS
+    ins, refs = refs[:6], refs[6:]
+    tokens, onehot, same, mod_part, ada_b, qkv_b, tail_b, up_b, in_b, mid_b, out_b = refs[:11]
+    refs = refs[11:]
+    full, refs = refs[:6], refs[6:]
+    (first_in, projected, heads, branch_attn, middle, second_in, up_pre, up_act, branch_mlp, mixed,
+     first_pre, first_act, second_pre, second_act, features, mod) = refs[:16]
+    refs = refs[16:]
+    slots, attn_w, mod_own, mod_core, mod_xy, mod_line, load_sem = refs[:7]
+    stage, finish, S = gather_program(n, ins, full, refs[7:14], rounds, QUARTERED)
+    images = mod.shape[0]
+
+    def mod_final(r, tot):
+        for i in range(images):
+            for k in range(6 * D // 128):
+                row = i * (6 * D // 128) + k
+                mod[i:i + 1, 128 * k:128 * (k + 1)] = tot[row:row + 1] + ada_b[:, 128 * k:128 * (k + 1)]
+    _, mod_stage, mod_finish, _ = scatter_program(
+        n, 1, lambda r: mod_own, lambda r: mod_core, lambda r: mod_xy, lambda r: mod_line, (1, 1, 1), refs[14:], mod_final)
+    mod_own[...] = mod_part[...]
+    barrier(Place(n))
+    R, Z = len(rounds), n // 8
+    last_of = {a: max(r for r in range(R) if rounds[r][0] == a) for a in range(6)}
+
+    def loads(r):
+        a, off, w, _ = rounds[r]
+        return weight_loads(rounds[r], full, slots.at[r % 2], attn_w.at[off // 384] if a == 0 else None, load_sem.at[r % 2])
+
+    def prepare():
+        oh, md = onehot[...], mod
+        values = tokens[...].astype(jnp.float32)
+        centred, scale = norm_parts(values)
+        first_in[...] = (centred * scale * (1.0 + token_rows(oh, md, 1)) + token_rows(oh, md, 0)).astype(jnp.bfloat16)
+
+    def attention():
+        def head(h, carry):
+            start, inside = head_window(h)
+            q = projected[:, pl.ds(start, 256)]
+            k = projected[:, pl.ds(pl.multiple_of(start + D, 128), 256)]
+            v = projected[:, pl.ds(pl.multiple_of(start + 2 * D, 128), 256)]
+            q = jnp.where(inside, q, jnp.zeros_like(q))
+            scores = jnp.where(same[...] > 0.0, dot_nt(q, k) * HD ** (-0.5), -1e30)
+            e = jnp.exp(scores - jnp.max(scores, axis=-1, keepdims=True))
+            p = (e / jnp.sum(e, axis=-1, keepdims=True)).astype(jnp.bfloat16)
+            o = dot(p, v).astype(jnp.bfloat16)
+            heads[:, pl.ds(start, 256)] = jnp.where(inside, o, heads[:, pl.ds(start, 256)])
+            return carry
+        heads[...] = jnp.zeros_like(heads)
+        lax.fori_loop(0, HEADS, head, 0)
+        for i in range(3):
+            w = attn_w[i].reshape(D, 384)
+            branch_attn[:, 384 * i:384 * (i + 1)] = dot(heads[...], w) + tail_b[:, 384 * i:384 * (i + 1)]
+        oh, md = onehot[...], mod
+        mid = tokens[...].astype(jnp.float32) + token_rows(oh, md, 2) * branch_attn[...]
+        middle[...] = mid
+        centred, scale = norm_parts(mid)
+        second_in[...] = (centred * scale * (1.0 + token_rows(oh, md, 4)) + token_rows(oh, md, 3)).astype(jnp.bfloat16)
+
+    def compute(r):
+        a, off, w, stacks = rounds[r]
+        slot = slots.at[r % 2]
+        if a == 0:
+            for j in range(3):
+                cols = slice(j * D + off, j * D + off + w)
+                projected[:, cols] = (dot(first_in[...], chunk_weight(rounds[r], slot, None, 0, j)) + qkv_b[:, cols]).astype(jnp.bfloat16)
+            if r == last_of[0]:
+                attention()
+        elif a == 1:
+            for j in range(4):
+                cols = slice(j * (FF // 4) + off, j * (FF // 4) + off + w)
+                pre = dot(second_in[...], chunk_weight(rounds[r], slot, None, 0, j)) + up_b[:, cols]
+                up_pre[:, cols] = pre
+                up_act[:, cols] = gelu_tanh(pre).astype(jnp.bfloat16)
+        elif a == 2:
+            cols = slice(off, off + w)
+            branch_mlp[:, cols] = dot(up_act[...], chunk_weight(rounds[r], slot, None, FF // n, 0)) + tail_b[:, D + off:D + off + w]
+            if r == last_of[2]:
+                hidden = middle[...] + token_rows(onehot[...], mod, 5) * branch_mlp[...]
+                mixed[...] = hidden.astype(jnp.bfloat16)
+        elif a == 3:
+            for j in range(4):
+                cols = slice(j * (P_SIZE // 4) + off, j * (P_SIZE // 4) + off + w)
+                pre = dot(mixed[...], chunk_weight(rounds[r], slot, None, 0, j)) + in_b[:, cols]
+                first_pre[:, cols] = pre
+                first_act[:, cols] = sigmoid_linear(pre).astype(jnp.bfloat16)
+        elif a == 4:
+            sw = w // stacks
+            for s in range(stacks):
+                cols = slice(off + s * sw, off + (s + 1) * sw)
+                pre = dot(first_act[...], chunk_weight(rounds[r], slot, None, P_SIZE // n, s)) + mid_b[:, cols]
+                second_pre[:, cols] = pre
+                second_act[:, cols] = sigmoid_linear(pre).astype(jnp.bfloat16)
+        else:
+            sw = w // stacks
+            for s in range(stacks):
+                cols = slice(off + s * sw, off + (s + 1) * sw)
+                features[:, cols] = dot(second_act[...], chunk_weight(rounds[r], slot, None, P_SIZE // n, s)) + out_b[:, cols]
+
+    offs = offs + (offs[-1] + 1, offs[-1] + 2)
+    for t in range(R + offs[-1]):
+        for s in list(reversed(range(S))) + [S, S + 1]:
+            r = t - offs[s]
+            if not 0 <= r < R:
+                continue
+            if s < S:
+                stage(r, s)
+            elif s == S:
+                for cp in loads(r): cp.start()
+            else:
+                for cp in loads(r): cp.wait()
+                compute(r)
+        if t < Z + 3:
+            mod_stage(0, t)
+        if t == Z + 3:
+            prepare()
+    for r in range(R):
+        finish(r)
+    mod_finish()
+
+def forward(n, images, shards, small, offs, cid):
+    Z, R = n // 8, len(CHUNKS)
+    f32, bf = jnp.float32, jnp.bfloat16
+    tok = small[0].shape[0]
+    shapes = []
+    for sh, qt in zip(shards, QUARTERED):
+        k, w = sh.shape
+        shapes.append(jax.ShapeDtypeStruct((Z, 2, k, 4 * w) if qt else (Z, 2, 2, 2, k, w), sh.dtype))
+    acts = [(D, bf), (3 * D, bf), (D, bf), (D, f32), (D, f32), (D, bf), (FF, f32), (FF, bf), (D, f32), (D, bf),
+            (P_SIZE, f32), (P_SIZE, bf), (P_SIZE, f32), (P_SIZE, bf), (Z_OUT, f32)]
+    mod_dims = small[3].shape[-2:]
+    shapes += [jax.ShapeDtypeStruct((tok, w), dt) for w, dt in acts]
+    shapes.append(jax.ShapeDtypeStruct((images, 6 * D), f32))
+    D_ = pltpu.SemaphoreType.DMA
+    hbm, vmem = pl.BlockSpec(memory_space=pltpu.HBM), pl.BlockSpec(memory_space=pltpu.VMEM)
+    return pl.pallas_call(
+        functools.partial(forward_kernel, n, offs),
+        out_shape=shapes,
+        in_specs=[hbm] * 6 + [vmem] * len(small),
+        out_specs=[hbm] * 6 + [vmem] * (len(acts) + 1),
+        scratch_shapes=[
+            pltpu.VMEM((2, 4, Z, 2, 144, 384), bf),
+            pltpu.VMEM((3, Z, 2, 144, 384), bf),
+            pltpu.VMEM((2, 2, Z, 2) + mod_dims, f32),
+            pltpu.VMEM((2, Z, 2) + mod_dims, f32),
+            pltpu.VMEM((3 * Z,) + mod_dims, f32),
+            pltpu.VMEM((2, Z) + mod_dims, f32),
+            D_((2, 8)),
+            D_((R,)), D_((R, 2, Z - 1)), D_((R, 2, Z - 1)), D_((R, 4)), D_((R, 4)), D_((R, 4)), D_((R, 4)),
+        ] + scatter_sems(1, Z),
+        compiler_params=pltpu.CompilerParams(collective_id=cid, has_side_effects=True, vmem_limit_bytes=56 * 2**20),
+    )(*shards, *small)
+
+
+BACK_CHUNKS = (
+    ((5, 0, 768, 2),)
+    + ((4, 0, 768, 2), (4, 768, 768, 2), (4, 1536, 512, 2))
+    + ((3, 0, 384, 1), (3, 384, 128, 1))
+    + tuple((2, 384 * i, 384, 1) for i in range(3))
+    + tuple((1, 384 * i, 384, 1) for i in range(3))
+    + tuple((0, 384 * i, 384, 1) for i in range(3))
+)
+CHAIN = BACK_CHUNKS[:12] + tuple((6, 384 * i, 384, 1) for i in range(3)) + BACK_CHUNKS[12:]
+
+def dot_tn(a, b):
+    return lax.dot_general(a, b, (((0,), (0,)), ((), ())), preferred_element_type=jnp.float32)
+
+def norm_back(centred, scale, grad):
+    normed = centred * scale
+    inner = jnp.mean(grad * normed, axis=-1, keepdims=True)
+    return scale * (grad - jnp.mean(grad, axis=-1, keepdims=True) - normed * inner)
+
+def sigmoid_linear_slope(v):
+    s = jax.nn.sigmoid(v)
+    return s * (1.0 + v * (1.0 - s))
+
+def gelu_slope(v):
+    t = jnp.tanh(0.7978845608028654 * (v + 0.044715 * v * v * v))
+    return 0.5 * (1.0 + t) + 0.5 * v * (1.0 - t * t) * 0.7978845608028654 * (1.0 + 3.0 * 0.044715 * v * v)
+
+def backward_kernel(n, images, chain_per_tick, scatter_offs, mod_offs, *refs):
+    Z = n // 8
+    full, refs = refs[:6], refs[6:]
+    (tokens, onehot, same, mod, targets, out_grad, first_in, projected, heads, branch_attn, middle, second_in,
+     up_pre, up_act, branch_mlp, mixed, first_pre, first_act, second_pre, second_act, features) = refs[:21]
+    refs = refs[21:]
+    outs, refs = refs[:6], refs[6:]
+    tokens_grad, qkv_sums, attn_sums, mlp_sums, up_sums, in_sums, mid_sums, out_sums, mod_all = refs[:9]
+    refs = refs[9:]
+    (slots, load_sem, G_, CR_, XR_, ZR_, feature_grad, second_back, first_back, hidden_grad, mlp_grad, up_grad,
+     middle_grad, attn_grad, heads_grad, projected_grad, wide, narrow, mod_grad, mod_rows, mod_lines) = refs[:21]
+    refs = refs[21:]
+    rounds, R = BACK_CHUNKS, len(BACK_CHUNKS)
+    bf = jnp.bfloat16
+    pc = Place(n)
+
+    def dims(r):
+        a, off, w, stacks = rounds[r]
+        return ((FF // n if QUARTERED[a] or a == 2 else stacks * (P_SIZE // n)), w // stacks)
+    keep = (G_.shape[0], CR_.shape[0], XR_.shape[0])
+    def cut(ref, r):
+        rows, w = dims(r)
+        lead = (slice(None),) * (len(ref.shape) - 3)
+        return ref.at[(r % ref.shape[0],) + lead + (slice(0, rows), slice(0, w))]
+    def final(r, tot):
+        a, off, w, stacks = rounds[r]
+        rows, sw = dims(r)
+        rows = rows // stacks
+        for s in range(stacks):
+            outs[a][:, off + s * sw:off + (s + 1) * sw] = tot[s * rows:(s + 1) * rows]
+    before, stage, finish, S = scatter_program(
+        n, R, lambda r: cut(G_, r), lambda r: cut(CR_, r), lambda r: cut(XR_, r), lambda r: cut(ZR_, r), keep, refs[:7], final)
+    mod_stage, mod_finish, _ = gather_program(n, [mod_rows], [mod_all], refs[7:], ((0, 0, 128),), (False,))
+    barrier(pc)
+    mod_lines[...] = jnp.zeros_like(mod_lines)
+
+    def image_sums(k, value):
+        cols = slice(k * D, (k + 1) * D)
+        for i in range(images):
+            mod_grad[i:i + 1, cols] = jnp.sum(value * onehot[:, i:i + 1], axis=0, keepdims=True)
+
+    def sums(value):
+        return jnp.sum(value.astype(jnp.float32), axis=0, keepdims=True)
+
+    def start_chain():
+        f, t = features[...], targets[...].astype(jnp.float32)
+        f_norm = jnp.sqrt(jnp.sum(f * f, axis=1, keepdims=True) + EPSILON)
+        t_norm = jnp.sqrt(jnp.sum(t * t, axis=1, keepdims=True) + EPSILON)
+        inner = jnp.sum(f * t, axis=1, keepdims=True)
+        grad = -0.5 * (t / (f_norm * t_norm) - f * (inner / (f_norm * f_norm * f_norm * t_norm)))
+        feature_grad[...] = grad.astype(bf)
+        out_sums[...] = sums(feature_grad[...])
+
+    def attention_back():
+        projected_grad[...] = jnp.zeros_like(projected_grad)
+        def head(h, carry):
+            start, inside = head_window(h)
+            at_q, at_k, at_v = [pl.ds(pl.multiple_of(start + i * D, 128), 256) for i in range(3)]
+            q, k, v = projected[:, at_q], projected[:, at_k], projected[:, at_v]
+            q = jnp.where(inside, q, jnp.zeros_like(q))
+            g = heads_grad[:, at_q]
+            g = jnp.where(inside, g, jnp.zeros_like(g))
+            scores = jnp.where(same[...] > 0.0, dot_nt(q, k) * HD ** (-0.5), -1e30)
+            e = jnp.exp(scores - jnp.max(scores, axis=-1, keepdims=True))
+            p = e / jnp.sum(e, axis=-1, keepdims=True)
+            pg = dot_nt(g, v)
+            sg = (p * (pg - jnp.sum(p * pg, axis=-1, keepdims=True))).astype(bf)
+            for at, value in (
+                (at_q, dot(sg, k) * HD ** (-0.5)),
+                (at_k, dot_tn(sg, q) * HD ** (-0.5)),
+                (at_v, dot_tn(p.astype(bf), g)),
+            ):
+                projected_grad[:, at] = jnp.where(inside, value.astype(bf), projected_grad[:, at])
+            return carry
+        lax.fori_loop(0, HEADS, head, 0)
+        qkv_sums[...] = sums(projected_grad[...])
+
+    C = len(CHAIN)
+    last = {a: max(k for k in range(C) if CHAIN[k][0] == a) for a in range(7)}
+    first = {a: min(k for k in range(C) if CHAIN[k][0] == a) for a in range(7)}
+
+    def chain_loads(k):
+        a, off, w, stacks = CHAIN[k]
+        slot, sem = slots.at[k % 2], load_sem.at[k % 2]
+        if a == 6:
+            return weight_loads((0, off, w, stacks), full, slot, slot.at[3], sem, (3,))
+        return weight_loads((a, off, w, stacks), full, slot, slot.at[3], sem, range(3) if a == 0 else range(4))
+
+    def accumulate(acc, cols, new, k, a):
+        acc[:, cols] = new if k == first[a] else acc[:, cols] + new
+
+    def chain(k):
+        a, off, w, stacks = CHAIN[k]
+        slot = slots.at[k % 2]
+        sw = w // stacks
+        if a in (4, 5):
+            grad = second_back if a == 4 else feature_grad
+            new = None
+            for s in range(stacks):
+                part = dot_nt(grad[:, off + s * sw:off + (s + 1) * sw], chunk_weight(CHAIN[k], slot, None, P_SIZE // n, s))
+                new = part if new is None else new + part
+            accumulate(wide, slice(0, P_SIZE), new, k, a)
+            if k == last[a]:
+                target, pre = (second_back, second_pre) if a == 5 else (first_back, first_pre)
+                target[...] = (wide[:, 0:P_SIZE] * sigmoid_linear_slope(pre[...])).astype(bf)
+                (mid_sums if a == 5 else in_sums)[...] = sums(target[...])
+        elif a == 2:
+            for q in range(4):
+                weight = chunk_weight(CHAIN[k], slot, None, FF // n, 0)[q * D:(q + 1) * D]
+                accumulate(wide, slice(q * D, (q + 1) * D), dot_nt(mlp_grad[:, off:off + w], weight), k, a)
+            if k == last[a]:
+                for q in range(4):
+                    cols = slice(q * D, (q + 1) * D)
+                    up_grad[:, cols] = (wide[:, cols] * gelu_slope(up_pre[:, cols])).astype(bf)
+                up_sums[...] = sums(up_grad[...])
+        else:
+            src, parts, width = {3: (first_back, range(4), P_SIZE // 4), 1: (up_grad, range(4), FF // 4),
+                                 0: (projected_grad, range(3), D), 6: (attn_grad, range(3, 4), D)}[a]
+            new = None
+            for j in parts:
+                col = off if a == 6 else j * width + off
+                weight = slot[j, :, :, :, 0:w].reshape(-1, w)
+                part = dot_nt(src[:, col:col + w], weight)
+                new = part if new is None else new + part
+            accumulate(narrow, slice(0, D), new, k, a)
+            if k == last[a]:
+                oh = onehot[...]
+                if a == 3:
+                    hg = out_grad[...].astype(jnp.float32) + narrow[...]
+                    hidden_grad[...] = hg
+                    mlp_grad[...] = (hg * token_rows(oh, mod, 5)).astype(bf)
+                    mlp_sums[...] = sums(mlp_grad[...])
+                    image_sums(5, hg * branch_mlp[...])
+                elif a == 1:
+                    g = narrow[...]
+                    centred, scale = norm_parts(middle[...])
+                    image_sums(3, g)
+                    image_sums(4, g * (centred * scale))
+                    mg = hidden_grad[...] + norm_back(centred, scale, g * (1.0 + token_rows(oh, mod, 4)))
+                    middle_grad[...] = mg
+                    attn_grad[...] = (mg * token_rows(oh, mod, 2)).astype(bf)
+                    attn_sums[...] = sums(attn_grad[...])
+                    image_sums(2, mg * branch_attn[...])
+                elif a == 6:
+                    heads_grad[...] = narrow[...].astype(bf)
+                    attention_back()
+                else:
+                    g = narrow[...]
+                    centred, scale = norm_parts(tokens[...].astype(jnp.float32))
+                    image_sums(0, g)
+                    image_sums(1, g * (centred * scale))
+                    tg = middle_grad[...] + norm_back(centred, scale, g * (1.0 + token_rows(oh, mod, 1)))
+                    tokens_grad[...] = tg.astype(bf)
+                    stacked = mod_grad[...]
+                    rows = 6 * D // 128
+                    for i in range(images):
+                        for k in range(rows):
+                            mod_lines[i * rows + k:i * rows + k + 1] = stacked[i:i + 1, 128 * k:128 * (k + 1)]
+                    mod_rows[...] = mod_lines[...].astype(bf)
+
+    def produce(r):
+        a, off, w, stacks = rounds[r]
+        before(r)
+        left, right = {5: (second_act, feature_grad), 4: (first_act, second_back), 3: (mixed, first_back), 2: (up_act, mlp_grad),
+                       1: (second_in, up_grad), 0: (first_in, projected_grad)}[a]
+        rows, sw = dims(r)
+        g = cut(G_, r)
+        if QUARTERED[a]:
+            for j in range(4):
+                if a == 0 and j == 3:
+                    value = dot_tn(heads[...], attn_grad[:, off:off + w])
+                else:
+                    q = {3: P_SIZE // 4, 1: FF // 4, 0: D}[a]
+                    value = dot_tn(left[...], right[:, j * q + off:j * q + off + w])
+                g[j % 2, j // 2] = value.astype(bf).reshape(Z, 2, rows, w)
+        else:
+            rows = rows // stacks
+            per = 1152 if a == 2 else 1024
+            for s in range(stacks):
+                for part in range(left.shape[1] // per):
+                    value = dot_tn(left[:, part * per:(part + 1) * per], right[:, off + s * sw:off + (s + 1) * sw]).astype(bf)
+                    for i in range(per // rows):
+                        d = part * (per // rows) + i
+                        g[d % 2, (d // 2) % 2, d // 8, (d // 4) % 2, s * rows:(s + 1) * rows] = value[i * rows:(i + 1) * rows]
+
+    need = {5: 0, 4: first[4], 3: first[3], 2: first[2], 1: first[1], 0: first[0]}
+    done = 0
+    mod_start = None
+    for cp in chain_loads(0): cp.start()
+    start_chain()
+    t = 0
+    while True:
+        busy = False
+        for s in reversed(range(1, S)):
+            r = t - scatter_offs[s]
+            if 0 <= r < R:
+                stage(r, s); busy = True
+        if t < R:
+            busy = True
+            while done < need[rounds[t][0]]:
+                done = advance(done, chain_loads, chain, C)
+            produce(t)
+            stage(t, 0)
+        for _ in range(chain_per_tick):
+            if done < C:
+                done = advance(done, chain_loads, chain, C)
+        if done == C and mod_start is None:
+            mod_start = t
+        if mod_start is not None:
+            for s in reversed(range(Z + 3)):
+                if t - mod_start == mod_offs[s]:
+                    mod_stage(0, s)
+            busy = busy or t - mod_start < mod_offs[-1]
+        if not busy:
+            break
+        t += 1
+    finish()
+    mod_finish(0)
+
+def advance(k, chain_loads, chain, total):
+    if k + 1 < total:
+        for cp in chain_loads(k + 1): cp.start()
+    for cp in chain_loads(k): cp.wait()
+    chain(k)
+    return k + 1
+
+def backward(n, images, weights, acts, mod_height, plan, cid):
+    Z, R = n // 8, len(BACK_CHUNKS)
+    f32, bf = jnp.float32, jnp.bfloat16
+    tok = acts[0].shape[0]
+    chain_per_tick, scatter_offs, mod_offs, keep = plan
+    shapes = [jax.ShapeDtypeStruct((w.shape[2], w.shape[3] // 4) if qt else w.shape[4:], f32) for w, qt in zip(weights, QUARTERED)]
+    shapes.append(jax.ShapeDtypeStruct((tok, D), bf))
+    shapes += [jax.ShapeDtypeStruct((1, w), f32) for w in (3 * D, D, D, FF, P_SIZE, P_SIZE, Z_OUT)]
+    hbm, vmem = pl.BlockSpec(memory_space=pltpu.HBM), pl.BlockSpec(memory_space=pltpu.VMEM)
+    shapes.append(jax.ShapeDtypeStruct((Z, 2, 2, 2, mod_height, 128), bf))
+    D_ = pltpu.SemaphoreType.DMA
+    V = pltpu.VMEM
+    return pl.pallas_call(
+        functools.partial(backward_kernel, n, images, chain_per_tick, scatter_offs, mod_offs),
+        out_shape=shapes,
+        in_specs=[hbm] * 6 + [vmem] * len(acts),
+        out_specs=[vmem] * 14 + [hbm],
+        scratch_shapes=[
+            V((2, 4, Z, 2, 144, 384), bf),
+            D_((2, 8)),
+            V((keep[0], 2, 2, Z, 2, 144, 384), bf),
+            V((keep[1], 2, Z, 2, 144, 384), bf),
+            V((keep[2], 3 * Z, 144, 384), bf),
+            V((keep[2], 2, Z, 144, 384), bf),
+            V((tok, Z_OUT), bf), V((tok, P_SIZE), bf), V((tok, P_SIZE), bf), V((tok, D), f32), V((tok, D), bf), V((tok, FF), bf),
+            V((tok, D), f32), V((tok, D), bf), V((tok, D), bf), V((tok, 3 * D), bf), V((tok, FF), f32), V((tok, D), f32),
+            V((images, 6 * D), f32), V((mod_height, 128), bf), V((mod_height, 128), f32),
+        ] + scatter_sems(R, Z)
+        + [D_((1,)), D_((1, 2, Z - 1)), D_((1, 2, Z - 1)), D_((1, 4)), D_((1, 4)), D_((1, 4)), D_((1, 4))],
+        compiler_params=pltpu.CompilerParams(collective_id=cid, has_side_effects=True, vmem_limit_bytes=61 * 2**20),
+    )(*weights, *acts)
 
 
 def per_device(
@@ -376,6 +1096,175 @@
     )
 
 
+def per_device_kernels(
+    tokens,
+    cond,
+    image_lengths,
+    ada_weight,
+    ada_bias,
+    qkv_weight,
+    qv_bias,
+    attn_weight,
+    tail_bias,
+    up_weight,
+    up_bias,
+    down_weight,
+    projector_in,
+    projector_in_bias,
+    projector_mid,
+    projector_mid_bias,
+    projector_out,
+    projector_out_bias,
+    targets,
+    out_grad,
+):
+    owners = lax.axis_size("fsdp")
+    me = lax.axis_index("fsdp")
+    groups = [[4 * g + i for i in range(4)] for g in range(owners // 4)]
+    row_count = tokens.shape[0]
+    rows = D // owners
+    row_sharded = jnp.concatenate(
+        [
+            qkv_weight.reshape(rows, 3 * D),
+            attn_weight.reshape(rows, D),
+            up_weight.reshape(rows, FF),
+            projector_in.reshape(rows, P_SIZE),
+        ],
+        axis=1,
+    )
+    quarters = jnp.concatenate(
+        [part.reshape(rows, 4, -1) for part in jnp.split(row_sharded, (4 * D, 8 * D), axis=1)], axis=2
+    ).transpose(1, 0, 2)
+    quarters = lax.all_to_all(
+        quarters, "fsdp", 0, 0, axis_index_groups=groups, tiled=True
+    ).reshape(4 * rows, -1)
+    bias_row = jnp.concatenate(
+        [ada_bias, qv_bias, tail_bias, up_bias, projector_in_bias, projector_mid_bias, projector_out_bias]
+    )
+    bias_width = bias_row.shape[0]
+    images = cond.shape[0]
+    cond_values = cond.astype(jnp.float32)
+    cond_low = lowered(sigmoid_linear(cond_values))
+    cond_parts = cond_low.reshape(images, owners, rows).transpose(1, 0, 2).reshape(owners, -1)
+    received = lax.all_to_all(
+        jnp.concatenate([jnp.broadcast_to(bias_row, (owners, bias_width)), cond_parts], axis=1),
+        "fsdp", 0, 0, tiled=True,
+    )
+    bias_all = received[:, :bias_width].astype(jnp.float32)
+    cond_mine = received[:, bias_width:].reshape(owners * images, rows)
+    widths = (6 * D, 2 * D, 2 * D, FF, P_SIZE, P_SIZE, Z)
+    ends, at = [], 0
+    for width in widths:
+        at += width // owners
+        ends.append(at)
+    (
+        ada_bias_full, qv_full, tail_full, up_bias_full, proj_in_bias_full, proj_mid_bias_full, proj_out_bias_full
+    ) = [part.reshape(-1) for part in jnp.split(bias_all, ends[:-1], axis=1)]
+    ada_mine = ada_weight.reshape(rows, 6 * D)
+    lines = owners // 8
+    used = images * 6 * D // 128
+    mod_height = -(-used // 16) * 16
+    mod_part = matmul(cond_mine, ada_mine).reshape(lines, 2, 2, 2, used, 128)
+    mod_part = jnp.pad(
+        mod_part.transpose(3, 2, 0, 1, 4, 5), ((0, 0),) * 4 + ((0, mod_height - used), (0, 0))
+    )
+    image_of, onehot = image_onehot(image_lengths[0], row_count)
+    key_zero = jnp.zeros((D,), jnp.float32)
+    bias_full = jnp.concatenate([qv_full[:D], key_zero, qv_full[D:]])
+    same_image = (image_of[:, None] == image_of[None, :]).astype(jnp.float32)
+    onehot = jnp.pad(onehot, ((0, 0), (0, 128 - onehot.shape[1])))
+    results = forward(
+        owners,
+        images,
+        (
+            quarters[:, :D],
+            quarters[:, D : 2 * D],
+            down_weight.reshape(-1, D),
+            quarters[:, 2 * D :],
+            projector_mid.reshape(-1, P_SIZE),
+            projector_out.reshape(-1, Z),
+        ),
+        (
+            tokens,
+            onehot,
+            same_image,
+            mod_part,
+            ada_bias_full[None],
+            bias_full[None],
+            tail_full[None],
+            up_bias_full[None],
+            proj_in_bias_full[None],
+            proj_mid_bias_full[None],
+            proj_out_bias_full[None],
+        ),
+        (0, 1, 2, 3, 5, 7, 8),
+        1,
+    )
+    mixed = results[15]
+    modulation = results[21]
+    sums = backward(
+        owners,
+        images,
+        results[:6],
+        (tokens, onehot, same_image, modulation, targets, out_grad) + tuple(results[6:21]),
+        mod_height,
+        (2, (0, 1, 2, 3, 4, 5, 6), (0, 1, 2, 3, 4, 5, 6), (3, 2, 6)),
+        2,
+    )
+    first_sum, up_sum, down_sum, in_sum, mid_sum, out_sum, tokens_grad = sums[:7]
+    qkv_cols, attn_cols, mlp_cols, up_cols, in_cols, mid_cols, out_cols = [part[0] for part in sums[7:14]]
+    modulation_all = sums[14].reshape(owners, mod_height, 128)[:, :used].reshape(owners * images, 6 * D)
+    grad_ada = transposed_left(cond_mine, modulation_all)
+    cond_back = transposed_right(modulation_all, ada_mine).reshape(owners, images * rows)
+    bias_parts = [
+        by_owner(part, owners)
+        for part in (
+            jnp.concatenate([qkv_cols[:D], qkv_cols[2 * D :]]),
+            jnp.concatenate([attn_cols, mlp_cols]),
+            up_cols,
+            in_cols,
+            mid_cols,
+            out_cols,
+        )
+    ]
+    received = lax.all_to_all(jnp.concatenate([cond_back] + bias_parts, axis=1), "fsdp", 0, 0, tiled=True)
+    cond_back = received[:, : images * rows].reshape(owners, images, rows).transpose(1, 0, 2).reshape(images, D)
+    cond_grad = pull_back(sigmoid_linear, cond_values, cond_back).astype(jnp.bfloat16)
+    small = jnp.sum(received[:, images * rows :], axis=0)
+    grad_ada_bias = lax.dynamic_slice(
+        column_sums(modulation_all), (me * (6 * D // owners),), (6 * D // owners,)
+    )
+    back = jnp.concatenate([first_sum, up_sum, in_sum], axis=1)
+    back = lax.all_to_all(back, "fsdp", 0, 0, axis_index_groups=groups, tiled=True)
+    back = back.reshape(4, rows, -1).transpose(1, 0, 2)
+    first_rows = back[:, :, :D].reshape(rows, 4 * D)
+    small_parts, at = [], 0
+    for width in widths[1:]:
+        small_parts.append(small[at : at + width // owners])
+        at += width // owners
+    qv_small, tail_small, up_small, in_small, mid_small, out_small = small_parts
+    return (
+        mixed,
+        tokens_grad,
+        cond_grad,
+        grad_ada.reshape(-1),
+        grad_ada_bias,
+        first_rows[:, : 3 * D].reshape(-1),
+        qv_small,
+        first_rows[:, 3 * D :].reshape(-1),
+        tail_small,
+        back[:, :, D : 2 * D].reshape(-1),
+        up_small,
+        down_sum.reshape(-1),
+        back[:, :, 2 * D :].reshape(-1),
+        in_small,
+        mid_sum.reshape(-1),
+        mid_small,
+        out_sum.reshape(-1),
+        out_small,
+    )
+
+
 def solution(mesh):
     in_specs = (
         P("fsdp", None),
@@ -419,6 +1308,8 @@
         P("fsdp"),
         P("fsdp"),
     )
+    owners = mesh.shape["fsdp"]
+    program = per_device_kernels if owners % 16 == 0 and D % owners == 0 else per_device
     return jax.shard_map(
-        per_device, mesh=mesh, in_specs=in_specs, out_specs=out_specs, check_vma=False
-    )
+        program, mesh=mesh, in_specs=in_specs, out_specs=out_specs, check_vma=False
+    )

time: 2910 us -> 584 us (0.20)
  waiting for transfers between devices: 2150 us -> 15.8 us
  Pallas kernels: 0 us -> 476 us
  local copies, waits for them, and re-layouts: 317 us -> 49.6 us
  other arithmetic: 231 us -> 7.51 us
  matrix products: 150 us -> 3.86 us
  blocking collectives: 43.7 us -> 0 us
    unnamed x14 -> x0, waiting for transfers between devices: 1830 us -> none
    pallas_call x0 -> x2, Pallas kernels: none -> 476 us  [the longest x1 243 us: backward(): pl.pallas_call(functools.partial(backward_kernel, n, images, chain_per_ti...]
    all_gather x8 -> x0, waiting for transfers between devices: 316 us -> none  [the longest x1 105 us: per_device(): lax.all_gather(qkv_weight, 'fsdp', axis=0, tiled=True)]
    reshape x26 -> x24, local copies, waits for them, and re-layouts: 270 us -> 19.8 us  [the longest x1 2.27 us: per_device_kernels(): grad_ada.reshape(-1)]
    all_gather x2 -> x0, other arithmetic: 214 us -> none  [the longest x1 167 us: per_device(): lax.all_gather(qkv_weight, 'fsdp', axis=0, tiled=True)]
    dot_general x8 -> x1, matrix products: 58 us -> 1.38 us  [transposed_left(): lax.dot_general(left, right, (((0,), (0,)), ((), ())), preferred_element_...]
    unnamed x1 -> x0, blocking collectives: 43.7 us -> none
    dot_general x8 -> x1, matrix products: 44 us -> 0.47 us  [transposed_right(): lax.dot_general(left, right, (((1,), (1,)), ((), ())), preferred_element_...]
  transfers between devices with their start and end apart: 11 -> 4, of which waited for: 8 -> 3; matrix products, arithmetic and copies ran while one was open for 17% -> 6% of each run, Pallas kernels for 0% -> 0%
where the time goes in v2:
time: 584 us; the launch traced here: 576 us
  Pallas kernels  476 us (82%)
  local copies, waits for them, and re-layouts  49.6 us (8%)
  starting transfers between devices  21.7 us (4%)
  waiting for transfers between devices  15.8 us (3%)
  other arithmetic  7.51 us (1%)
    pallas_call x1, Pallas kernels, backward(): pl.pallas_call(functools.partial(backward_kernel, n, images, chain_per_ti...  243 us
    pallas_call x1, Pallas kernels, forward(): pl.pallas_call(functools.partial(forward_kernel, n, offs), out_shape=shap...  233 us
  transfers between devices with their start and end apart: 4, of which 3 were waited for; matrix products, arithmetic and copies ran while one was open for 6% of the time, Pallas kernels for 0%

profile of v2, /device:TPU:0, one launch (start us, length us, event | category | flops | bytes accessed | tf_op | source)
XLA Modules:
  0.0 575.9 jit_solution(17782547831407675631)
XLA Ops:
  0.7 0.8 fusion.3
  1.7 4.8 concatenate.39
  6.5 0.5 broadcast.32
  7.0 0.7 reduce.16
  7.7 0.7 reshape.214
  8.4 7.3 %all-to-all-start.1 = ((bf16[32,2,382]{2,1,0:T(2,128)(2,1)}), bf16[32,2,382]{2,1,0:T(2,128)(2,1)S(1)}, u32[]{:S(2)}, u32[]{:S(2)}) async-start(bf16[32,2,382]{2,1,0:T(2,128)(2,1)} %reshape.214), calls=%async_computation.1 | async-start | bytes 98304 | tf_op jit(solution)/shard_map/all_to_all | solution.py:1149
  15.8 0.8 reduce-window.8
  16.8 1.2 reshape.163
  18.0 1.0 reshape.164
  19.4 0.4 maximum_bitcast_fusion
  19.8 0.7 compare_convert_fusion
  20.5 0.5 reshape.175
  21.1 1.0 copy.72
  22.1 1.1 reshape.167.refs_2_
  23.2 0.8 reshape.168.refs_4_
  24.0 0.7 reshape.169.refs_5_
  24.8 4.2 all-to-all-start
  29.7 0.6 broadcast_in_dim.8.refs_11_
  30.4 0.7 broadcast_in_dim_reshape.21.refs_14_
  31.1 0.7 broadcast_in_dim_reshape.22.refs_15_
  31.8 0.7 broadcast_in_dim_reshape.18.refs_10_
  32.5 0.7 broadcast_in_dim_reshape.20.refs_13_
  33.2 0.7 broadcast_in_dim_reshape.19.refs_12_
  33.9 0.7 broadcast_in_dim_reshape.23.refs_16_
  34.7 2.0 fusion.13
  36.7 2.0 reshape.176
  39.0 1.9 pad.12.refs_9_
  40.9 1.1 all-to-all-done
  41.9 1.3 reshape.166
  43.3 0.9 fusion.8
  44.2 0.7 slice.106.refs_3_
  44.8 232.8 %shard_map.331 = (bf16[4,2,144,4608]{3,2,1,0:T(8,128)(2,1)}, bf16[4,2,144,4608]{3,2,1,0:T(8,128)(2,1)}, bf16[4,2,2,2,144,1152]{5,4,3,2,1,0:T(8,128)(2,1)}, bf16[...) custom-call(bf16[144,1152]{1,0:T(8,128)(2,1)} %get-tuple-element.97., ...), custom_call_target="tpu_custom_call" | custom-call | tf_op jit(solution)/shard_map/pallas_call | solution.py:518
  277.7 242.9 %shard_map.332 = (f32[144,1152]{1,0:T(8,128)}, f32[144,1152]{1,0:T(8,128)}, f32[144,1152]{1,0:T(8,128)}, f32[144,512]{1,0:T(8,128)}, f32[64,2048]{1,0:T(8,128)},...) custom-call(bf16[4,2,144,4608]{3,2,1,0:T(8,128)(2,1)} %get-tuple-ele, ...), custom_call_target="tpu_custom_call" | custom-call | tf_op jit(solution)/shard_map/pallas_call | solution.py:801
  520.6 1.4 slice.111
  522.0 1.5 reshape.178
  524.1 0.5 fusion.14
  524.8 0.5 broadcast.30
  525.3 0.7 reduce.14
  526.0 0.7 reduce.15
  527.0 0.7 all_to_all.29
  527.7 6.6 %all-to-all-start.2 = ((f32[32,1,548]{2,1,0:T(1,128)}), f32[32,1,548]{2,1,0:T(1,128)S(1)}, u32[]{:S(2)}, u32[]{:S(2)}) async-start(f32[32,1,548]{2,1,0:T(1,128)} %all_to_all.29), calls=%async_computation.2 | async-start | bytes 163840 | tf_op jit(solution)/shard_map/all_to_all | solution.py:1230
  534.4 1.5 pad_maximum_fusion
  535.9 1.4 all_to_all.32
  537.3 4.7 all-to-all-done.2
  542.0 3.6 all-to-all-start.3
  545.6 1.4 fusion.15
  546.9 2.3 reshape.182
  549.2 2.0 reshape.187
  551.2 1.9 copy.86
  553.2 0.7 reshape.190
  554.1 0.6 dynamic_slice.3
  554.8 0.6 slice.99
  555.5 0.6 slice.103
  556.3 0.6 fusion.12
  556.9 0.6 fusion.11
  557.5 0.6 fusion.6
  558.1 10.0 %all-to-all-done.3 = f32[4,36,2816]{2,1,0:T(8,128)S(1)} async-done(((f32[4,36,2816]{2,1,0:T(8,128)}), f32[4,36,2816]{2,1,0:T(8,128)S(1)}, u32[]{:S(2)}, u32[]{:S(2)}) %all-to-all-start.3) | async-done | bytes 1622048 | tf_op jit(solution)/shard_map/all_to_all | solution.py:1238
  568.6 0.7 slice.116
  569.3 0.8 reshape.184
  570.1 1.6 reshape.185
  571.9 1.1 reshape.186
  573.2 0.8 copy.85
  574.0 0.7 copy.100
  574.7 0.7 copy.101
  (94 shorter events, 4.3 us)
Async XLA Ops:
  0.7 18.5 %copy-start.2 = (bf16[165888]{0:T(1024)(128)(2,1)S(1)}, bf16[165888]{0:T(1024)(128)(2,1)}, u32[]{:S(2)}) copy-start(bf16[165888]{0:T(1024)(128)(2,1)} %param.29) | copy-start | bytes 995332
  1.6 17.7 %copy-start.7 = (bf16[73728]{0:T(1024)(128)(2,1)S(1)}, bf16[73728]{0:T(1024)(128)(2,1)}, u32[]{:S(2)}) copy-start(bf16[73728]{0:T(1024)(128)(2,1)} %param.32) | copy-start | bytes 442372
  8.4 16.3 %all-to-all-start.1 = ((bf16[32,2,382]{2,1,0:T(2,128)(2,1)}), bf16[32,2,382]{2,1,0:T(2,128)(2,1)S(1)}, u32[]{:S(2)}, u32[]{:S(2)}) async-start(bf16[32,2,382]{2,1,0:T(2,128)(2,1)} %reshape.214), calls=%async_computation.1 | async-start | bytes 98304 | tf_op jit(solution)/shard_map/all_to_all | solution.py:1149
  19.1 1.4 copy-start.1
  19.8 2.3 copy-start.3
  20.5 2.7 copy-start.5
  21.0 3.0 copy-start.8
  24.8 17.2 %all-to-all-start = ((bf16[4,36,2816]{2,1,0:T(8,128)(2,1)}), bf16[4,36,2816]{2,1,0:T(8,128)(2,1)}, u32[]{:S(2)}, u32[]{:S(2)}) async-start(bf16[4,36,2816]{2,1,0:T(8,128)(2,1)} %copy.72), calls=%async_computation | async-start | bytes 1802240 | tf_op jit(solution)/shard_map/all_to_all | solution.py:1138
  522.0 1.6 copy-start.15
  522.0 1.7 copy-start.14
  522.0 1.8 copy-start.13
  523.6 1.1 copy-start.10
  523.6 1.7 copy-start.12
  523.6 2.4 copy-start.11
  523.6 3.2 copy-start.16
  527.7 14.3 %all-to-all-start.2 = ((f32[32,1,548]{2,1,0:T(1,128)}), f32[32,1,548]{2,1,0:T(1,128)S(1)}, u32[]{:S(2)}, u32[]{:S(2)}) async-start(f32[32,1,548]{2,1,0:T(1,128)} %all_to_all.29), calls=%async_computation.2 | async-start | bytes 163840 | tf_op jit(solution)/shard_map/all_to_all | solution.py:1230
  542.0 26.1 %all-to-all-start.3 = ((f32[4,36,2816]{2,1,0:T(8,128)}), f32[4,36,2816]{2,1,0:T(8,128)S(1)}, u32[]{:S(2)}, u32[]{:S(2)}) async-start(f32[4,36,2816]{2,1,0:T(8,128)} %all_to_all.32), calls=%async_computation.3 | async-start | bytes 3604480 | tf_op jit(solution)/shard_map/all_to_all | solution.py:1238
  549.2 4.0 copy-start.6
  551.2 6.2 %copy-start.9 = (bf16[3,1152]{1,0:T(4,128)(2,1)S(1)}, bf16[3,1152]{1,0:T(4,128)(2,1)}, u32[]{:S(2)}) copy-start(bf16[3,1152]{1,0:T(4,128)(2,1)} %param.21) | copy-start | bytes 20740
  571.9 2.1 copy-start
  571.9 2.8 copy-start.4

commit v3 on v2

--- a/solution.py
+++ b/solution.py
@@ -115,8 +115,15 @@
         self.yp = me + 4 - 8 * self.y
         self.cp = me + 1 - 2 * self.c
 
-def barrier(pc):
+def barrier(pc, everyone=0):
     sem = pltpu.get_barrier_semaphore()
+    if everyone:
+        def greet(k, carry):
+            pl.semaphore_signal(sem, inc=1, device_id=(lax.rem(pc.me + k, everyone),), device_id_type=MESH)
+            return carry
+        lax.fori_loop(1, everyone, greet, 0)
+        pl.semaphore_wait(sem, everyone - 1)
+        return
     for q in (pc.xp, pc.yp, pc.cp):
         pl.semaphore_signal(sem, inc=1, device_id=(q,), device_id_type=MESH)
     @pl.when(pc.z > 0)
@@ -128,23 +135,18 @@
     ends = (pc.z == 0).astype(jnp.int32) + (pc.z == pc.Z - 1).astype(jnp.int32)
     pl.semaphore_wait(sem, 5 - ends)
 
-def region(out, quart, zs, y, x, c, off, w):
-    if quart:
-        q = out.shape[3] // 4
-        col = pl.multiple_of((x * 2 + c) * q + off, 128)
-        return out.at[zs, y, :, pl.ds(col, w)]
-    return out.at[zs, y, x, c, :, pl.ds(off, w)]
-
-
-CHUNKS = (
-    tuple((0, 384 * i, 384, 1) for i in range(3))
-    + tuple((1, 384 * i, 384, 1) for i in range(3))
-    + tuple((2, 384 * i, 384, 1) for i in range(3))
-    + ((3, 0, 384, 1), (3, 384, 128, 1))
-    + ((4, 0, 768, 2), (4, 768, 768, 2), (4, 1536, 512, 2))
-    + ((5, 0, 768, 2),)
-)
-QUARTERED = (True, True, False, True, False, False)
+
+SLABBED = (True, True, False, True, False, False)
+
+def gather_rounds():
+    out = []
+    for a in range(3):
+        out += [(a, 0, 384, 1, 0), (a, 384, 256, 1, 1), (a, 640, 384, 1, 0), (a, 1024, 128, 1, 0)]
+    out += [(3, 0, 384, 1, 0), (3, 384, 128, 1, 1)]
+    out += [(4, 0, 768, 2, 0), (4, 768, 512, 2, 1), (4, 1280, 768, 2, 0)]
+    out += [(5, 0, 256, 2, 1), (5, 256, 512, 2, 0)]
+    return tuple(out)
+CHUNKS = gather_rounds()
 
 def dot(a, b):
     return jnp.dot(a, b, preferred_element_type=jnp.float32)
@@ -158,10 +160,10 @@
     return centred, lax.rsqrt(spread + EPSILON)
 
 def token_rows(onehot, mod, k):
-    cols = slice(k * D, (k + 1) * D)
-    total = onehot[:, 0:1] * mod[0:1, cols]
-    for i in range(1, mod.shape[0]):
-        total = total + onehot[:, i:i + 1] * mod[i:i + 1, cols]
+    images = mod.shape[0] // 6
+    total = onehot[:, 0:1] * mod[k * images:k * images + 1]
+    for i in range(1, images):
+        total = total + onehot[:, i:i + 1] * mod[k * images + i:k * images + i + 1]
     return total
 
 def head_window(h):
@@ -170,37 +172,50 @@
     lane = lax.broadcasted_iota(jnp.int32, (1, 256), 1) + start
     return start, (lane >= h * HD) & (lane < h * HD + HD)
 
-def gather_program(n, ins, outs, sems, rounds, quarts):
+def region(out, zs, y, x, c, off, w):
+    return out.at[zs, y, x, c, :, pl.ds(off, w)]
+
+def gather_program(n, ins, outs, sems, rounds):
     lsem, zs_sem, zr_sem, xs_sem, xr_sem, cs_sem, cr_sem = sems
     pc = Place(n)
     Z = pc.Z
     z, y, x, c = pc.z, pc.y, pc.x, pc.c
-    def reg(r, zs, y_, x_, c_=None):
+    allz = slice(None); lo = slice(0, Z // 2); hi = slice(Z // 2, Z)
+    def plane(r): return rounds[r][4]
+    def reg(r, zs, y_, x_):
         a, off, w = rounds[r][:3]
-        return region(outs[a], quarts[a], zs, y_, x_, c if c_ is None else c_, off, w)
+        return region(outs[a], zs, y_, x_, c, off, w)
     def own_in(r):
         a, off, w = rounds[r][:3]
         return ins[a].at[:, pl.ds(off, w)]
     def rcopy(src, dst, ss, rs, dev):
         return pltpu.make_async_remote_copy(src_ref=src, dst_ref=dst, send_sem=ss, recv_sem=rs, device_id=(dev,), device_id_type=MESH)
+    def line_part(r, org):
+        return reg(r, org, slice(None), slice(None)) if plane(r) else reg(r, org, y, x)
     def zcopy(r, side, s):
         org = z - s if side == 0 else z + s
-        dst = reg(r, org, y, x)
-        return rcopy(own_in(r) if s == 0 else dst, dst, zs_sem.at[r, side, s], zr_sem.at[r, side, s], pc.me + (8 if side == 0 else -8))
+        dst = line_part(r, org)
+        src = own_in(r) if s == 0 and not plane(r) else dst
+        return rcopy(src, dst, zs_sem.at[r, side, s], zr_sem.at[r, side, s], pc.me + (8 if side == 0 else -8))
     def zrecv(r, side, s):
         org = z - 1 - s if side == 0 else z + 1 + s
-        d = reg(r, org, y, x)
+        d = line_part(r, org)
         rcopy(d, d, zs_sem.at[r, side, s], zr_sem.at[r, side, s], pc.me).wait_recv()
     def local(r):
         return pltpu.make_async_copy(own_in(r), reg(r, z, y, x), lsem.at[r])
-    allz = slice(None); lo = slice(0, Z // 2); hi = slice(Z // 2, Z)
     def xy(r, k):
+        if plane(r):
+            if k < 2:
+                return rcopy(own_in(r), reg(r, z, y, x), xs_sem.at[r, k], xr_sem.at[r, k], pc.yp if k else pc.xp)
+            d = reg(r, z, y, 1 - x) if r % 2 else reg(r, z, 1 - y, x)
+            return rcopy(d, d, xs_sem.at[r, 2], xr_sem.at[r, 2], pc.yp if r % 2 else pc.xp)
         if k < 2: d = reg(r, allz, y, x)
         elif k == 2: d = reg(r, lo, y, 1 - x)
         else: d = reg(r, hi, 1 - y, x)
         return rcopy(d, d, xs_sem.at[r, k], xr_sem.at[r, k], pc.xp if k in (0, 3) else pc.yp)
     def core(r, k):
-        d = reg(r, allz, y if k in (0, 1) else 1 - y, x if k in (0, 2) else 1 - x)
+        if plane(r): d = reg(r, allz, slice(None), slice(None))
+        else: d = reg(r, allz, y if k in (0, 1) else 1 - y, x if k in (0, 2) else 1 - x)
         return rcopy(d, d, cs_sem.at[r, k], cr_sem.at[r, k], pc.cp)
     def zstart(r, s):
         @pl.when((z - s >= 0) & (z < Z - 1))
@@ -213,6 +228,26 @@
         @pl.when(z + 1 + s <= Z - 1)
         def _(): zrecv(r, 1, s)
     def stage(r, s):
+        if plane(r):
+            if s == 0:
+                local(r).start()
+                xy(r, 0).start(); xy(r, 1).start()
+            elif s == 1:
+                local(r).wait()
+                xy(r, 0).wait_recv(); xy(r, 1).wait_recv()
+                xy(r, 2).start()
+            elif s == 2:
+                xy(r, 2).wait_recv()
+                zstart(r, 0)
+            elif s < Z + 1:
+                zwait(r, s - 3)
+                zstart(r, s - 2)
+            elif s == Z + 1:
+                zwait(r, Z - 2)
+                core(r, 0).start()
+            else:
+                core(r, 0).wait_recv()
+            return
         if s == 0:
             local(r).start()
             zstart(r, 0)
@@ -236,33 +271,28 @@
             def _(): zcopy(r, 0, s).wait_send()
             @pl.when((z + s <= Z - 1) & (z > 0))
             def _(): zcopy(r, 1, s).wait_send()
-        for k in range(4):
-            xy(r, k).wait_send(); core(r, k).wait_send()
+        for k in range(3 if plane(r) else 4):
+            xy(r, k).wait_send()
+        for k in range(1 if plane(r) else 4):
+            core(r, k).wait_send()
     return stage, finish, Z + 3
 
-def weight_loads(chunk, full, slot, attn_slot, sem, parts=range(4)):
-    a, off, w, stacks = chunk
+def weight_loads(chunk, full, slot, sem, top=0, bottom=None):
+    a, off, w, stacks = chunk[:4]
     ref, cps = full[a], []
-    for j in parts:
-        if QUARTERED[a]:
-            dst = attn_slot if a == 0 and j == 3 else slot.at[j, :, :, :, pl.ds(0, w)]
-            cps.append((ref.at[:, :, :, pl.ds(j * (ref.shape[3] // 4) + off, w)], dst))
-        else:
-            rows, sw = ref.shape[4], w // stacks
-            for s in range(stacks):
-                cps.append((ref.at[:, :, j // 2, j % 2, :, pl.ds(off + s * sw, sw)],
-                            slot.at[j, :, :, pl.ds(s * rows, rows), pl.ds(0, sw)]))
+    rows, sw = ref.shape[4], w // stacks
+    bottom = bottom or rows
+    for j in range(4):
+        for s in range(stacks):
+            cps.append((ref.at[:, :, j // 2, j % 2, pl.ds(top, bottom - top), pl.ds(off + s * sw, sw)],
+                        slot.at[j, :, :, pl.ds(s * rows + top, bottom - top), pl.ds(0, sw)]))
     return [pltpu.make_async_copy(s, d, sem.at[k]) for k, (s, d) in enumerate(cps)]
 
-def chunk_weight(chunk, slot, attn_slot, rows, part):
-    a, off, w, stacks = chunk
-    if QUARTERED[a]:
-        value = attn_slot[...] if a == 0 and part == 3 else slot[part, :, :, :, 0:w]
-        return value.reshape(-1, w)
-    sw = w // stacks
-    value = slot[:, :, :, part * rows:(part + 1) * rows, 0:sw]
-    Z = value.shape[1]
-    return jnp.concatenate([value[j, zz, yy] for zz in range(Z) for yy in range(2) for j in range(4)], axis=0)
+def chunk_weight(chunk, slot, rows, part):
+    sw = chunk[2] // chunk[3]
+    Z = slot.shape[1]
+    return jnp.concatenate(
+        [slot[j, zz, yy, part * rows:(part + 1) * rows, 0:sw] for zz in range(Z) for yy in range(2) for j in range(4)], axis=0)
 
 def scatter_program(n, R, G, CR, XR, ZR, keep, sems, final):
     cs, cr, xs, xr, zs_, zr, credit = sems
@@ -380,34 +410,75 @@
     D_ = pltpu.SemaphoreType.DMA
     return [D_((R,)), D_((R,)), D_((R, 4)), D_((R, 4)), D_((R, 2, Z)), D_((R, 2, Z)), pltpu.SemaphoreType.REGULAR((5,))]
 
-def forward_kernel(n, offs, *refs):
+BIASES = (6 * D, 2 * D, 2 * D, FF, P_SIZE, P_SIZE, Z_OUT)
+
+def forward_kernel(n, images, offs, *refs):
     rounds = CHUNKS
-    ins, refs = refs[:6], refs[6:]
-    tokens, onehot, same, mod_part, ada_b, qkv_b, tail_b, up_b, in_b, mid_b, out_b = refs[:11]
-    refs = refs[11:]
+    qkv_w, attn_in, up_w, in_w, down_w, mid_w, out_w, ada_w, mail, tokens, onehot, same = refs[:12]
+    refs = refs[12:]
     full, refs = refs[:6], refs[6:]
     (first_in, projected, heads, branch_attn, middle, second_in, up_pre, up_act, branch_mlp, mixed,
-     first_pre, first_act, second_pre, second_act, features, mod) = refs[:16]
-    refs = refs[16:]
-    slots, attn_w, mod_own, mod_core, mod_xy, mod_line, load_sem = refs[:7]
-    stage, finish, S = gather_program(n, ins, full, refs[7:14], rounds, QUARTERED)
-    images = mod.shape[0]
+     first_pre, first_act, second_pre, second_act, features, mod, cond_mine) = refs[:17]
+    refs = refs[17:]
+    slots, attn_w, first_own, up_own, in_own, box, mod_own, mod_core, mod_xy, mod_line = refs[:10]
+    bias_rows, refs = refs[10:17], refs[17:]
+    load_sem, mail_send, mail_recv = refs[:3]
+    ada_b, qv_b, tail_b, up_b, in_b, mid_b, out_b = bias_rows
+    R, Z = len(rounds), n // 8
+    pc = Place(n)
+    stage, finish, S = gather_program(
+        n, (first_own, up_own, down_w, in_own, mid_w, out_w), full, refs[3:10], rounds)
+    per = D // n
+    for s in range(4):
+        first_own[s * per:(s + 1) * per] = qkv_w[:, s * D:(s + 1) * D] if s < 3 else attn_in[...]
+        up_own[s * per:(s + 1) * per] = up_w[:, s * (FF // 4):(s + 1) * (FF // 4)]
+        in_own[s * per:(s + 1) * per] = in_w[:, s * (P_SIZE // 4):(s + 1) * (P_SIZE // 4)]
 
     def mod_final(r, tot):
-        for i in range(images):
-            for k in range(6 * D // 128):
-                row = i * (6 * D // 128) + k
-                mod[i:i + 1, 128 * k:128 * (k + 1)] = tot[row:row + 1] + ada_b[:, 128 * k:128 * (k + 1)]
+        for k in range(6):
+            for i in range(images):
+                row = k * images + i
+                mod[row:row + 1] = tot[row:row + 1] + ada_b[:, k * D:(k + 1) * D]
     _, mod_stage, mod_finish, _ = scatter_program(
-        n, 1, lambda r: mod_own, lambda r: mod_core, lambda r: mod_xy, lambda r: mod_line, (1, 1, 1), refs[14:], mod_final)
-    mod_own[...] = mod_part[...]
-    barrier(Place(n))
-    R, Z = len(rounds), n // 8
+        n, 1, lambda r: mod_own, lambda r: mod_core, lambda r: mod_xy, lambda r: mod_line, (1, 1, 1), refs[10:], mod_final)
+
+    def letter(k):
+        dest = lax.rem(pc.me + k, n)
+        return pltpu.make_async_remote_copy(
+            src_ref=mail.at[dest], dst_ref=box.at[pc.me], send_sem=mail_send.at[k], recv_sem=mail_recv.at[k],
+            device_id=(dest,), device_id_type=MESH)
+
+    def send_mail():
+        def go(k, carry):
+            letter(k).start()
+            return carry
+        lax.fori_loop(1, n, go, 0)
+        box[pc.me] = mail[pc.me]
+
+    def read_mail():
+        def wait(k, carry):
+            letter(k).wait()
+            return carry
+        lax.fori_loop(1, n, wait, 0)
+        cond_mine[...] = jnp.concatenate([box[d, 0:images, 0:per] for d in range(n)], axis=0)
+        row = images
+        for ref, width in zip(bias_rows, BIASES):
+            part = width // n
+            for at in range(0, part, 128):
+                size = min(128, part - at)
+                for d in range(n):
+                    ref[:, d * part + at:d * part + at + size] = box[d, row:row + 1, 0:size].astype(jnp.float32)
+                row += 1
+        mod_own[...] = jnp.zeros_like(mod_own)
+        for k in range(6):
+            value = dot(cond_mine[...], ada_w[:, k * D:(k + 1) * D])
+            for d in range(n):
+                mod_own[d % 2, (d // 2) % 2, d // 8, (d // 4) % 2, k * images:(k + 1) * images] = value[d * images:(d + 1) * images]
+    barrier(pc, n)
     last_of = {a: max(r for r in range(R) if rounds[r][0] == a) for a in range(6)}
 
     def loads(r):
-        a, off, w, _ = rounds[r]
-        return weight_loads(rounds[r], full, slots.at[r % 2], attn_w.at[off // 384] if a == 0 else None, load_sem.at[r % 2])
+        return weight_loads(rounds[r], full, slots.at[r % 2], load_sem.at[r % 2])
 
     def prepare():
         oh, md = onehot[...], mod
@@ -431,8 +502,8 @@
         heads[...] = jnp.zeros_like(heads)
         lax.fori_loop(0, HEADS, head, 0)
         for i in range(3):
-            w = attn_w[i].reshape(D, 384)
-            branch_attn[:, 384 * i:384 * (i + 1)] = dot(heads[...], w) + tail_b[:, 384 * i:384 * (i + 1)]
+            cols = slice(384 * i, 384 * (i + 1))
+            branch_attn[:, cols] = dot(heads[...], attn_w[:, cols]) + tail_b[:, cols]
         oh, md = onehot[...], mod
         mid = tokens[...].astype(jnp.float32) + token_rows(oh, md, 2) * branch_attn[...]
         middle[...] = mid
@@ -440,62 +511,80 @@
         second_in[...] = (centred * scale * (1.0 + token_rows(oh, md, 4)) + token_rows(oh, md, 3)).astype(jnp.bfloat16)
 
     def compute(r):
-        a, off, w, stacks = rounds[r]
+        a, off, w, stacks = rounds[r][:4]
         slot = slots.at[r % 2]
+        sw = w // stacks
+        def weight(part):
+            return chunk_weight(rounds[r], slot, per if SLABBED[a] else slot_rows[a], part)
         if a == 0:
             for j in range(3):
                 cols = slice(j * D + off, j * D + off + w)
-                projected[:, cols] = (dot(first_in[...], chunk_weight(rounds[r], slot, None, 0, j)) + qkv_b[:, cols]).astype(jnp.bfloat16)
+                value = dot(first_in[...], weight(j))
+                if j != 1:
+                    at = (j // 2) * D + off
+                    value = value + qv_b[:, at:at + w]
+                projected[:, cols] = value.astype(jnp.bfloat16)
+            attn_w[:, off:off + w] = weight(3)
             if r == last_of[0]:
                 attention()
         elif a == 1:
             for j in range(4):
                 cols = slice(j * (FF // 4) + off, j * (FF // 4) + off + w)
-                pre = dot(second_in[...], chunk_weight(rounds[r], slot, None, 0, j)) + up_b[:, cols]
+                pre = dot(second_in[...], weight(j)) + up_b[:, cols]
                 up_pre[:, cols] = pre
                 up_act[:, cols] = gelu_tanh(pre).astype(jnp.bfloat16)
         elif a == 2:
-            cols = slice(off, off + w)
-            branch_mlp[:, cols] = dot(up_act[...], chunk_weight(rounds[r], slot, None, FF // n, 0)) + tail_b[:, D + off:D + off + w]
+            branch_mlp[:, off:off + w] = dot(up_act[...], weight(0)) + tail_b[:, D + off:D + off + w]
             if r == last_of[2]:
                 hidden = middle[...] + token_rows(onehot[...], mod, 5) * branch_mlp[...]
                 mixed[...] = hidden.astype(jnp.bfloat16)
         elif a == 3:
             for j in range(4):
                 cols = slice(j * (P_SIZE // 4) + off, j * (P_SIZE // 4) + off + w)
-                pre = dot(mixed[...], chunk_weight(rounds[r], slot, None, 0, j)) + in_b[:, cols]
+                pre = dot(mixed[...], weight(j)) + in_b[:, cols]
                 first_pre[:, cols] = pre
                 first_act[:, cols] = sigmoid_linear(pre).astype(jnp.bfloat16)
-        elif a == 4:
-            sw = w // stacks
+        else:
             for s in range(stacks):
                 cols = slice(off + s * sw, off + (s + 1) * sw)
-                pre = dot(first_act[...], chunk_weight(rounds[r], slot, None, P_SIZE // n, s)) + mid_b[:, cols]
-                second_pre[:, cols] = pre
-                second_act[:, cols] = sigmoid_linear(pre).astype(jnp.bfloat16)
-        else:
-            sw = w // stacks
-            for s in range(stacks):
-                cols = slice(off + s * sw, off + (s + 1) * sw)
-                features[:, cols] = dot(second_act[...], chunk_weight(rounds[r], slot, None, P_SIZE // n, s)) + out_b[:, cols]
-
-    offs = offs + (offs[-1] + 1, offs[-1] + 2)
-    for t in range(R + offs[-1]):
-        for s in list(reversed(range(S))) + [S, S + 1]:
-            r = t - offs[s]
-            if not 0 <= r < R:
-                continue
-            if s < S:
-                stage(r, s)
-            elif s == S:
-                for cp in loads(r): cp.start()
-            else:
-                for cp in loads(r): cp.wait()
-                compute(r)
-        if t < Z + 3:
-            mod_stage(0, t)
-        if t == Z + 3:
+                if a == 4:
+                    pre = dot(first_act[...], weight(s)) + mid_b[:, cols]
+                    second_pre[:, cols] = pre
+                    second_act[:, cols] = sigmoid_linear(pre).astype(jnp.bfloat16)
+                else:
+                    features[:, cols] = dot(second_act[...], weight(s)) + out_b[:, cols]
+    slot_rows = {2: FF // n, 4: P_SIZE // n, 5: P_SIZE // n}
+
+    offs_of = lambda r: offs[rounds[r][4]]
+    ready = [max(r2 + offs_of(r2)[S - 1] for r2 in range(r + 1)) for r in range(R)]
+    mod_at = 2
+    t, computed, loaded, began = 0, 0, 0, []
+    while computed < R:
+        for s in reversed(range(S)):
+            for r in range(R):
+                if r + offs_of(r)[s] == t:
+                    stage(r, s)
+        if t == 0:
+            send_mail()
+        if t == mod_at:
+            read_mail()
+        if mod_at <= t < mod_at + Z + 3:
+            mod_stage(0, t - mod_at)
+        if t == mod_at + Z + 2:
             prepare()
+        done_now = 0
+        while True:
+            while loaded < R and ready[loaded] <= t and loaded < computed + 2:
+                for cp in loads(loaded): cp.start()
+                loaded += 1
+                began.append(t)
+            if computed == loaded or t < mod_at + Z + 2 or (t < ready[-1] and (done_now == 2 or began[computed] == t)):
+                break
+            for cp in loads(computed): cp.wait()
+            compute(computed)
+            computed += 1
+            done_now += 1
+        t += 1
     for r in range(R):
         finish(r)
     mod_finish()
@@ -503,34 +592,31 @@
 def forward(n, images, shards, small, offs, cid):
     Z, R = n // 8, len(CHUNKS)
     f32, bf = jnp.float32, jnp.bfloat16
-    tok = small[0].shape[0]
-    shapes = []
-    for sh, qt in zip(shards, QUARTERED):
-        k, w = sh.shape
-        shapes.append(jax.ShapeDtypeStruct((Z, 2, k, 4 * w) if qt else (Z, 2, 2, 2, k, w), sh.dtype))
+    tok = small[2].shape[0]
+    blocks = ((4 * D // n, D), (4 * D // n, FF // 4), (FF // n, D), (4 * D // n, P_SIZE // 4), (P_SIZE // n, P_SIZE), (P_SIZE // n, Z_OUT))
+    shapes = [jax.ShapeDtypeStruct((Z, 2, 2, 2) + b, bf) for b in blocks]
     acts = [(D, bf), (3 * D, bf), (D, bf), (D, f32), (D, f32), (D, bf), (FF, f32), (FF, bf), (D, f32), (D, bf),
             (P_SIZE, f32), (P_SIZE, bf), (P_SIZE, f32), (P_SIZE, bf), (Z_OUT, f32)]
-    mod_dims = small[3].shape[-2:]
     shapes += [jax.ShapeDtypeStruct((tok, w), dt) for w, dt in acts]
-    shapes.append(jax.ShapeDtypeStruct((images, 6 * D), f32))
-    D_ = pltpu.SemaphoreType.DMA
+    mod_dims = (-(-6 * images // 8) * 8, D)
+    shapes.append(jax.ShapeDtypeStruct((6 * images, D), f32))
+    shapes.append(jax.ShapeDtypeStruct((n * images, D // n), bf))
+    D_, V = pltpu.SemaphoreType.DMA, pltpu.VMEM
     hbm, vmem = pl.BlockSpec(memory_space=pltpu.HBM), pl.BlockSpec(memory_space=pltpu.VMEM)
     return pl.pallas_call(
-        functools.partial(forward_kernel, n, offs),
+        functools.partial(forward_kernel, n, images, offs),
         out_shape=shapes,
-        in_specs=[hbm] * 6 + [vmem] * len(small),
-        out_specs=[hbm] * 6 + [vmem] * (len(acts) + 1),
+        in_specs=[vmem] * 4 + [hbm] * 3 + [vmem] * len(small),
+        out_specs=[hbm] * 6 + [vmem] * (len(acts) + 2),
         scratch_shapes=[
-            pltpu.VMEM((2, 4, Z, 2, 144, 384), bf),
-            pltpu.VMEM((3, Z, 2, 144, 384), bf),
-            pltpu.VMEM((2, 2, Z, 2) + mod_dims, f32),
-            pltpu.VMEM((2, Z, 2) + mod_dims, f32),
-            pltpu.VMEM((3 * Z,) + mod_dims, f32),
-            pltpu.VMEM((2, Z) + mod_dims, f32),
-            D_((2, 8)),
+            V((2, 4, Z, 2, 144, 384), bf), V((D, D), bf), V(blocks[0], bf), V(blocks[1], bf), V(blocks[3], bf),
+            V((n, 16, 128), bf),
+            V((2, 2, Z, 2) + mod_dims, f32), V((2, Z, 2) + mod_dims, f32), V((3 * Z,) + mod_dims, f32), V((2, Z) + mod_dims, f32),
+        ] + [V((1, w), f32) for w in BIASES] + [
+            D_((2, 8)), D_((n,)), D_((n,)),
             D_((R,)), D_((R, 2, Z - 1)), D_((R, 2, Z - 1)), D_((R, 4)), D_((R, 4)), D_((R, 4)), D_((R, 4)),
         ] + scatter_sems(1, Z),
-        compiler_params=pltpu.CompilerParams(collective_id=cid, has_side_effects=True, vmem_limit_bytes=56 * 2**20),
+        compiler_params=pltpu.CompilerParams(collective_id=cid, has_side_effects=True, vmem_limit_bytes=58 * 2**20),
     )(*shards, *small)
 
 
@@ -566,19 +652,20 @@
     (tokens, onehot, same, mod, targets, out_grad, first_in, projected, heads, branch_attn, middle, second_in,
      up_pre, up_act, branch_mlp, mixed, first_pre, first_act, second_pre, second_act, features) = refs[:21]
     refs = refs[21:]
-    outs, refs = refs[:6], refs[6:]
+    outs, refs = refs[:7], refs[7:]
     tokens_grad, qkv_sums, attn_sums, mlp_sums, up_sums, in_sums, mid_sums, out_sums, mod_all = refs[:9]
     refs = refs[9:]
     (slots, load_sem, G_, CR_, XR_, ZR_, feature_grad, second_back, first_back, hidden_grad, mlp_grad, up_grad,
      middle_grad, attn_grad, heads_grad, projected_grad, wide, narrow, mod_grad, mod_rows, mod_lines) = refs[:21]
     refs = refs[21:]
     rounds, R = BACK_CHUNKS, len(BACK_CHUNKS)
+    per = D // n
     bf = jnp.bfloat16
     pc = Place(n)
 
     def dims(r):
         a, off, w, stacks = rounds[r]
-        return ((FF // n if QUARTERED[a] or a == 2 else stacks * (P_SIZE // n)), w // stacks)
+        return (4 * per if a < 4 else stacks * (P_SIZE // n)), w // stacks
     keep = (G_.shape[0], CR_.shape[0], XR_.shape[0])
     def cut(ref, r):
         rows, w = dims(r)
@@ -587,12 +674,23 @@
     def final(r, tot):
         a, off, w, stacks = rounds[r]
         rows, sw = dims(r)
-        rows = rows // stacks
-        for s in range(stacks):
-            outs[a][:, off + s * sw:off + (s + 1) * sw] = tot[s * rows:(s + 1) * rows]
+        qkv_out, attn_out, up_out, down_out, in_out, mid_out, out_out = outs
+        if SLABBED[a]:
+            for s in range(4):
+                part = tot[s * per:(s + 1) * per]
+                if a == 0 and s == 3:
+                    attn_out[:, off:off + w] = part
+                else:
+                    ref, q = {0: (qkv_out, D), 1: (up_out, FF // 4), 3: (in_out, P_SIZE // 4)}[a]
+                    ref[:, s * q + off:s * q + off + w] = part
+        else:
+            rows = rows // stacks
+            ref = {2: down_out, 4: mid_out, 5: out_out}[a]
+            for s in range(stacks):
+                ref[:, off + s * sw:off + (s + 1) * sw] = tot[s * rows:(s + 1) * rows]
     before, stage, finish, S = scatter_program(
         n, R, lambda r: cut(G_, r), lambda r: cut(CR_, r), lambda r: cut(XR_, r), lambda r: cut(ZR_, r), keep, refs[:7], final)
-    mod_stage, mod_finish, _ = gather_program(n, [mod_rows], [mod_all], refs[7:], ((0, 0, 128),), (False,))
+    mod_stage, mod_finish, _ = gather_program(n, [mod_rows], [mod_all], refs[7:], ((0, 0, 128, 1, 0),))
     barrier(pc)
     mod_lines[...] = jnp.zeros_like(mod_lines)
 
@@ -645,8 +743,8 @@
         a, off, w, stacks = CHAIN[k]
         slot, sem = slots.at[k % 2], load_sem.at[k % 2]
         if a == 6:
-            return weight_loads((0, off, w, stacks), full, slot, slot.at[3], sem, (3,))
-        return weight_loads((a, off, w, stacks), full, slot, slot.at[3], sem, range(3) if a == 0 else range(4))
+            return weight_loads((0, off, w, stacks), full, slot, sem, 3 * per // 16 * 16)
+        return weight_loads((a, off, w, stacks), full, slot, sem, 0, -(-3 * per // 16) * 16 if a == 0 else None)
 
     def accumulate(acc, cols, new, k, a):
         acc[:, cols] = new if k == first[a] else acc[:, cols] + new
@@ -659,7 +757,7 @@
             grad = second_back if a == 4 else feature_grad
             new = None
             for s in range(stacks):
-                part = dot_nt(grad[:, off + s * sw:off + (s + 1) * sw], chunk_weight(CHAIN[k], slot, None, P_SIZE // n, s))
+                part = dot_nt(grad[:, off + s * sw:off + (s + 1) * sw], chunk_weight(CHAIN[k], slot, P_SIZE // n, s))
                 new = part if new is None else new + part
             accumulate(wide, slice(0, P_SIZE), new, k, a)
             if k == last[a]:
@@ -667,8 +765,9 @@
                 target[...] = (wide[:, 0:P_SIZE] * sigmoid_linear_slope(pre[...])).astype(bf)
                 (mid_sums if a == 5 else in_sums)[...] = sums(target[...])
         elif a == 2:
+            whole = chunk_weight(CHAIN[k], slot, FF // n, 0)
             for q in range(4):
-                weight = chunk_weight(CHAIN[k], slot, None, FF // n, 0)[q * D:(q + 1) * D]
+                weight = whole[q * D:(q + 1) * D]
                 accumulate(wide, slice(q * D, (q + 1) * D), dot_nt(mlp_grad[:, off:off + w], weight), k, a)
             if k == last[a]:
                 for q in range(4):
@@ -681,7 +780,7 @@
             new = None
             for j in parts:
                 col = off if a == 6 else j * width + off
-                weight = slot[j, :, :, :, 0:w].reshape(-1, w)
+                weight = chunk_weight(CHAIN[k], slot, per, j)
                 part = dot_nt(src[:, col:col + w], weight)
                 new = part if new is None else new + part
             accumulate(narrow, slice(0, D), new, k, a)
@@ -727,23 +826,27 @@
                        1: (second_in, up_grad), 0: (first_in, projected_grad)}[a]
         rows, sw = dims(r)
         g = cut(G_, r)
-        if QUARTERED[a]:
-            for j in range(4):
-                if a == 0 and j == 3:
+        def put(d, at, value):
+            g[d % 2, (d // 2) % 2, d // 8, (d // 4) % 2, at:at + value.shape[0]] = value
+        if SLABBED[a]:
+            for s in range(4):
+                if a == 0 and s == 3:
                     value = dot_tn(heads[...], attn_grad[:, off:off + w])
                 else:
-                    q = {3: P_SIZE // 4, 1: FF // 4, 0: D}[a]
-                    value = dot_tn(left[...], right[:, j * q + off:j * q + off + w])
-                g[j % 2, j // 2] = value.astype(bf).reshape(Z, 2, rows, w)
+                    at = {3: P_SIZE // 4, 1: FF // 4, 0: D}[a] * s + off
+                    value = dot_tn(left[...], right[:, at:at + w])
+                value = value.astype(bf)
+                for d in range(n):
+                    put(d, s * per, value[d * per:(d + 1) * per])
         else:
             rows = rows // stacks
-            per = 1152 if a == 2 else 1024
+            piece = 1152 if a == 2 else 1024
             for s in range(stacks):
-                for part in range(left.shape[1] // per):
-                    value = dot_tn(left[:, part * per:(part + 1) * per], right[:, off + s * sw:off + (s + 1) * sw]).astype(bf)
-                    for i in range(per // rows):
-                        d = part * (per // rows) + i
-                        g[d % 2, (d // 2) % 2, d // 8, (d // 4) % 2, s * rows:(s + 1) * rows] = value[i * rows:(i + 1) * rows]
+                for part in range(left.shape[1] // piece):
+                    at = off + s * sw
+                    value = dot_tn(left[:, part * piece:(part + 1) * piece], right[:, at:at + sw]).astype(bf)
+                    for i in range(piece // rows):
+                        put(part * (piece // rows) + i, s * rows, value[i * rows:(i + 1) * rows])
 
     need = {5: 0, 4: first[4], 3: first[3], 2: first[2], 1: first[1], 0: first[0]}
     done = 0
@@ -791,7 +894,8 @@
     f32, bf = jnp.float32, jnp.bfloat16
     tok = acts[0].shape[0]
     chain_per_tick, scatter_offs, mod_offs, keep = plan
-    shapes = [jax.ShapeDtypeStruct((w.shape[2], w.shape[3] // 4) if qt else w.shape[4:], f32) for w, qt in zip(weights, QUARTERED)]
+    shapes = [jax.ShapeDtypeStruct((k // n, w), f32) for k, w in (
+        (D, 3 * D), (D, D), (D, FF), (FF, D), (D, P_SIZE), (P_SIZE, P_SIZE), (P_SIZE, Z_OUT))]
     shapes.append(jax.ShapeDtypeStruct((tok, D), bf))
     shapes += [jax.ShapeDtypeStruct((1, w), f32) for w in (3 * D, D, D, FF, P_SIZE, P_SIZE, Z_OUT)]
     hbm, vmem = pl.BlockSpec(memory_space=pltpu.HBM), pl.BlockSpec(memory_space=pltpu.VMEM)
@@ -802,7 +906,7 @@
         functools.partial(backward_kernel, n, images, chain_per_tick, scatter_offs, mod_offs),
         out_shape=shapes,
         in_specs=[hbm] * 6 + [vmem] * len(acts),
-        out_specs=[vmem] * 14 + [hbm],
+        out_specs=[vmem] * 15 + [hbm],
         scratch_shapes=[
             V((2, 4, Z, 2, 144, 384), bf),
             D_((2, 8)),
@@ -1120,88 +1224,44 @@
 ):
     owners = lax.axis_size("fsdp")
     me = lax.axis_index("fsdp")
-    groups = [[4 * g + i for i in range(4)] for g in range(owners // 4)]
     row_count = tokens.shape[0]
     rows = D // owners
-    row_sharded = jnp.concatenate(
-        [
-            qkv_weight.reshape(rows, 3 * D),
-            attn_weight.reshape(rows, D),
-            up_weight.reshape(rows, FF),
-            projector_in.reshape(rows, P_SIZE),
-        ],
-        axis=1,
-    )
-    quarters = jnp.concatenate(
-        [part.reshape(rows, 4, -1) for part in jnp.split(row_sharded, (4 * D, 8 * D), axis=1)], axis=2
-    ).transpose(1, 0, 2)
-    quarters = lax.all_to_all(
-        quarters, "fsdp", 0, 0, axis_index_groups=groups, tiled=True
-    ).reshape(4 * rows, -1)
-    bias_row = jnp.concatenate(
-        [ada_bias, qv_bias, tail_bias, up_bias, projector_in_bias, projector_mid_bias, projector_out_bias]
-    )
-    bias_width = bias_row.shape[0]
     images = cond.shape[0]
     cond_values = cond.astype(jnp.float32)
     cond_low = lowered(sigmoid_linear(cond_values))
-    cond_parts = cond_low.reshape(images, owners, rows).transpose(1, 0, 2).reshape(owners, -1)
-    received = lax.all_to_all(
-        jnp.concatenate([jnp.broadcast_to(bias_row, (owners, bias_width)), cond_parts], axis=1),
-        "fsdp", 0, 0, tiled=True,
-    )
-    bias_all = received[:, :bias_width].astype(jnp.float32)
-    cond_mine = received[:, bias_width:].reshape(owners * images, rows)
-    widths = (6 * D, 2 * D, 2 * D, FF, P_SIZE, P_SIZE, Z)
-    ends, at = [], 0
-    for width in widths:
-        at += width // owners
-        ends.append(at)
-    (
-        ada_bias_full, qv_full, tail_full, up_bias_full, proj_in_bias_full, proj_mid_bias_full, proj_out_bias_full
-    ) = [part.reshape(-1) for part in jnp.split(bias_all, ends[:-1], axis=1)]
+    letters = [jnp.pad(cond_low.reshape(images, owners, rows).transpose(1, 0, 2), ((0, 0), (0, 0), (0, 128 - rows)))]
+    biases = (ada_bias, qv_bias, tail_bias, up_bias, projector_in_bias, projector_mid_bias, projector_out_bias)
+    for bias in biases:
+        height = -(-bias.shape[0] // 128)
+        lines = jnp.pad(bias, (0, height * 128 - bias.shape[0])).reshape(1, height, 128)
+        letters.append(jnp.broadcast_to(lines, (owners, height, 128)))
+    letters = jnp.concatenate(letters, axis=1)
+    letters = jnp.pad(letters, ((0, 0), (0, 16 - letters.shape[1]), (0, 0)))
     ada_mine = ada_weight.reshape(rows, 6 * D)
-    lines = owners // 8
     used = images * 6 * D // 128
     mod_height = -(-used // 16) * 16
-    mod_part = matmul(cond_mine, ada_mine).reshape(lines, 2, 2, 2, used, 128)
-    mod_part = jnp.pad(
-        mod_part.transpose(3, 2, 0, 1, 4, 5), ((0, 0),) * 4 + ((0, mod_height - used), (0, 0))
-    )
+    widths = (6 * D, 2 * D, 2 * D, FF, P_SIZE, P_SIZE, Z)
     image_of, onehot = image_onehot(image_lengths[0], row_count)
-    key_zero = jnp.zeros((D,), jnp.float32)
-    bias_full = jnp.concatenate([qv_full[:D], key_zero, qv_full[D:]])
     same_image = (image_of[:, None] == image_of[None, :]).astype(jnp.float32)
     onehot = jnp.pad(onehot, ((0, 0), (0, 128 - onehot.shape[1])))
     results = forward(
         owners,
         images,
         (
-            quarters[:, :D],
-            quarters[:, D : 2 * D],
+            qkv_weight.reshape(rows, 3 * D),
+            attn_weight.reshape(rows, D),
+            up_weight.reshape(rows, FF),
+            projector_in.reshape(rows, P_SIZE),
             down_weight.reshape(-1, D),
-            quarters[:, 2 * D :],
             projector_mid.reshape(-1, P_SIZE),
             projector_out.reshape(-1, Z),
         ),
-        (
-            tokens,
-            onehot,
-            same_image,
-            mod_part,
-            ada_bias_full[None],
-            bias_full[None],
-            tail_full[None],
-            up_bias_full[None],
-            proj_in_bias_full[None],
-            proj_mid_bias_full[None],
-            proj_out_bias_full[None],
-        ),
-        (0, 1, 2, 3, 5, 7, 8),
+        (ada_mine, letters, tokens, onehot, same_image),
+        ((0, 1, 2, 3, 5, 7, 8), (0, 1, 2, 4, 6, 8, 9)),
         1,
     )
     mixed = results[15]
-    modulation = results[21]
+    modulation, cond_mine = results[21:]
     sums = backward(
         owners,
         images,
@@ -1211,9 +1271,9 @@
         (2, (0, 1, 2, 3, 4, 5, 6), (0, 1, 2, 3, 4, 5, 6), (3, 2, 6)),
         2,
     )
-    first_sum, up_sum, down_sum, in_sum, mid_sum, out_sum, tokens_grad = sums[:7]
-    qkv_cols, attn_cols, mlp_cols, up_cols, in_cols, mid_cols, out_cols = [part[0] for part in sums[7:14]]
-    modulation_all = sums[14].reshape(owners, mod_height, 128)[:, :used].reshape(owners * images, 6 * D)
+    qkv_sum, attn_sum, up_sum, down_sum, in_sum, mid_sum, out_sum, tokens_grad = sums[:8]
+    qkv_cols, attn_cols, mlp_cols, up_cols, in_cols, mid_cols, out_cols = [part[0] for part in sums[8:15]]
+    modulation_all = sums[15].reshape(owners, mod_height, 128)[:, :used].reshape(owners * images, 6 * D)
     grad_ada = transposed_left(cond_mine, modulation_all)
     cond_back = transposed_right(modulation_all, ada_mine).reshape(owners, images * rows)
     bias_parts = [
@@ -1234,10 +1294,6 @@
     grad_ada_bias = lax.dynamic_slice(
         column_sums(modulation_all), (me * (6 * D // owners),), (6 * D // owners,)
     )
-    back = jnp.concatenate([first_sum, up_sum, in_sum], axis=1)
-    back = lax.all_to_all(back, "fsdp", 0, 0, axis_index_groups=groups, tiled=True)
-    back = back.reshape(4, rows, -1).transpose(1, 0, 2)
-    first_rows = back[:, :, :D].reshape(rows, 4 * D)
     small_parts, at = [], 0
     for width in widths[1:]:
         small_parts.append(small[at : at + width // owners])
@@ -1249,14 +1305,14 @@
         cond_grad,
         grad_ada.reshape(-1),
         grad_ada_bias,
-        first_rows[:, : 3 * D].reshape(-1),
+        qkv_sum.reshape(-1),
         qv_small,
-        first_rows[:, 3 * D :].reshape(-1),
+        attn_sum.reshape(-1),
         tail_small,
-        back[:, :, D : 2 * D].reshape(-1),
+        up_sum.reshape(-1),
         up_small,
         down_sum.reshape(-1),
-        back[:, :, 2 * D :].reshape(-1),
+        in_sum.reshape(-1),
         in_small,
         mid_sum.reshape(-1),
         mid_small,

time: 584 us -> 517 us (0.89)
  local copies, waits for them, and re-layouts: 49.6 us -> 27.4 us
  waiting for transfers between devices: 15.8 us -> 0.01 us
  starting transfers between devices: 21.7 us -> 6.73 us
  Pallas kernels: 476 us -> 468 us
    all_to_all x3 -> x0, starting transfers between devices: 15.1 us -> none  [the longest x1 7.3 us: per_device_kernels(): lax.all_to_all(jnp.concatenate([jnp.broadcast_to(bias_row, (owners, bias_...]
    all_to_all x3 -> x0, waiting for transfers between devices: 11.1 us -> none  [the longest x1 9.98 us: per_device_kernels(): lax.all_to_all(back, 'fsdp', 0, 0, axis_index_groups=groups, tiled=True)]
    pallas_call x1, Pallas kernels: 233 us -> 225 us  [forward(): pl.pallas_call(functools.partial(forward_kernel, n, images, offs), out_sh...]
  transfers between devices with their start and end apart: 4 -> 1, of which waited for: 3 -> 0; matrix products, arithmetic and copies ran while one was open for 6% -> 2% of each run, Pallas kernels for 0% -> 0%
where the time goes in v3:
time: 517 us; the launch traced here: 510 us
  Pallas kernels  468 us (91%)
  local copies, waits for them, and re-layouts  27.4 us (5%)
  starting transfers between devices  6.73 us (1%)
    pallas_call x1, Pallas kernels, backward(): pl.pallas_call(functools.partial(backward_kernel, n, images, chain_per_ti...  243 us
    pallas_call x1, Pallas kernels, forward(): pl.pallas_call(functools.partial(forward_kernel, n, images, offs), out_sh...  225 us
  transfers between devices with their start and end apart: 1, of which 0 were waited for; matrix products, arithmetic and copies ran while one was open for 2% of the time, Pallas kernels for 0%

profile of v3, /device:TPU:0, one launch (start us, length us, event | category | flops | bytes accessed | tf_op | source)
XLA Modules:
  0.0 509.7 jit_solution(3586109439610841931)
XLA Ops:
  0.7 0.9 reduce-window.8
  1.6 0.1 convert_reduce_fusion.1
  1.7 0.1 iota_compare_fusion
  1.8 0.7 compare_convert_fusion
  2.5 2.4 reshape.173.refs_7_
  4.9 0.8 fusion.3
  5.7 0.1 reshape.174
  5.9 0.0 copy-done.26
  5.9 0.0 copy-start.10
  6.2 0.5 concatenate.22
  6.7 0.0 copy-start.14
  6.7 0.7 pad.48.refs_8_
  7.4 1.1 reshape.168.refs_2_
  8.5 1.1 reshape.170.refs_4_
  9.6 1.0 reshape.166.refs_0_
  10.6 0.8 reshape.171.refs_5_
  11.5 0.8 reshape.169.refs_3_
  12.2 0.7 reshape.172.refs_6_
  13.0 0.8 reshape.167.refs_1_
  13.7 225.3 %shard_map.331 = (bf16[4,2,2,2,144,1152]{5,4,3,2,1,0:T(8,128)(2,1)}, bf16[4,2,2,2,144,1152]{5,4,3,2,1,0:T(8,128)(2,1)}, bf16[4,2,2,2,144,1152]{5,4,3,2,1,0:T(8,1...) custom-call(bf16[36,3456]{1,0:T(8,128)(2,1)} %reshape.166.refs_0_, ...), custom_call_target="tpu_custom_call" | custom-call | tf_op jit(solution)/shard_map/pallas_call | solution.py:606
  239.0 242.9 %shard_map.332 = (f32[36,3456]{1,0:T(8,128)}, f32[36,1152]{1,0:T(8,128)}, f32[36,4608]{1,0:T(8,128)}, f32[144,1152]{1,0:T(8,128)}, f32[36,2048]{1,0:T(8,128)}, /...) custom-call(bf16[4,2,2,2,144,1152]{5,4,3,2,1,0:T(8,128)(2,1)} %get-t, ...), custom_call_target="tpu_custom_call" | custom-call | tf_op jit(solution)/shard_map/pallas_call | solution.py:905
  481.9 1.4 slice.46
  483.4 0.0 copy-start
  483.4 1.5 reshape.178
  485.0 0.1 concatenate.26
  485.1 0.1 concatenate.27
  485.2 0.1 concatenate.23
  485.3 0.1 concatenate.24
  485.4 0.5 fusion.9
  485.9 0.1 reshape.179
  486.1 0.1 reshape_squeeze.12
  486.1 0.5 broadcast.54
  486.7 0.7 reduce.14
  487.3 0.1 reshape_squeeze.13
  487.4 0.7 reduce.15
  488.1 0.1 reshape_squeeze.14
  488.2 0.1 reshape_squeeze.15
  488.3 0.1 concatenate.29
  488.4 0.7 all_to_all.8
  489.1 6.7 %all-to-all-start = ((f32[32,1,548]{2,1,0:T(1,128)}), f32[32,1,548]{2,1,0:T(1,128)S(1)}, u32[]{:S(2)}, u32[]{:S(2)}) async-start(f32[32,1,548]{2,1,0:T(1,128)} %all_to_all.8), calls=%async_computation | async-start | bytes 163840 | tf_op jit(solution)/shard_map/all_to_all | solution.py:1290
  495.8 0.4 fusion.10
  496.2 1.0 reshape.182
  497.3 0.4 copy-done.2
  497.6 0.9 reshape.185
  498.5 0.9 reshape.186
  499.4 0.4 copy-done.5
  499.8 0.9 copy.52
  500.7 0.8 reshape.183
  501.5 0.8 reshape.187
  502.3 0.7 reshape.189
  503.0 0.7 reshape.184
  503.6 0.2 convert_reduce_fusion
  503.9 0.6 dynamic_slice.3
  504.5 0.0 all-to-all-done
  504.5 0.1 slice_reduce_fusion
  504.6 0.6 fusion.8
  505.2 0.6 fusion.7
  505.8 0.6 slice.42
  506.4 0.6 slice.45
  507.0 0.1 reshape.180
  507.1 0.1 reshape.181
  507.2 0.6 fusion.6
  507.9 0.7 copy.59
  508.6 0.7 copy.60
  (86 shorter events, 0.4 us)
Async XLA Ops:
  0.7 5.2 %copy-start.26 = (bf16[216]{0:T(256)(128)(2,1)S(1)}, bf16[216]{0:T(256)(128)(2,1)}, u32[]{:S(2)}) copy-start(bf16[216]{0:T(256)(128)(2,1)} %param.24) | copy-start | bytes 1300
  0.7 5.3 %copy-start.27 = (bf16[72]{0:T(256)(128)(2,1)S(1)}, bf16[72]{0:T(256)(128)(2,1)}, u32[]{:S(2)}) copy-start(bf16[72]{0:T(256)(128)(2,1)} %param.26) | copy-start | bytes 436
  0.7 5.3 %copy-start.28 = (bf16[72]{0:T(256)(128)(2,1)S(1)}, bf16[72]{0:T(256)(128)(2,1)}, u32[]{:S(2)}) copy-start(bf16[72]{0:T(256)(128)(2,1)} %param.28) | copy-start | bytes 436
  0.7 5.3 %copy-start.29 = (bf16[144]{0:T(256)(128)(2,1)S(1)}, bf16[144]{0:T(256)(128)(2,1)}, u32[]{:S(2)}) copy-start(bf16[144]{0:T(256)(128)(2,1)} %param.30) | copy-start | bytes 868
  0.7 5.3 %copy-start.30 = (bf16[64]{0:T(256)(128)(2,1)S(1)}, bf16[64]{0:T(256)(128)(2,1)}, u32[]{:S(2)}) copy-start(bf16[64]{0:T(256)(128)(2,1)} %param.33) | copy-start | bytes 388
  0.7 5.3 %copy-start.31 = (bf16[64]{0:T(256)(128)(2,1)S(1)}, bf16[64]{0:T(256)(128)(2,1)}, u32[]{:S(2)}) copy-start(bf16[64]{0:T(256)(128)(2,1)} %param.35) | copy-start | bytes 388
  0.7 5.3 %copy-start.32 = (bf16[24]{0:T(256)(128)(2,1)S(1)}, bf16[24]{0:T(256)(128)(2,1)}, u32[]{:S(2)}) copy-start(bf16[24]{0:T(256)(128)(2,1)} %param.37) | copy-start | bytes 148
  0.7 6.7 %copy-start.7 = (bf16[165888]{0:T(1024)(128)(2,1)S(1)}, bf16[165888]{0:T(1024)(128)(2,1)}, u32[]{:S(2)}) copy-start(bf16[165888]{0:T(1024)(128)(2,1)} %param.29) | copy-start | bytes 995332
  2.5 6.0 %copy-start.6 = (bf16[165888]{0:T(1024)(128)(2,1)S(1)}, bf16[165888]{0:T(1024)(128)(2,1)}, u32[]{:S(2)}) copy-start(bf16[165888]{0:T(1024)(128)(2,1)} %param.31) | copy-start | bytes 995332
  4.9 4.7 copy-start.11
  5.9 4.8 copy-start.10
  6.7 4.8 copy-start.14
  7.4 4.8 copy-start.15
  7.4 5.6 %copy-start.16 = (bf16[41472]{0:T(1024)(128)(2,1)S(1)}, bf16[41472]{0:T(1024)(128)(2,1)}, u32[]{:S(2)}) copy-start(bf16[41472]{0:T(1024)(128)(2,1)} %param.27) | copy-start | bytes 248836
  483.4 1.6 copy-start.24
  483.4 1.7 copy-start.23
  483.4 1.8 copy-start.22
  483.4 2.0 copy-start
  484.9 1.1 copy-start.19
  484.9 1.7 copy-start.21
  484.9 2.5 copy-start.20
  484.9 3.2 copy-start.25
  485.4 10.4 %copy-start.18 = (bf16[96,36]{1,0:T(8,128)(2,1)S(1)}, bf16[96,36]{1,0:T(8,128)(2,1)}, u32[]{:S(2)}) copy-start(bf16[96,36]{1,0:T(8,128)(2,1)} %get-tuple-element.88) | copy-start | bytes 20740
  489.1 15.4 %all-to-all-start = ((f32[32,1,548]{2,1,0:T(1,128)}), f32[32,1,548]{2,1,0:T(1,128)S(1)}, u32[]{:S(2)}, u32[]{:S(2)}) async-start(f32[32,1,548]{2,1,0:T(1,128)} %all_to_all.8), calls=%async_computation | async-start | bytes 163840 | tf_op jit(solution)/shard_map/all_to_all | solution.py:1290
  496.2 1.4 copy-start.2
  497.3 1.3 copy-start.3
  498.5 1.3 copy-start.5
  498.5 2.1 copy-start.4
  499.4 2.1 copy-start.8
  499.8 2.5 copy-start.12
  499.8 3.2 copy-start.13
  502.3 5.0 copy-start.17
  502.3 5.6 %copy-start.1 = (bf16[128,1152]{1,0:T(8,128)(2,1)S(1)}, bf16[128,1152]{1,0:T(8,128)(2,1)}, u32[]{:S(2)}) copy-start(bf16[128,1152]{1,0:T(8,128)(2,1)} %get-tuple-element.122.refs_21_) | copy-start | bytes 884740
  503.6 5.0 copy-start.9

commit v4 on v3

--- a/solution.py
+++ b/solution.py
@@ -138,15 +138,13 @@
 
 SLABBED = (True, True, False, True, False, False)
 
-def gather_rounds():
-    out = []
-    for a in range(3):
-        out += [(a, 0, 384, 1, 0), (a, 384, 256, 1, 1), (a, 640, 384, 1, 0), (a, 1024, 128, 1, 0)]
-    out += [(3, 0, 384, 1, 0), (3, 384, 128, 1, 1)]
-    out += [(4, 0, 768, 2, 0), (4, 768, 512, 2, 1), (4, 1280, 768, 2, 0)]
-    out += [(5, 0, 256, 2, 1), (5, 256, 512, 2, 0)]
-    return tuple(out)
-CHUNKS = gather_rounds()
+CHUNKS = tuple(
+    (a, off, w, stacks, 1 if k in (1, 5, 9) else 0)
+    for k, (a, off, w, stacks) in enumerate(
+        tuple((a, off, 384, 1) for a in range(3) for off in (0, 384, 768))
+        + ((3, 0, 384, 1), (3, 384, 128, 1), (4, 0, 768, 2), (4, 768, 768, 2), (4, 1536, 512, 2), (5, 0, 512, 2), (5, 512, 256, 2))
+    )
+)
 
 def dot(a, b):
     return jnp.dot(a, b, preferred_element_type=jnp.float32)
@@ -294,70 +292,151 @@
     return jnp.concatenate(
         [slot[j, zz, yy, part * rows:(part + 1) * rows, 0:sw] for zz in range(Z) for yy in range(2) for j in range(4)], axis=0)
 
-def scatter_program(n, R, G, CR, XR, ZR, keep, sems, final):
+def scatter_program(n, R, G, CR, OWN, XR, ZR, keep, sems, final, late=(), P=None):
     cs, cr, xs, xr, zs_, zr, credit = sems
-    keep_g, keep_c, keep_x = keep
+    keep_g, keep_c, keep_o, keep_x, keep_p = keep
     pc = Place(n)
     Z = pc.Z; H = Z // 2
     z, y, x, c = pc.z, pc.y, pc.x, pc.c
     up_dev = jnp.minimum(pc.me + 8, n - 1)
     down_dev = jnp.maximum(pc.me - 8, 0)
+    early = [r for r in range(R) if r not in late]
+    def turn(r): return (late if r in late else early).index(r)
+    def first_use(r): return turn(r) < (keep_p if r in late else keep_x)
+    def last_use(r): return turn(r) + (keep_p if r in late else keep_x) >= len(late if r in late else early)
+    def base(r): return 5 if r in late else 1
     def rcopy(src, dst, ss, rs, dev):
         return pltpu.make_async_remote_copy(src_ref=src, dst_ref=dst, send_sem=ss, recv_sem=rs, device_id=(dev,), device_id_type=MESH)
     def signal(k, dev):
         pl.semaphore_signal(credit.at[k], inc=1, device_id=(dev,), device_id_type=MESH)
+    def spend(k):
+        pl.semaphore_wait(credit.at[k], 1)
     def core(r): return rcopy(G(r).at[1 - c], CR(r), cs.at[r], cr.at[r], pc.cp)
     def xy(r, k):
-        b, xb = G(r).at[c], XR(r)
+        if r in late:
+            own, _, px = P(r)
+            dev = (pc.yp if r % 2 else pc.xp, pc.xp, pc.yp)[k]
+            src = own.at[x if k == 2 else 1 - x, z, y if k == 1 else 1 - y]
+            return rcopy(src, px.at[k], xs.at[r, k], xr.at[r, k], dev)
+        b, xb = OWN(r), XR(r)
         if k == 0: return rcopy(b.at[1 - x, 0:H, 1 - y], xb.at[0:H], xs.at[r, 0], xr.at[r, 0], pc.yp)
         if k == 1: return rcopy(b.at[1 - x, H:Z, 1 - y], xb.at[H:Z], xs.at[r, 1], xr.at[r, 1], pc.xp)
         if k == 2: return rcopy(b.at[1 - x, :, y], xb.at[Z:2 * Z], xs.at[r, 2], xr.at[r, 2], pc.xp)
         return rcopy(b.at[x, :, 1 - y], xb.at[2 * Z:3 * Z], xs.at[r, 3], xr.at[r, 3], pc.yp)
+    def line_refs(r, d):
+        if r in late:
+            own, pz, _ = P(r)
+            return own.at[:, d], pz
+        return XR(r).at[Z + d], ZR(r)
     def zc(r, side, d):
-        return rcopy(XR(r).at[Z + d], ZR(r).at[side, d], zs_.at[r, side, d], zr.at[r, side, d], up_dev if side == 0 else down_dev)
-    def waits_send(r):
-        core(r).wait_send()
-        for k in range(4): xy(r, k).wait_send()
+        src, dst = line_refs(r, d)
+        at = d - z - 1 if side == 0 else Z - z + 1 + d
+        return rcopy(src, dst.at[at], zs_.at[r, side, d], zr.at[r, side, d], up_dev if side == 0 else down_dev)
+    def zgot(r, side, d):
+        src, dst = line_refs(r, d)
+        at = d - z if side == 0 else Z - z + d
+        rcopy(src, dst.at[at], zs_.at[r, side, d], zr.at[r, side, d], up_dev if side == 0 else down_dev).wait_recv()
+    def plane_sent(o):
+        for k in range(4): xy(early[o], k).wait_send()
     def zwaits_send(r):
         for d in range(Z):
             @pl.when(d > z)
             def _(): zc(r, 0, d).wait_send()
             @pl.when(d < z)
             def _(): zc(r, 1, d).wait_send()
+    def add_line(r, side, d, at):
+        if r in late:
+            own, pz, _ = P(r)
+            for xx in range(2):
+                for yy in range(2):
+                    own[xx, d, yy] = own[xx, d, yy] + pz[at, xx, yy]
+        else:
+            XR(r)[Z + d] = XR(r)[Z + d] + ZR(r)[at]
     def zstep(r, s):
         for side in (0, 1):
             p = s if side == 0 else Z - 1 - s
             @pl.when(z == p)
             def _():
-                if r >= keep_x and (p < Z - 1 if side == 0 else p > 0):
-                    pl.semaphore_wait(credit.at[3 + side], 1)
+                if not first_use(r) and (p < Z - 1 if side == 0 else p > 0):
+                    spend(base(r) + 2 + side)
                 for d in range(Z):
                     if (d > p) if side == 0 else (d < p):
                         if s > 0:
-                            zc(r, side, d).wait_recv()
-                            XR(r)[Z + d] = XR(r)[Z + d] + ZR(r)[side, d]
+                            zgot(r, side, d)
+                            add_line(r, side, d, d - p if side == 0 else Z - p + d)
                         zc(r, side, d).start()
+    def give_back(r):
+        if not last_use(r):
+            signal(base(r), pc.xp)
+            signal(base(r) + 1, pc.yp)
+            @pl.when(z < Z - 1)
+            def _(): signal(base(r) + 3, up_dev)
+            @pl.when(z > 0)
+            def _(): signal(base(r) + 2, down_dev)
     def before(r):
         if r >= keep_g:
-            waits_send(r - keep_g)
+            core(r - keep_g).wait_send()
+    def core_sum(r, out):
+        b = G(r).at[c]
+        core(r).wait_recv()
+        def add(i, carry):
+            xx, zz, yy = i // (2 * Z), (i // 2) % Z, i % 2
+            out[xx, zz, yy] = b[xx, zz, yy] + CR(r)[xx, zz, yy]
+            return carry
+        lax.fori_loop(0, 4 * Z, add, 0)
+        if r + keep_c < R:
+            signal(0, pc.cp)
+    def late_stage(r, s):
+        own, pz, px = P(r)
+        if s == 1:
+            core_sum(r, own)
+            zstep(r, 0)
+        elif s < Z:
+            zstep(r, s - 1)
+        elif s == Z:
+            for d in range(Z):
+                @pl.when(d == z)
+                def _():
+                    if d > 0:
+                        zgot(r, 0, d)
+                        add_line(r, 0, d, 0)
+                    if d < Z - 1:
+                        zgot(r, 1, d)
+                        add_line(r, 1, d, Z)
+            if not first_use(r):
+                spend(base(r))
+                spend(base(r) + 1)
+            xy(r, 0).start()
+            xy(r, 2 if r % 2 else 1).start()
+        elif s == Z + 1:
+            xy(r, 0).wait_recv()
+            if r % 2:
+                own[1 - x, z, y] = own[1 - x, z, y] + px[0]
+            else:
+                own[x, z, 1 - y] = own[x, z, 1 - y] + px[0]
+            xy(r, 1 if r % 2 else 2).start()
+        else:
+            xy(r, 1).wait_recv()
+            xy(r, 2).wait_recv()
+            final(r, own[x, z, y].astype(jnp.float32) + px[1].astype(jnp.float32) + px[2].astype(jnp.float32))
+            for k in range(3): xy(r, k).wait_send()
+            zwaits_send(r)
+            give_back(r)
     def stage(r, s):
-        b = G(r).at[c]
+        b = None if r in late else OWN(r)
         if s == 0:
             if r >= keep_c:
-                pl.semaphore_wait(credit.at[0], 1)
+                spend(0)
             core(r).start()
+        elif r in late:
+            late_stage(r, s)
         elif s == 1:
-            core(r).wait_recv()
-            def add(i, carry):
-                xx, zz, yy = i // (2 * Z), (i // 2) % Z, i % 2
-                b[xx, zz, yy] = b[xx, zz, yy] + CR(r)[xx, zz, yy]
-                return carry
-            lax.fori_loop(0, 4 * Z, add, 0)
-            if r + keep_c < R:
-                signal(0, pc.cp)
-            if r >= keep_x:
-                pl.semaphore_wait(credit.at[1], 1)
-                pl.semaphore_wait(credit.at[2], 1)
+            if turn(r) >= keep_o:
+                plane_sent(turn(r) - keep_o)
+            core_sum(r, b)
+            if not first_use(r):
+                spend(base(r))
+                spend(base(r) + 1)
             xy(r, 0).start(); xy(r, 1).start()
         elif s == 2:
             xy(r, 0).wait_recv()
@@ -387,28 +466,24 @@
                 def _():
                     tot = XR(r)[Z + d].astype(jnp.float32)
                     if d > 0:
-                        zc(r, 0, d).wait_recv()
-                        tot = tot + ZR(r)[0, d].astype(jnp.float32)
+                        zgot(r, 0, d)
+                        tot = tot + ZR(r)[0].astype(jnp.float32)
                     if d < Z - 1:
-                        zc(r, 1, d).wait_recv()
-                        tot = tot + ZR(r)[1, d].astype(jnp.float32)
+                        zgot(r, 1, d)
+                        tot = tot + ZR(r)[Z].astype(jnp.float32)
                     final(r, tot)
             zwaits_send(r)
-            if r + keep_x < R:
-                signal(1, pc.xp)
-                signal(2, pc.yp)
-                @pl.when(z < Z - 1)
-                def _(): signal(4, up_dev)
-                @pl.when(z > 0)
-                def _(): signal(3, down_dev)
+            give_back(r)
     def finish():
         for r in range(max(0, R - keep_g), R):
-            waits_send(r)
+            core(r).wait_send()
+        for o in range(max(0, len(early) - keep_o), len(early)):
+            plane_sent(o)
     return before, stage, finish, Z + 3
 
 def scatter_sems(R, Z):
     D_ = pltpu.SemaphoreType.DMA
-    return [D_((R,)), D_((R,)), D_((R, 4)), D_((R, 4)), D_((R, 2, Z)), D_((R, 2, Z)), pltpu.SemaphoreType.REGULAR((5,))]
+    return [D_((R,)), D_((R,)), D_((R, 4)), D_((R, 4)), D_((R, 2, Z)), D_((R, 2, Z)), pltpu.SemaphoreType.REGULAR((9,))]
 
 BIASES = (6 * D, 2 * D, 2 * D, FF, P_SIZE, P_SIZE, Z_OUT)
 
@@ -417,9 +492,14 @@
     qkv_w, attn_in, up_w, in_w, down_w, mid_w, out_w, ada_w, mail, tokens, onehot, same = refs[:12]
     refs = refs[12:]
     full, refs = refs[:6], refs[6:]
+    act_outs, (mod, cond_mine) = refs[:15], refs[15:17]
+    refs = refs[17:]
+    acts, refs = refs[:15], refs[15:]
     (first_in, projected, heads, branch_attn, middle, second_in, up_pre, up_act, branch_mlp, mixed,
-     first_pre, first_act, second_pre, second_act, features, mod, cond_mine) = refs[:17]
-    refs = refs[17:]
+     first_pre, first_act, second_pre, second_act, features) = acts
+    act_sem, refs = refs[0], refs[1:]
+    def leave(*which):
+        return [pltpu.make_async_copy(acts[k], act_outs[k], act_sem.at[k]) for k in which]
     slots, attn_w, first_own, up_own, in_own, box, mod_own, mod_core, mod_xy, mod_line = refs[:10]
     bias_rows, refs = refs[10:17], refs[17:]
     load_sem, mail_send, mail_recv = refs[:3]
@@ -440,7 +520,7 @@
                 row = k * images + i
                 mod[row:row + 1] = tot[row:row + 1] + ada_b[:, k * D:(k + 1) * D]
     _, mod_stage, mod_finish, _ = scatter_program(
-        n, 1, lambda r: mod_own, lambda r: mod_core, lambda r: mod_xy, lambda r: mod_line, (1, 1, 1), refs[10:], mod_final)
+        n, 1, lambda r: mod_own, lambda r: mod_core, lambda r: mod_own.at[pc.c], lambda r: mod_xy, lambda r: mod_line, (1, 1, 1, 1, 1), refs[10:], mod_final)
 
     def letter(k):
         dest = lax.rem(pc.me + k, n)
@@ -553,7 +633,10 @@
                     second_act[:, cols] = sigmoid_linear(pre).astype(jnp.bfloat16)
                 else:
                     features[:, cols] = dot(second_act[...], weight(s)) + out_b[:, cols]
+        if r == last_of[a]:
+            for cp in leave(*left_by[a]): cp.start()
     slot_rows = {2: FF // n, 4: P_SIZE // n, 5: P_SIZE // n}
+    left_by = {0: (0, 1, 2, 3, 4, 5), 1: (6, 7), 2: (8, 9), 3: (10, 11), 4: (12, 13), 5: (14,)}
 
     offs_of = lambda r: offs[rounds[r][4]]
     ready = [max(r2 + offs_of(r2)[S - 1] for r2 in range(r + 1)) for r in range(R)]
@@ -585,6 +668,7 @@
             computed += 1
             done_now += 1
         t += 1
+    for cp in leave(*range(15)): cp.wait()
     for r in range(R):
         finish(r)
     mod_finish()
@@ -607,11 +691,11 @@
         functools.partial(forward_kernel, n, images, offs),
         out_shape=shapes,
         in_specs=[vmem] * 4 + [hbm] * 3 + [vmem] * len(small),
-        out_specs=[hbm] * 6 + [vmem] * (len(acts) + 2),
-        scratch_shapes=[
+        out_specs=[hbm] * (6 + len(acts)) + [vmem] * 2,
+        scratch_shapes=[V((tok, w), dt) for w, dt in acts] + [D_((len(acts),))] + [
             V((2, 4, Z, 2, 144, 384), bf), V((D, D), bf), V(blocks[0], bf), V(blocks[1], bf), V(blocks[3], bf),
             V((n, 16, 128), bf),
-            V((2, 2, Z, 2) + mod_dims, f32), V((2, Z, 2) + mod_dims, f32), V((3 * Z,) + mod_dims, f32), V((2, Z) + mod_dims, f32),
+            V((2, 2, Z, 2) + mod_dims, f32), V((2, Z, 2) + mod_dims, f32), V((3 * Z,) + mod_dims, f32), V((Z + 1,) + mod_dims, f32),
         ] + [V((1, w), f32) for w in BIASES] + [
             D_((2, 8)), D_((n,)), D_((n,)),
             D_((R,)), D_((R, 2, Z - 1)), D_((R, 2, Z - 1)), D_((R, 4)), D_((R, 4)), D_((R, 4)), D_((R, 4)),
@@ -620,15 +704,15 @@
     )(*shards, *small)
 
 
-BACK_CHUNKS = (
-    ((5, 0, 768, 2),)
-    + ((4, 0, 768, 2), (4, 768, 768, 2), (4, 1536, 512, 2))
-    + ((3, 0, 384, 1), (3, 384, 128, 1))
-    + tuple((2, 384 * i, 384, 1) for i in range(3))
-    + tuple((1, 384 * i, 384, 1) for i in range(3))
-    + tuple((0, 384 * i, 384, 1) for i in range(3))
-)
-CHAIN = BACK_CHUNKS[:12] + tuple((6, 384 * i, 384, 1) for i in range(3)) + BACK_CHUNKS[12:]
+def back_rounds(order):
+    out = []
+    for a, total, width, stacks in order:
+        out += [(a, off, min(width, total - off), stacks) for off in range(0, total, width)]
+    return tuple(out)
+
+BACK_CHUNKS = back_rounds(((5, 768, 512, 2), (4, P_SIZE, 512, 2), (3, P_SIZE // 4, 256, 1), (2, D, 256, 1), (1, FF // 4, 256, 1), (0, D, 256, 1)))
+LATE = (3, 8, 12, 16)
+CHAIN = back_rounds(((5, 768, 768, 2), (4, P_SIZE, 768, 2), (3, P_SIZE // 4, 384, 1), (2, D, 384, 1), (1, FF // 4, 384, 1), (6, D, 384, 1), (0, D, 384, 1)))
 
 def dot_tn(a, b):
     return lax.dot_general(a, b, (((0,), (0,)), ((), ())), preferred_element_type=jnp.float32)
@@ -649,15 +733,20 @@
 def backward_kernel(n, images, chain_per_tick, scatter_offs, mod_offs, *refs):
     Z = n // 8
     full, refs = refs[:6], refs[6:]
-    (tokens, onehot, same, mod, targets, out_grad, first_in, projected, heads, branch_attn, middle, second_in,
-     up_pre, up_act, branch_mlp, mixed, first_pre, first_act, second_pre, second_act, features) = refs[:21]
-    refs = refs[21:]
+    (tokens, onehot, same, mod, targets, out_grad), act_ins, refs = refs[:6], refs[6:21], refs[21:]
     outs, refs = refs[:7], refs[7:]
     tokens_grad, qkv_sums, attn_sums, mlp_sums, up_sums, in_sums, mid_sums, out_sums, mod_all = refs[:9]
     refs = refs[9:]
-    (slots, load_sem, G_, CR_, XR_, ZR_, feature_grad, second_back, first_back, hidden_grad, mlp_grad, up_grad,
-     middle_grad, attn_grad, heads_grad, projected_grad, wide, narrow, mod_grad, mod_rows, mod_lines) = refs[:21]
-    refs = refs[21:]
+    acts, act_sem, refs = refs[:15], refs[15], refs[16:]
+    (first_in, projected, heads, branch_attn, middle, second_in, up_pre, up_act, branch_mlp, mixed,
+     first_pre, first_act, second_pre, second_act, features) = acts
+    def bring(which):
+        return [pltpu.make_async_copy(act_ins[k], acts[k], act_sem.at[k]) for k in which]
+    soon, later = (14, 12, 13, 11, 10), (9, 8, 6, 7, 5, 4, 3, 2, 1, 0)
+    for cp in bring(soon + later): cp.start()
+    (slots, load_sem, G_, CR_, OWN_, XR_, ZR_, PB_, PZ_, PX_, feature_grad, second_back, first_back, hidden_grad, mlp_grad, up_grad,
+     middle_grad, attn_grad, heads_grad, projected_grad, wide, narrow, mod_grad, mod_rows, mod_lines) = refs[:25]
+    refs = refs[25:]
     rounds, R = BACK_CHUNKS, len(BACK_CHUNKS)
     per = D // n
     bf = jnp.bfloat16
@@ -666,11 +755,12 @@
     def dims(r):
         a, off, w, stacks = rounds[r]
         return (4 * per if a < 4 else stacks * (P_SIZE // n)), w // stacks
-    keep = (G_.shape[0], CR_.shape[0], XR_.shape[0])
-    def cut(ref, r):
+    keep = (G_.shape[0], CR_.shape[0], OWN_.shape[0], XR_.shape[0], PB_.shape[0])
+    early = [r for r in range(R) if r not in LATE]
+    def cut(ref, r, at):
         rows, w = dims(r)
         lead = (slice(None),) * (len(ref.shape) - 3)
-        return ref.at[(r % ref.shape[0],) + lead + (slice(0, rows), slice(0, w))]
+        return ref.at[(at % ref.shape[0],) + lead + (slice(0, rows), slice(0, w))]
     def final(r, tot):
         a, off, w, stacks = rounds[r]
         rows, sw = dims(r)
@@ -689,7 +779,9 @@
             for s in range(stacks):
                 ref[:, off + s * sw:off + (s + 1) * sw] = tot[s * rows:(s + 1) * rows]
     before, stage, finish, S = scatter_program(
-        n, R, lambda r: cut(G_, r), lambda r: cut(CR_, r), lambda r: cut(XR_, r), lambda r: cut(ZR_, r), keep, refs[:7], final)
+        n, R, lambda r: cut(G_, r, r), lambda r: cut(CR_, r, r),
+        lambda r: cut(OWN_, r, early.index(r)), lambda r: cut(XR_, r, early.index(r)), lambda r: cut(ZR_, r, early.index(r)), keep, refs[:7], final, LATE,
+        lambda r: tuple(cut(ref, r, LATE.index(r)) for ref in (PB_, PZ_, PX_)))
     mod_stage, mod_finish, _ = gather_program(n, [mod_rows], [mod_all], refs[7:], ((0, 0, 128, 1, 0),))
     barrier(pc)
     mod_lines[...] = jnp.zeros_like(mod_lines)
@@ -751,6 +843,8 @@
 
     def chain(k):
         a, off, w, stacks = CHAIN[k]
+        if k == first[3]:
+            for cp in bring(later): cp.wait()
         slot = slots.at[k % 2]
         sw = w // stacks
         if a in (4, 5):
@@ -825,7 +919,7 @@
         left, right = {5: (second_act, feature_grad), 4: (first_act, second_back), 3: (mixed, first_back), 2: (up_act, mlp_grad),
                        1: (second_in, up_grad), 0: (first_in, projected_grad)}[a]
         rows, sw = dims(r)
-        g = cut(G_, r)
+        g = cut(G_, r, r)
         def put(d, at, value):
             g[d % 2, (d // 2) % 2, d // 8, (d // 4) % 2, at:at + value.shape[0]] = value
         if SLABBED[a]:
@@ -852,14 +946,15 @@
     done = 0
     mod_start = None
     for cp in chain_loads(0): cp.start()
+    for cp in bring(soon): cp.wait()
     start_chain()
     t = 0
     while True:
-        busy = False
         for s in reversed(range(1, S)):
-            r = t - scatter_offs[s]
-            if 0 <= r < R:
-                stage(r, s); busy = True
+            for r in range(R):
+                if r + scatter_offs[r in LATE][s] == t:
+                    stage(r, s)
+        busy = any(r + scatter_offs[r in LATE][S - 1] >= t for r in range(R))
         if t < R:
             busy = True
             while done < need[rounds[t][0]]:
@@ -894,6 +989,8 @@
     f32, bf = jnp.float32, jnp.bfloat16
     tok = acts[0].shape[0]
     chain_per_tick, scatter_offs, mod_offs, keep = plan
+    most = (144, max(c[2] // c[3] for c in BACK_CHUNKS))
+    late = most if LATE else (16, 128)
     shapes = [jax.ShapeDtypeStruct((k // n, w), f32) for k, w in (
         (D, 3 * D), (D, D), (D, FF), (FF, D), (D, P_SIZE), (P_SIZE, P_SIZE), (P_SIZE, Z_OUT))]
     shapes.append(jax.ShapeDtypeStruct((tok, D), bf))
@@ -905,21 +1002,23 @@
     return pl.pallas_call(
         functools.partial(backward_kernel, n, images, chain_per_tick, scatter_offs, mod_offs),
         out_shape=shapes,
-        in_specs=[hbm] * 6 + [vmem] * len(acts),
+        in_specs=[hbm] * 6 + [vmem] * 6 + [hbm] * (len(acts) - 6),
         out_specs=[vmem] * 15 + [hbm],
-        scratch_shapes=[
+        scratch_shapes=[V(a.shape, a.dtype) for a in acts[6:]] + [D_((len(acts) - 6,))] + [
             V((2, 4, Z, 2, 144, 384), bf),
             D_((2, 8)),
-            V((keep[0], 2, 2, Z, 2, 144, 384), bf),
-            V((keep[1], 2, Z, 2, 144, 384), bf),
-            V((keep[2], 3 * Z, 144, 384), bf),
-            V((keep[2], 2, Z, 144, 384), bf),
+            V((keep[0], 2, 2, Z, 2) + most, bf),
+            V((keep[1], 2, Z, 2) + most, bf),
+            V((keep[2], 2, Z, 2) + most, bf),
+            V((keep[3], 3 * Z) + most, bf),
+            V((keep[3], Z + 1) + most, bf),
+            V((keep[4], 2, Z, 2) + late, bf), V((keep[4], Z + 1, 2, 2) + late, bf), V((keep[4], 3) + late, bf),
             V((tok, Z_OUT), bf), V((tok, P_SIZE), bf), V((tok, P_SIZE), bf), V((tok, D), f32), V((tok, D), bf), V((tok, FF), bf),
             V((tok, D), f32), V((tok, D), bf), V((tok, D), bf), V((tok, 3 * D), bf), V((tok, FF), f32), V((tok, D), f32),
             V((images, 6 * D), f32), V((mod_height, 128), bf), V((mod_height, 128), f32),
         ] + scatter_sems(R, Z)
         + [D_((1,)), D_((1, 2, Z - 1)), D_((1, 2, Z - 1)), D_((1, 4)), D_((1, 4)), D_((1, 4)), D_((1, 4))],
-        compiler_params=pltpu.CompilerParams(collective_id=cid, has_side_effects=True, vmem_limit_bytes=61 * 2**20),
+        compiler_params=pltpu.CompilerParams(collective_id=cid, has_side_effects=True, vmem_limit_bytes=63 * 2**20),
     )(*weights, *acts)
 
 
@@ -1268,7 +1367,7 @@
         results[:6],
         (tokens, onehot, same_image, modulation, targets, out_grad) + tuple(results[6:21]),
         mod_height,
-        (2, (0, 1, 2, 3, 4, 5, 6), (0, 1, 2, 3, 4, 5, 6), (3, 2, 6)),
+        (1, ((0, 1, 3, 5, 6, 7, 8), (0, 1, 4, 6, 8, 9, 10)), (0, 1, 2, 3, 4, 5, 6), (2, 2, 5, 8, 3)),
         2,
     )
     qkv_sum, attn_sum, up_sum, down_sum, in_sum, mid_sum, out_sum, tokens_grad = sums[:8]

time: 517 us -> 486 us (0.940)
  Pallas kernels: 468 us -> 440 us
    pallas_call x1, Pallas kernels: 243 us -> 225 us  [backward(): pl.pallas_call(functools.partial(backward_kernel, n, images, chain_per_ti...]
    pallas_call x1, Pallas kernels: 225 us -> 215 us  [forward(): pl.pallas_call(functools.partial(forward_kernel, n, images, offs), out_sh...]
where the time goes in v4:
time: 486 us; the launch traced here: 479 us
  Pallas kernels  440 us (91%)
  local copies, waits for them, and re-layouts  27.4 us (6%)
  other arithmetic  4.93 us (1%)
    pallas_call x1, Pallas kernels, backward(): pl.pallas_call(functools.partial(backward_kernel, n, images, chain_per_ti...  225 us
    pallas_call x1, Pallas kernels, forward(): pl.pallas_call(functools.partial(forward_kernel, n, images, offs), out_sh...  215 us
  transfers between devices with their start and end apart: 1, of which 0 were waited for; matrix products, arithmetic and copies ran while one was open for 2% of the time, Pallas kernels for 0%

profile of v4, /device:TPU:0, one launch (start us, length us, event | category | flops | bytes accessed | tf_op | source)
XLA Modules:
  0.0 479.2 jit_solution(4953870135609641237)
XLA Ops:
  0.7 0.0 copy-start.26
  0.7 0.9 reduce-window.8
  1.6 0.1 convert_reduce_fusion.1
  1.7 0.1 iota_compare_fusion
  1.8 0.7 compare_convert_fusion
  2.5 2.4 reshape.173.refs_7_
  4.9 0.8 fusion.3
  5.7 0.1 reshape.174
  5.9 0.0 copy-start.10
  6.2 0.5 concatenate.22
  6.7 0.0 copy-start.14
  6.7 0.7 pad.48.refs_8_
  7.4 1.1 reshape.168.refs_2_
  8.5 1.1 reshape.170.refs_4_
  9.6 1.0 reshape.166.refs_0_
  10.6 0.8 reshape.171.refs_5_
  11.5 0.8 reshape.169.refs_3_
  12.2 0.7 reshape.172.refs_6_
  13.0 0.8 reshape.167.refs_1_
  13.7 215.2 %shard_map.331 = (bf16[4,2,2,2,144,1152]{5,4,3,2,1,0:T(8,128)(2,1)}, bf16[4,2,2,2,144,1152]{5,4,3,2,1,0:T(8,128)(2,1)}, bf16[4,2,2,2,144,1152]{5,4,3,2,1,0:T(8,1...) custom-call(bf16[36,3456]{1,0:T(8,128)(2,1)} %reshape.166.refs_0_, ...), custom_call_target="tpu_custom_call" | custom-call | tf_op jit(solution)/shard_map/pallas_call | solution.py:690
  228.9 224.9 %shard_map.332 = (f32[36,3456]{1,0:T(8,128)}, f32[36,1152]{1,0:T(8,128)}, f32[36,4608]{1,0:T(8,128)}, f32[144,1152]{1,0:T(8,128)}, f32[36,2048]{1,0:T(8,128)}, /...) custom-call(bf16[4,2,2,2,144,1152]{5,4,3,2,1,0:T(8,128)(2,1)} %get-t, ...), custom_call_target="tpu_custom_call" | custom-call | tf_op jit(solution)/shard_map/pallas_call | solution.py:1002
  453.8 1.4 slice.46
  455.3 0.0 copy-start
  455.3 1.5 reshape.178
  456.9 0.1 concatenate.26
  457.0 0.1 concatenate.27
  457.1 0.1 concatenate.23
  457.2 0.1 concatenate.24
  457.3 0.5 fusion.9
  457.8 0.1 reshape.179
  458.0 0.1 reshape_squeeze.12
  458.0 0.5 broadcast.54
  458.6 0.7 reduce.14
  459.2 0.1 reshape_squeeze.13
  459.3 0.7 reduce.15
  460.0 0.1 reshape_squeeze.14
  460.1 0.1 reshape_squeeze.15
  460.2 0.1 concatenate.29
  460.3 0.7 all_to_all.8
  461.0 4.3 all-to-all-start
  465.3 0.4 fusion.10
  465.6 1.0 reshape.182
  466.7 0.4 copy-done.2
  467.0 0.9 reshape.185
  467.9 0.9 reshape.186
  468.8 0.4 copy-done.5
  469.2 0.9 copy.52
  470.1 0.8 reshape.183
  470.9 0.8 reshape.187
  471.7 0.7 reshape.189
  472.4 0.7 reshape.184
  473.1 0.2 convert_reduce_fusion
  473.3 0.6 dynamic_slice.3
  473.9 0.0 all-to-all-done
  473.9 0.1 slice_reduce_fusion
  474.0 0.6 fusion.8
  474.6 0.6 fusion.7
  475.2 0.6 slice.42
  475.9 0.6 slice.45
  476.4 0.1 reshape.180
  476.5 0.1 reshape.181
  476.7 0.6 fusion.6
  477.3 0.7 copy.59
  478.0 0.7 copy.60
  (86 shorter events, 0.4 us)
Async XLA Ops:
  0.7 5.2 %copy-start.26 = (bf16[216]{0:T(256)(128)(2,1)S(1)}, bf16[216]{0:T(256)(128)(2,1)}, u32[]{:S(2)}) copy-start(bf16[216]{0:T(256)(128)(2,1)} %param.24) | copy-start | bytes 1300
  0.7 5.3 %copy-start.27 = (bf16[72]{0:T(256)(128)(2,1)S(1)}, bf16[72]{0:T(256)(128)(2,1)}, u32[]{:S(2)}) copy-start(bf16[72]{0:T(256)(128)(2,1)} %param.26) | copy-start | bytes 436
  0.7 5.3 %copy-start.28 = (bf16[72]{0:T(256)(128)(2,1)S(1)}, bf16[72]{0:T(256)(128)(2,1)}, u32[]{:S(2)}) copy-start(bf16[72]{0:T(256)(128)(2,1)} %param.28) | copy-start | bytes 436
  0.7 5.3 %copy-start.29 = (bf16[144]{0:T(256)(128)(2,1)S(1)}, bf16[144]{0:T(256)(128)(2,1)}, u32[]{:S(2)}) copy-start(bf16[144]{0:T(256)(128)(2,1)} %param.30) | copy-start | bytes 868
  0.7 5.3 %copy-start.30 = (bf16[64]{0:T(256)(128)(2,1)S(1)}, bf16[64]{0:T(256)(128)(2,1)}, u32[]{:S(2)}) copy-start(bf16[64]{0:T(256)(128)(2,1)} %param.33) | copy-start | bytes 388
  0.7 5.3 %copy-start.31 = (bf16[64]{0:T(256)(128)(2,1)S(1)}, bf16[64]{0:T(256)(128)(2,1)}, u32[]{:S(2)}) copy-start(bf16[64]{0:T(256)(128)(2,1)} %param.35) | copy-start | bytes 388
  0.7 5.3 %copy-start.32 = (bf16[24]{0:T(256)(128)(2,1)S(1)}, bf16[24]{0:T(256)(128)(2,1)}, u32[]{:S(2)}) copy-start(bf16[24]{0:T(256)(128)(2,1)} %param.37) | copy-start | bytes 148
  0.7 6.7 %copy-start.7 = (bf16[165888]{0:T(1024)(128)(2,1)S(1)}, bf16[165888]{0:T(1024)(128)(2,1)}, u32[]{:S(2)}) copy-start(bf16[165888]{0:T(1024)(128)(2,1)} %param.29) | copy-start | bytes 995332
  2.5 6.0 %copy-start.6 = (bf16[165888]{0:T(1024)(128)(2,1)S(1)}, bf16[165888]{0:T(1024)(128)(2,1)}, u32[]{:S(2)}) copy-start(bf16[165888]{0:T(1024)(128)(2,1)} %param.31) | copy-start | bytes 995332
  4.9 4.7 copy-start.11
  5.9 4.8 copy-start.10
  6.7 4.8 copy-start.14
  7.4 4.8 %copy-start.15 = (bf16[49152]{0:T(1024)(128)(2,1)S(1)}, bf16[49152]{0:T(1024)(128)(2,1)}, u32[]{:S(2)}) copy-start(bf16[49152]{0:T(1024)(128)(2,1)} %param.36) | copy-start | bytes 294916
  7.4 5.6 %copy-start.16 = (bf16[41472]{0:T(1024)(128)(2,1)S(1)}, bf16[41472]{0:T(1024)(128)(2,1)}, u32[]{:S(2)}) copy-start(bf16[41472]{0:T(1024)(128)(2,1)} %param.27) | copy-start | bytes 248836
  455.3 1.6 copy-start.24
  455.3 1.7 copy-start.23
  455.3 1.8 copy-start.22
  455.3 2.0 copy-start
  456.8 1.1 copy-start.19
  456.8 1.7 copy-start.21
  456.8 2.5 copy-start.20
  456.8 3.2 copy-start.25
  457.3 7.9 %copy-start.18 = (bf16[96,36]{1,0:T(8,128)(2,1)S(1)}, bf16[96,36]{1,0:T(8,128)(2,1)}, u32[]{:S(2)}) copy-start(bf16[96,36]{1,0:T(8,128)(2,1)} %get-tuple-element.88) | copy-start | bytes 20740
  461.0 12.9 %all-to-all-start = ((f32[32,1,548]{2,1,0:T(1,128)}), f32[32,1,548]{2,1,0:T(1,128)S(1)}, u32[]{:S(2)}, u32[]{:S(2)}) async-start(f32[32,1,548]{2,1,0:T(1,128)} %all_to_all.8), calls=%async_computation | async-start | bytes 163840 | tf_op jit(solution)/shard_map/all_to_all | solution.py:1389
  465.6 1.4 copy-start.2
  466.7 1.3 copy-start.3
  467.9 1.3 copy-start.5
  467.9 2.1 copy-start.4
  468.8 2.1 copy-start.8
  469.2 2.5 copy-start.12
  469.2 3.2 copy-start.13
  471.7 5.0 %copy-start.17 = (bf16[3,1152]{1,0:T(4,128)(2,1)S(1)}, bf16[3,1152]{1,0:T(4,128)(2,1)}, u32[]{:S(2)}) copy-start(bf16[3,1152]{1,0:T(4,128)(2,1)} %param.21) | copy-start | bytes 20740
  471.7 5.6 %copy-start.1 = (bf16[128,1152]{1,0:T(8,128)(2,1)S(1)}, bf16[128,1152]{1,0:T(8,128)(2,1)}, u32[]{:S(2)}) copy-start(bf16[128,1152]{1,0:T(8,128)(2,1)} %get-tuple-element.122.refs_21_) | copy-start | bytes 884740
  473.1 5.0 %copy-start.9 = (bf16[128,1152]{1,0:T(8,128)(2,1)S(1)}, bf16[128,1152]{1,0:T(8,128)(2,1)}, u32[]{:S(2)}) copy-start(bf16[128,1152]{1,0:T(8,128)(2,1)} %get-tuple-element.123) | copy-start | bytes 884740

commit v5 on v4

--- a/solution.py
+++ b/solution.py
@@ -712,7 +712,9 @@
 
 BACK_CHUNKS = back_rounds(((5, 768, 512, 2), (4, P_SIZE, 512, 2), (3, P_SIZE // 4, 256, 1), (2, D, 256, 1), (1, FF // 4, 256, 1), (0, D, 256, 1)))
 LATE = (3, 8, 12, 16)
-CHAIN = back_rounds(((5, 768, 768, 2), (4, P_SIZE, 768, 2), (3, P_SIZE // 4, 384, 1), (2, D, 384, 1), (1, FF // 4, 384, 1), (6, D, 384, 1), (0, D, 384, 1)))
+CHAIN = back_rounds(((5, 768, 768, 2), (4, P_SIZE, 768, 2), (3, P_SIZE // 4, 384, 1), (2, D, 384, 1), (1, FF // 4, 384, 1), (6, D, 384, 1))) + tuple(
+    (7, 4 * i, 4, 1) for i in range(HEADS // 4)
+) + back_rounds(((0, D, 384, 1),))
 
 def dot_tn(a, b):
     return lax.dot_general(a, b, (((0,), (0,)), ((), ())), preferred_element_type=jnp.float32)
@@ -803,8 +805,9 @@
         feature_grad[...] = grad.astype(bf)
         out_sums[...] = sums(feature_grad[...])
 
-    def attention_back():
-        projected_grad[...] = jnp.zeros_like(projected_grad)
+    def attention_back(begin, count):
+        if begin == 0:
+            projected_grad[...] = jnp.zeros_like(projected_grad)
         def head(h, carry):
             start, inside = head_window(h)
             at_q, at_k, at_v = [pl.ds(pl.multiple_of(start + i * D, 128), 256) for i in range(3)]
@@ -824,16 +827,19 @@
             ):
                 projected_grad[:, at] = jnp.where(inside, value.astype(bf), projected_grad[:, at])
             return carry
-        lax.fori_loop(0, HEADS, head, 0)
-        qkv_sums[...] = sums(projected_grad[...])
+        lax.fori_loop(begin, begin + count, head, 0)
+        if begin + count == HEADS:
+            qkv_sums[...] = sums(projected_grad[...])
 
     C = len(CHAIN)
-    last = {a: max(k for k in range(C) if CHAIN[k][0] == a) for a in range(7)}
-    first = {a: min(k for k in range(C) if CHAIN[k][0] == a) for a in range(7)}
+    last = {a: max(k for k in range(C) if CHAIN[k][0] == a) for a in range(8)}
+    first = {a: min(k for k in range(C) if CHAIN[k][0] == a) for a in range(8)}
 
     def chain_loads(k):
         a, off, w, stacks = CHAIN[k]
         slot, sem = slots.at[k % 2], load_sem.at[k % 2]
+        if a == 7:
+            return []
         if a == 6:
             return weight_loads((0, off, w, stacks), full, slot, sem, 3 * per // 16 * 16)
         return weight_loads((a, off, w, stacks), full, slot, sem, 0, -(-3 * per // 16) * 16 if a == 0 else None)
@@ -843,6 +849,9 @@
 
     def chain(k):
         a, off, w, stacks = CHAIN[k]
+        if a == 7:
+            attention_back(off, w)
+            return
         if k == first[3]:
             for cp in bring(later): cp.wait()
         slot = slots.at[k % 2]
@@ -898,7 +907,6 @@
                     image_sums(2, mg * branch_attn[...])
                 elif a == 6:
                     heads_grad[...] = narrow[...].astype(bf)
-                    attention_back()
                 else:
                     g = narrow[...]
                     centred, scale = norm_parts(tokens[...].astype(jnp.float32))

time: 486 us -> 483 us (level)
  no operation moved by 1% of the time
where the time goes in v5:
time: 483 us; the launch traced here: 476 us
  Pallas kernels  437 us (90%)
  local copies, waits for them, and re-layouts  27.4 us (6%)
  other arithmetic  4.93 us (1%)
    pallas_call x1, Pallas kernels, backward(): pl.pallas_call(functools.partial(backward_kernel, n, images, chain_per_ti...  222 us
    pallas_call x1, Pallas kernels, forward(): pl.pallas_call(functools.partial(forward_kernel, n, images, offs), out_sh...  215 us
  transfers between devices with their start and end apart: 1, of which 0 were waited for; matrix products, arithmetic and copies ran while one was open for 2% of the time, Pallas kernels for 0%

profile of v5, /device:TPU:0, one launch (start us, length us, event | category | flops | bytes accessed | tf_op | source)
XLA Modules:
  0.0 475.9 jit_solution(1790861111885680821)
XLA Ops:
  0.7 0.0 copy-start.26
  0.7 0.9 reduce-window.8
  1.6 0.1 convert_reduce_fusion.1
  1.7 0.1 iota_compare_fusion
  1.8 0.7 compare_convert_fusion
  2.5 2.4 reshape.173.refs_7_
  4.9 0.8 fusion.3
  5.7 0.1 reshape.174
  5.9 0.0 copy-start.10
  6.2 0.5 concatenate.22
  6.7 0.0 copy-start.14
  6.7 0.7 pad.48.refs_8_
  7.4 1.1 reshape.168.refs_2_
  8.5 1.1 reshape.170.refs_4_
  9.6 1.0 reshape.166.refs_0_
  10.6 0.8 reshape.171.refs_5_
  11.5 0.8 reshape.169.refs_3_
  12.2 0.7 reshape.172.refs_6_
  13.0 0.8 reshape.167.refs_1_
  13.7 215.2 %shard_map.331 = (bf16[4,2,2,2,144,1152]{5,4,3,2,1,0:T(8,128)(2,1)}, bf16[4,2,2,2,144,1152]{5,4,3,2,1,0:T(8,128)(2,1)}, bf16[4,2,2,2,144,1152]{5,4,3,2,1,0:T(8,1...) custom-call(bf16[36,3456]{1,0:T(8,128)(2,1)} %reshape.166.refs_0_, ...), custom_call_target="tpu_custom_call" | custom-call | tf_op jit(solution)/shard_map/pallas_call | solution.py:690
  228.9 222.2 %shard_map.332 = (f32[36,3456]{1,0:T(8,128)}, f32[36,1152]{1,0:T(8,128)}, f32[36,4608]{1,0:T(8,128)}, f32[144,1152]{1,0:T(8,128)}, f32[36,2048]{1,0:T(8,128)}, /...) custom-call(bf16[4,2,2,2,144,1152]{5,4,3,2,1,0:T(8,128)(2,1)} %get-t, ...), custom_call_target="tpu_custom_call" | custom-call | tf_op jit(solution)/shard_map/pallas_call | solution.py:1010
  451.1 1.4 slice.46
  452.6 0.0 copy-start
  452.6 1.5 reshape.178
  454.2 0.1 concatenate.26
  454.3 0.1 concatenate.27
  454.4 0.1 concatenate.23
  454.5 0.1 concatenate.24
  454.6 0.5 fusion.9
  455.1 0.1 reshape.179
  455.2 0.1 reshape_squeeze.12
  455.3 0.5 broadcast.54
  455.8 0.7 reduce.14
  456.5 0.1 reshape_squeeze.13
  456.6 0.7 reduce.15
  457.2 0.1 reshape_squeeze.14
  457.3 0.1 reshape_squeeze.15
  457.5 0.1 concatenate.29
  457.6 0.7 all_to_all.8
  458.3 3.7 all-to-all-start
  462.0 0.4 fusion.10
  462.4 1.0 reshape.182
  463.4 0.4 copy-done.2
  463.8 0.9 reshape.185
  464.7 0.9 reshape.186
  465.6 0.4 copy-done.5
  465.9 0.9 copy.52
  466.8 0.8 reshape.183
  467.6 0.8 reshape.187
  468.4 0.7 reshape.189
  469.1 0.7 reshape.184
  469.8 0.2 convert_reduce_fusion
  470.0 0.6 dynamic_slice.3
  470.7 0.0 all-to-all-done
  470.7 0.1 slice_reduce_fusion
  470.8 0.6 fusion.8
  471.4 0.6 fusion.7
  472.0 0.6 slice.42
  472.6 0.6 slice.45
  473.2 0.1 reshape.180
  473.3 0.1 reshape.181
  473.4 0.6 fusion.6
  474.0 0.7 copy.59
  474.7 0.7 copy.60
  (86 shorter events, 0.4 us)
Async XLA Ops:
  0.7 5.2 %copy-start.26 = (bf16[216]{0:T(256)(128)(2,1)S(1)}, bf16[216]{0:T(256)(128)(2,1)}, u32[]{:S(2)}) copy-start(bf16[216]{0:T(256)(128)(2,1)} %param.24) | copy-start | bytes 1300
  0.7 5.3 %copy-start.27 = (bf16[72]{0:T(256)(128)(2,1)S(1)}, bf16[72]{0:T(256)(128)(2,1)}, u32[]{:S(2)}) copy-start(bf16[72]{0:T(256)(128)(2,1)} %param.26) | copy-start | bytes 436
  0.7 5.3 %copy-start.28 = (bf16[72]{0:T(256)(128)(2,1)S(1)}, bf16[72]{0:T(256)(128)(2,1)}, u32[]{:S(2)}) copy-start(bf16[72]{0:T(256)(128)(2,1)} %param.28) | copy-start | bytes 436
  0.7 5.3 %copy-start.29 = (bf16[144]{0:T(256)(128)(2,1)S(1)}, bf16[144]{0:T(256)(128)(2,1)}, u32[]{:S(2)}) copy-start(bf16[144]{0:T(256)(128)(2,1)} %param.30) | copy-start | bytes 868
  0.7 5.3 %copy-start.30 = (bf16[64]{0:T(256)(128)(2,1)S(1)}, bf16[64]{0:T(256)(128)(2,1)}, u32[]{:S(2)}) copy-start(bf16[64]{0:T(256)(128)(2,1)} %param.33) | copy-start | bytes 388
  0.7 5.3 %copy-start.31 = (bf16[64]{0:T(256)(128)(2,1)S(1)}, bf16[64]{0:T(256)(128)(2,1)}, u32[]{:S(2)}) copy-start(bf16[64]{0:T(256)(128)(2,1)} %param.35) | copy-start | bytes 388
  0.7 5.3 %copy-start.32 = (bf16[24]{0:T(256)(128)(2,1)S(1)}, bf16[24]{0:T(256)(128)(2,1)}, u32[]{:S(2)}) copy-start(bf16[24]{0:T(256)(128)(2,1)} %param.37) | copy-start | bytes 148
  0.7 6.7 %copy-start.7 = (bf16[165888]{0:T(1024)(128)(2,1)S(1)}, bf16[165888]{0:T(1024)(128)(2,1)}, u32[]{:S(2)}) copy-start(bf16[165888]{0:T(1024)(128)(2,1)} %param.29) | copy-start | bytes 995332
  2.5 6.0 %copy-start.6 = (bf16[165888]{0:T(1024)(128)(2,1)S(1)}, bf16[165888]{0:T(1024)(128)(2,1)}, u32[]{:S(2)}) copy-start(bf16[165888]{0:T(1024)(128)(2,1)} %param.31) | copy-start | bytes 995332
  4.9 4.7 copy-start.11
  5.9 4.8 %copy-start.10 = (bf16[131072]{0:T(1024)(128)(2,1)S(1)}, bf16[131072]{0:T(1024)(128)(2,1)}, u32[]{:S(2)}) copy-start(bf16[131072]{0:T(1024)(128)(2,1)} %param.34) | copy-start | bytes 786436
  6.7 4.8 %copy-start.14 = (bf16[73728]{0:T(1024)(128)(2,1)S(1)}, bf16[73728]{0:T(1024)(128)(2,1)}, u32[]{:S(2)}) copy-start(bf16[73728]{0:T(1024)(128)(2,1)} %param.32) | copy-start | bytes 442372
  7.4 4.8 %copy-start.15 = (bf16[49152]{0:T(1024)(128)(2,1)S(1)}, bf16[49152]{0:T(1024)(128)(2,1)}, u32[]{:S(2)}) copy-start(bf16[49152]{0:T(1024)(128)(2,1)} %param.36) | copy-start | bytes 294916
  7.4 5.6 %copy-start.16 = (bf16[41472]{0:T(1024)(128)(2,1)S(1)}, bf16[41472]{0:T(1024)(128)(2,1)}, u32[]{:S(2)}) copy-start(bf16[41472]{0:T(1024)(128)(2,1)} %param.27) | copy-start | bytes 248836
  452.5 1.6 copy-start.24
  452.5 1.7 copy-start.23
  452.6 1.8 copy-start.22
  452.6 2.0 copy-start
  454.1 1.1 copy-start.19
  454.1 1.7 copy-start.21
  454.1 2.5 copy-start.20
  454.1 3.2 copy-start.25
  454.6 7.4 %copy-start.18 = (bf16[96,36]{1,0:T(8,128)(2,1)S(1)}, bf16[96,36]{1,0:T(8,128)(2,1)}, u32[]{:S(2)}) copy-start(bf16[96,36]{1,0:T(8,128)(2,1)} %get-tuple-element.88) | copy-start | bytes 20740
  458.3 12.4 %all-to-all-start = ((f32[32,1,548]{2,1,0:T(1,128)}), f32[32,1,548]{2,1,0:T(1,128)S(1)}, u32[]{:S(2)}, u32[]{:S(2)}) async-start(f32[32,1,548]{2,1,0:T(1,128)} %all_to_all.8), calls=%async_computation | async-start | bytes 163840 | tf_op jit(solution)/shard_map/all_to_all | solution.py:1397
  462.4 1.4 copy-start.2
  463.4 1.3 copy-start.3
  464.7 1.3 copy-start.5
  464.7 2.1 copy-start.4
  465.6 2.1 copy-start.8
  465.9 2.5 copy-start.12
  465.9 3.2 copy-start.13
  468.4 5.0 %copy-start.17 = (bf16[3,1152]{1,0:T(4,128)(2,1)S(1)}, bf16[3,1152]{1,0:T(4,128)(2,1)}, u32[]{:S(2)}) copy-start(bf16[3,1152]{1,0:T(4,128)(2,1)} %param.21) | copy-start | bytes 20740
  468.4 5.6 %copy-start.1 = (bf16[128,1152]{1,0:T(8,128)(2,1)S(1)}, bf16[128,1152]{1,0:T(8,128)(2,1)}, u32[]{:S(2)}) copy-start(bf16[128,1152]{1,0:T(8,128)(2,1)} %get-tuple-element.122.refs_21_) | copy-start | bytes 884740
  469.8 5.0 %copy-start.9 = (bf16[128,1152]{1,0:T(8,128)(2,1)S(1)}, bf16[128,1152]{1,0:T(8,128)(2,1)}, u32[]{:S(2)}) copy-start(bf16[128,1152]{1,0:T(8,128)(2,1)} %get-tuple-element.123) | copy-start | bytes 884740
